TPU v7x, 32 devices: a whole 2x2x4 slice. The times are simulated.
32 devices in a mesh: groups: 2 (over y), slab: 16 (over z, x, core).
Axes of the slice: x: 2, y: 2, z: 4, core: 2. Of those that a mesh axis runs over, the one named last changes fastest.
Arguments:
- charges: bfloat16 [131072, 512], P(('groups', 'slab')), parts along dimension 0, may hold values from -6 to 6
- near_blocks: bfloat16 [1024, 3, 128, 128], P(('groups', 'slab')), parts along dimension 0, may hold values from -0.3125 to 0.3125
- near_pattern: int32 [1024, 3], P(('groups', 'slab')), parts along dimension 0, may hold values from 0 to 1, as said below
- leaf_basis: bfloat16 [1024, 64, 128], P(('groups', 'slab')), parts along dimension 0, may hold values from -0.5 to 0.5
- transfers: bfloat16 [992, 64, 128], P(('groups', 'slab')), parts along dimension 0, may hold values from -0.5 to 0.5
- couplings: bfloat16 [2016, 64, 256], P(('groups', 'slab')), parts along dimension 0, may hold values from -0.375 to 0.375
- interactions: int32 [2016, 4], P(('groups', 'slab')), parts along dimension 0, may hold values 0 or 1
Outputs:
- potentials: bfloat16 [131072, 512], P(('groups', 'slab')), parts along dimension 0
There are 2 independent parts, one for each index of `groups`. A program takes and returns all parts, laid end to end along the dimension named above; each array names one. Nothing has to cross between parts.
Inputs may be any that keep to these rules, and one draw needn't show every extreme that they name: `near_pattern`: the middle column, a leaf's block with itself, is 1 for every leaf.
All inputs are finite; a program needn't handle non-finite values. No bound on the sum of `interactions` on one device may be relied on, other than what follows from the above.
Results may differ from a plain program's by a relative error of at most 0.0073.
Values may be sent and summed in bfloat16 or wider, within the bound.
No kernel may reach another device: no remote copies, remote signals or barrier semaphores. Data moves between devices by JAX's collectives and lax.ppermute only.
A program may use at most 128 MiB of HBM per device.

v0:
```python
import jax
import jax.numpy as jnp
from jax import lax
from jax.sharding import PartitionSpec as P

LEVELS = 6


OFFSETS = (-3, -2, 2, 3)


def padded_2(block, sides, width):
    for axis, dim in sides:
        count = lax.axis_size(axis)
        forward = [(i, i + 1) for i in range(count - 1)]
        backward = [(target, source) for source, target in forward]
        low = lax.ppermute(
            lax.slice_in_dim(block, block.shape[dim] - width, None, axis=dim), axis, forward
        )
        high = lax.ppermute(lax.slice_in_dim(block, 0, width, axis=dim), axis, backward)
        block = jnp.concatenate([low, block, high], axis=dim)
    return block


def shifted(array, axis, by):
    peers = lax.axis_size(axis)
    pairs = [(i, i + by) for i in range(peers) if 0 <= i + by < peers]
    return lax.ppermute(array, axis, pairs)


def couple(matrix, chosen, padded, box_count, center):
    pieces = []
    flags = chosen.astype(jnp.bfloat16)
    for column, offset in enumerate(OFFSETS):
        position = center + offset
        pieces.append(padded[position : position + box_count] * flags[:, column][:, None, None])
    stacked = jnp.concatenate(pieces, axis=1)
    return jnp.einsum("bkj,bjr->bkr", matrix, stacked, preferred_element_type=jnp.float32)


def body(charges, near_blocks, near_pattern, leaf_basis, transfers, couplings, interactions):
    leaves = near_blocks.shape[0]
    panels = near_blocks.shape[2]
    poles_dim = leaf_basis.shape[1]
    rhs_count = charges.shape[1]
    source = charges.reshape(leaves, panels, rhs_count)
    rimmed = padded_2(source, (("slab", 0),), 1)
    pattern = near_pattern.astype(jnp.float32)
    near_sum = jnp.zeros((leaves, panels, rhs_count), jnp.float32)
    for column in range(3):
        product = jnp.einsum(
            "ipq,iqr->ipr",
            near_blocks[:, column],
            rimmed[column : column + leaves],
            preferred_element_type=jnp.float32,
        )
        near_sum = near_sum + product * pattern[:, column][:, None, None]
    multipoles = [
        jnp.einsum("ikp,ipr->ikr", leaf_basis, source, preferred_element_type=jnp.float32).astype(
            jnp.bfloat16
        )
    ]
    transfer_levels = []
    first_box = 0
    for tree_level in range(1, LEVELS):
        box_count = leaves >> tree_level
        matrix = transfers[first_box : first_box + box_count]
        first_box += box_count
        transfer_levels.append(matrix)
        children = multipoles[-1].reshape(box_count, 2 * poles_dim, rhs_count)
        multipoles.append(
            jnp.einsum("bkj,bjr->bkr", matrix, children, preferred_element_type=jnp.float32).astype(
                jnp.bfloat16
            )
        )
    lower_count = LEVELS - 2
    padded_levels = [padded_2(multipoles[level], (("slab", 0),), 3) for level in range(lower_count)]
    expansions = []
    first_box = 0
    for tree_level in range(lower_count):
        box_count = leaves >> tree_level
        expansions.append(
            couple(
                couplings[first_box : first_box + box_count],
                interactions[first_box : first_box + box_count],
                padded_levels[tree_level],
                box_count,
                3,
            )
        )
        first_box += box_count
    summit = jnp.concatenate([multipoles[LEVELS - 2], multipoles[LEVELS - 1]], axis=0)
    below_window = summit[None]
    for distance in (1, 2):
        below_window = jnp.concatenate(
            [shifted(below_window, "slab", distance), below_window], axis=0
        )
    above_window = summit[None]
    for distance in (1, 2):
        above_window = jnp.concatenate(
            [above_window, shifted(above_window, "slab", -distance)], axis=0
        )
    window = jnp.concatenate([below_window[:3], above_window], axis=0)
    pair_count = multipoles[LEVELS - 2].shape[0]
    second = window[:, :pair_count].reshape(7 * pair_count, poles_dim, rhs_count)
    expansions.append(
        couple(
            couplings[first_box : first_box + pair_count],
            interactions[first_box : first_box + pair_count],
            second,
            pair_count,
            3 * pair_count,
        )
    )
    first_box += pair_count
    top_level = window[:, pair_count]
    expansions.append(
        couple(
            couplings[first_box : first_box + 1],
            interactions[first_box : first_box + 1],
            top_level,
            1,
            3,
        )
    )
    for tree_level in range(LEVELS - 1, 0, -1):
        matrix = transfer_levels[tree_level - 1]
        pushed = jnp.einsum(
            "bkj,bkr->bjr",
            matrix,
            expansions[tree_level].astype(jnp.bfloat16),
            preferred_element_type=jnp.float32,
        )
        expansions[tree_level - 1] = expansions[tree_level - 1] + pushed.reshape(
            -1, poles_dim, rhs_count
        )
    leaf_local = expansions[0].astype(jnp.bfloat16)
    far_field = jnp.einsum(
        "ikp,ikr->ipr", leaf_basis, leaf_local, preferred_element_type=jnp.float32
    )
    return (near_sum + far_field).astype(jnp.bfloat16).reshape(leaves * panels, rhs_count)


def solution(mesh):
    in_specs = (
        P(("groups", "slab"), None),
        P(("groups", "slab"), None, None, None),
        P(("groups", "slab"), None),
        P(("groups", "slab"), None, None),
        P(("groups", "slab"), None, None),
        P(("groups", "slab"), None, None),
        P(("groups", "slab"), None),
    )
    out_specs = P(("groups", "slab"), None)
    return jax.shard_map(body, mesh=mesh, in_specs=in_specs, out_specs=out_specs, check_vma=False)
```

profile of v0, /device:TPU:16, one launch (start us, length us, event | category | flops | bytes accessed | tf_op | source)
XLA Modules:
  0.0 133.0 jit_solution(10724485319873975491)
XLA Ops:
  0.0 1.0 copy-done
  1.0 3.0 %convolution_convert_fusion = bf16[32,64,512]{2,1,0:T(8,128)(2,1)S(1)} fusion(bf16[32,64,128]{2,1,0:T(8,128)(2,1)S(1)} %copy-done, bf16[32,128,512]{2,1,0:T(8,128)(2,1)} %bitcast.200), kind=kOutput, calls=%fused_computation.51 | convolution fusion | flops 269484032 | bytes 6815744 | tf_op jit(solution)/shard_map/ikp,ipr->ikr/dot_general | solution.py:59
  4.0 0.4 convolution_convert_fusion.1
  4.5 0.0 copy-start.2
  4.5 0.0 copy-start.36
  4.5 0.3 convolution_convert_fusion.2
  4.8 0.0 copy-start.37
  4.8 0.2 convolution_convert_fusion.3
  5.0 0.2 convolution_convert_fusion.4
  5.2 0.1 fusion.66
  5.4 0.6 copy-done.5
  6.0 0.7 maximum_bitcast_fusion.3
  6.7 2.7 %collective-permute-start.12 = (bf16[1,3,64,512]{3,2,1,0:T(8,128)(2,1)}, bf16[1,3,64,512]{3,2,1,0:T(8,128)(2,1)}, u32[]{:S(2)}, u32[]{:S(2)}) collective-permute-start(bf16[1,3,64,512]{3,2,1,0:T(8,128)(2,1)} %maximum_bitcast_fusion.3), channel_id=1, source_target_pairs={{1,0},{2,1},{3,2},{4,3},{5,4},{6,5},{7,6},{8,7},{9,8},{10,9},{11,1... | collective-permute-start | bytes 589832 | tf_op jit(solution)/shard_map/ppermute | solution.py:28
  9.4 1.9 %collective-permute-start.10 = (bf16[1,3,64,512]{3,2,1,0:T(8,128)(2,1)}, bf16[1,3,64,512]{3,2,1,0:T(8,128)(2,1)}, u32[]{:S(2)}, u32[]{:S(2)}) collective-permute-start(bf16[1,3,64,512]{3,2,1,0:T(8,128)(2,1)} %maximum_bitcast_fusion.3), channel_id=1, source_target_pairs={{0,1},{1,2},{2,3},{3,4},{4,5},{5,6},{6,7},{7,8},{8,9},{9,10},{10,1... | collective-permute-start | bytes 589832 | tf_op jit(solution)/shard_map/ppermute | solution.py:28
  11.3 0.7 slice_bitcast_fusion.2
  12.1 4.5 %collective-permute-start.1 = (bf16[1,128,512]{2,1,0:T(8,128)(2,1)}, bf16[1,128,512]{2,1,0:T(8,128)(2,1)}, u32[]{:S(2)}, u32[]{:S(2)}) collective-permute-start(bf16[1,128,512]{2,1,0:T(8,128)(2,1)} %get-tuple-element.5), channel_id=1, source_target_pairs={{1,0},{2,1},{3,2},{4,3},{5,4},{6,5},{7,6},{8,7},{9,8},{10,9},{11,1... | collective-permute-start | bytes 393224 | tf_op jit(solution)/shard_map/ppermute | solution.py:20
  16.6 1.9 %collective-permute-start = (bf16[1,128,512]{2,1,0:T(8,128)(2,1)}, bf16[1,128,512]{2,1,0:T(8,128)(2,1)}, u32[]{:S(2)}, u32[]{:S(2)}) collective-permute-start(bf16[1,128,512]{2,1,0:T(8,128)(2,1)} %get-tuple-element.6), channel_id=1, source_target_pairs={{0,1},{1,2},{2,3},{3,4},{4,5},{5,6},{6,7},{7,8},{8,9},{9,10},{10,1... | collective-permute-start | bytes 393224 | tf_op jit(solution)/shard_map/ppermute | solution.py:17
  18.5 0.8 fusion.180
  19.3 1.9 %collective-permute-start.8 = (bf16[3,64,512]{2,1,0:T(8,128)(2,1)}, bf16[3,64,512]{2,1,0:T(8,128)(2,1)}, u32[]{:S(2)}, u32[]{:S(2)}) collective-permute-start(bf16[3,64,512]{2,1,0:T(8,128)(2,1)} %get-tuple-element.43), channel_id=1, source_target_pairs={{0,1},{1,2},{2,3},{3,4},{4,5},{5,6},{6,7},{7,8},{8,9},{9,10},{10,1... | collective-permute-start | bytes 589832 | tf_op jit(solution)/shard_map/ppermute | solution.py:17
  21.3 0.7 slice_bitcast_fusion.8
  21.9 0.6 slice_bitcast_fusion.20
  22.5 0.7 slice_bitcast_fusion.16
  23.2 0.7 slice_bitcast_fusion.12
  23.9 0.6 slice_bitcast_fusion.4
  24.5 0.8 fusion.177
  25.3 0.5 slice_bitcast_fusion.27
  25.8 0.8 fusion.178
  26.6 0.8 fusion.179
  27.4 5.8 %fusion.88 = f32[32,128,512]{2,1,0:T(8,128)} fusion(bf16[32,128,512]{2,1,0:T(8,128)(2,1)S(1)} %bitcast.203, bf16[32,3,128,128]{3,2,1,0:T(8,128)(2,1)} %param.8), kind=kOutput, calls=%fused_computation.94 | convolution fusion | flops 536870912 | bytes 13631488 | tf_op jit(solution)/shard_map/ipq,iqr->ipr/dot_general | solution.py:51
  33.2 0.6 slice_bitcast_fusion.24
  33.8 1.4 %dot_general.110 = bf16[2,64,64]{1,0,2:T(2,128)(2,1)} reshape(bf16[128,64]{0,1:T(8,128)(2,1)} %slice_bitcast_fusion.4) | data formatting | bytes 32768 | tf_op jit(solution)/shard_map/bkj,bkr->bjr/dot_general | solution.py:128
  35.2 0.7 fusion.181
  35.9 4.7 %collective-permute-start.9 = (bf16[3,64,512]{2,1,0:T(8,128)(2,1)}, bf16[3,64,512]{2,1,0:T(8,128)(2,1)S(1)}, u32[]{:S(2)}, u32[]{:S(2)}) collective-permute-start(bf16[3,64,512]{2,1,0:T(8,128)(2,1)} %get-tuple-element.44), channel_id=1, source_target_pairs={{1,0},{2,1},{3,2},{4,3},{5,4},{6,5},{7,6},{8,7},{9,8},{10,9},{11,1... | collective-permute-start | bytes 589832 | tf_op jit(solution)/shard_map/ppermute | solution.py:20
  40.6 7.0 %fusion.11 = f32[32,512,128]{1,2,0:T(8,128)} fusion(bf16[32,128,512]{2,1,0:T(8,128)(2,1)} %bitcast.201, bf16[1,128,512]{2,1,0:T(8,128)(2,1)} %collective-permute-done, bf16[32,3,128,128]{3,2,1,0:T(8,128)(2,1)} %param.8), kind=kOutput, calls=%fused_computation.16 | convolution fusion | flops 545259520 | bytes 13762560 | tf_op jit(solution)/shard_map/ipq,iqr->ipr/dot_general | solution.py:51
  47.7 2.1 %collective-permute-start.2 = (bf16[3,64,512]{2,1,0:T(8,128)(2,1)S(1)}, bf16[3,64,512]{2,1,0:T(8,128)(2,1)S(1)}, u32[]{:S(2)}, u32[]{:S(2)}) collective-permute-start(bf16[3,64,512]{2,1,0:T(8,128)(2,1)S(1)} %copy-done.16), channel_id=1, source_target_pairs={{0,1},{1,2},{2,3},{3,4},{4,5},{5,6},{6,7},{7,8},{8,9},{9,10},{10,1... | collective-permute-start | bytes 589832 | tf_op jit(solution)/shard_map/ppermute | solution.py:17
  49.8 4.5 %collective-permute-start.3 = (bf16[3,64,512]{2,1,0:T(8,128)(2,1)S(1)}, bf16[3,64,512]{2,1,0:T(8,128)(2,1)S(1)}, u32[]{:S(2)}, u32[]{:S(2)}) collective-permute-start(bf16[3,64,512]{2,1,0:T(8,128)(2,1)S(1)} %copy-done.15), channel_id=1, source_target_pairs={{1,0},{2,1},{3,2},{4,3},{5,4},{6,5},{7,6},{8,7},{9,8},{10,9},{11,1... | collective-permute-start | bytes 589832 | tf_op jit(solution)/shard_map/ppermute | solution.py:20
  54.3 1.3 pad_maximum_fusion.12
  55.6 1.9 %collective-permute-start.6 = (bf16[3,64,512]{2,1,0:T(8,128)(2,1)S(1)}, bf16[3,64,512]{2,1,0:T(8,128)(2,1)S(1)}, u32[]{:S(2)}, u32[]{:S(2)}) collective-permute-start(bf16[3,64,512]{2,1,0:T(8,128)(2,1)S(1)} %copy-done.18), channel_id=1, source_target_pairs={{0,1},{1,2},{2,3},{3,4},{4,5},{5,6},{6,7},{7,8},{8,9},{9,10},{10,1... | collective-permute-start | bytes 589832 | tf_op jit(solution)/shard_map/ppermute | solution.py:17
  57.6 4.5 %collective-permute-start.7 = (bf16[3,64,512]{2,1,0:T(8,128)(2,1)S(1)}, bf16[3,64,512]{2,1,0:T(8,128)(2,1)S(1)}, u32[]{:S(2)}, u32[]{:S(2)}) collective-permute-start(bf16[3,64,512]{2,1,0:T(8,128)(2,1)S(1)} %copy-done.17), channel_id=1, source_target_pairs={{1,0},{2,1},{3,2},{4,3},{5,4},{6,5},{7,6},{8,7},{9,8},{10,9},{11,1... | collective-permute-start | bytes 589832 | tf_op jit(solution)/shard_map/ppermute | solution.py:20
  62.2 2.1 %fusion.121 = (bf16[4,64,512]{2,1,0:T(8,128)(2,1)}, bf16[4,64,512]{2,1,0:T(8,128)(2,1)}, bf16[4,64,512]{2,1,0:T(8,128)(2,1)}, bf16[4,64,512]{2,1,0:T(8,128)(2,1)}) fusion(bf16[3,64,512]{2,1,0:T(8,128)(2,1)} %collective-permute-done.8, bf16[4,64,512]{2,1,0:T(8,128)(2,1)S(1)} %bitcast.213, bf16[4]{0:T(256)(128)(2,1)S(1)} %copy-done.32, ...), kind=kLoop, calls=%fused_computation.130 | loop fusion | flops 1048576 | bytes 1703968 | tf_op jit(solution)/shard_map/mul | solution.py:36
  64.3 1.9 %collective-permute-start.4 = (bf16[3,64,512]{2,1,0:T(8,128)(2,1)S(1)}, bf16[3,64,512]{2,1,0:T(8,128)(2,1)S(1)}, u32[]{:S(2)}, u32[]{:S(2)}) collective-permute-start(bf16[3,64,512]{2,1,0:T(8,128)(2,1)S(1)} %copy-done.14), channel_id=1, source_target_pairs={{0,1},{1,2},{2,3},{3,4},{4,5},{5,6},{6,7},{7,8},{8,9},{9,10},{10,1... | collective-permute-start | bytes 589832 | tf_op jit(solution)/shard_map/ppermute | solution.py:17
  66.2 4.5 %collective-permute-start.5 = (bf16[3,64,512]{2,1,0:T(8,128)(2,1)S(1)}, bf16[3,64,512]{2,1,0:T(8,128)(2,1)S(1)}, u32[]{:S(2)}, u32[]{:S(2)}) collective-permute-start(bf16[3,64,512]{2,1,0:T(8,128)(2,1)S(1)} %copy-done.13), channel_id=1, source_target_pairs={{1,0},{2,1},{3,2},{4,3},{5,4},{6,5},{7,6},{8,7},{9,8},{10,9},{11,1... | collective-permute-start | bytes 589832 | tf_op jit(solution)/shard_map/ppermute | solution.py:20
  70.8 1.5 %fusion.99 = (bf16[8,64,512]{2,1,0:T(8,128)(2,1)}, bf16[8,64,512]{2,1,0:T(8,128)(2,1)}, bf16[8,64,512]{2,1,0:T(8,128)(2,1)}, bf16[8,64,512]{2,1,0:T(8,128)(2,1)}) fusion(bf16[3,64,512]{2,1,0:T(8,128)(2,1)S(1)} %collective-permute-done.6, bf16[8,64,512]{2,1,0:T(8,128)(2,1)S(1)} %bitcast.210, bf16[8]{0:T(256)(128)(2,1)S(1)} %copy-done.28, ...), kind=kLoop, calls=%fused_computation.108 | loop fusion | flops 2097152 | bytes 3014720 | tf_op jit(solution)/shard_map/mul | solution.py:36
  72.3 1.6 %fusion.140 = bf16[2,64,512]{2,1,0:T(8,128)(2,1)} fusion(bf16[1,3,64,512]{3,2,1,0:T(8,128)(2,1)} %collective-permute-done.12, bf16[2]{0:T(256)(128)(2,1)S(1)} %copy-done.23), kind=kLoop, calls=%fused_computation.148 | loop fusion | flops 65536 | bytes 262148 | tf_op jit(solution)/shard_map/mul | solution.py:36
  73.9 1.9 %collective-permute-start.11 = (bf16[2,3,64,512]{3,2,1,0:T(8,128)(2,1)S(1)}, bf16[2,3,64,512]{3,2,1,0:T(8,128)(2,1)S(1)}, u32[]{:S(2)}, u32[]{:S(2)}) collective-permute-start(bf16[2,3,64,512]{3,2,1,0:T(8,128)(2,1)S(1)} %get-tuple-element.45), channel_id=1, source_target_pairs={{0,2},{1,3},{2,4},{3,5},{4,6},{5,7},{6,8},{7,9},{8,10},{9,11},{10,... | collective-permute-start | bytes 1179656 | tf_op jit(solution)/shard_map/ppermute | solution.py:28
  75.9 5.0 %collective-permute-start.13 = (bf16[2,3,64,512]{3,2,1,0:T(8,128)(2,1)S(1)}, bf16[2,3,64,512]{3,2,1,0:T(8,128)(2,1)S(1)}, u32[]{:S(2)}, u32[]{:S(2)}) collective-permute-start(bf16[2,3,64,512]{3,2,1,0:T(8,128)(2,1)S(1)} %get-tuple-element.46), channel_id=1, source_target_pairs={{2,0},{3,1},{4,2},{5,3},{6,4},{7,5},{8,6},{9,7},{10,8},{11,9},{12,... | collective-permute-start | bytes 1179656 | tf_op jit(solution)/shard_map/ppermute | solution.py:28
  81.0 4.0 %fusion.30 = (bf16[32,64,512]{2,1,0:T(8,128)(2,1)}, bf16[32,64,512]{2,1,0:T(8,128)(2,1)}, bf16[32,64,512]{2,1,0:T(8,128)(2,1)}, bf16[32,64,512]{2,1,0:T(8,128)(2,1)}) fusion(bf16[3,64,512]{2,1,0:T(8,128)(2,1)S(1)} %collective-permute-done.2, bf16[32,64,512]{2,1,0:T(8,128)(2,1)S(1)} %convolution_convert_fusion, bf16[32]{0:T(256)(128)(2,1)S(1)} %copy-done.24, ...), kind=kLoop, calls=%fused_computation.36 | loop fusion | flops 8388608 | bytes 10879232 | tf_op jit(solution)/shard_map/mul | solution.py:36
  85.0 1.0 fusion.141
  86.0 2.5 %fusion.70 = (bf16[16,64,512]{2,1,0:T(8,128)(2,1)}, bf16[16,64,512]{2,1,0:T(8,128)(2,1)}, bf16[16,64,512]{2,1,0:T(8,128)(2,1)}, bf16[16,64,512]{2,1,0:T(8,128)(2,1)}) fusion(bf16[3,64,512]{2,1,0:T(8,128)(2,1)S(1)} %collective-permute-done.4, bf16[16,64,512]{2,1,0:T(8,128)(2,1)S(1)} %bitcast.207, bf16[16]{0:T(256)(128)(2,1)S(1)} %get-tuple-element.54, ...), kind=kLoop, calls=%fused_computation.81 | loop fusion | flops 4194304 | bytes 5636224 | tf_op jit(solution)/shard_map/mul | solution.py:36
  88.6 4.8 %collective-permute-done.11 = bf16[2,3,64,512]{3,2,1,0:T(8,128)(2,1)S(1)} collective-permute-done((bf16[2,3,64,512]{3,2,1,0:T(8,128)(2,1)S(1)}, bf16[2,3,64,512]{3,2,1,0:T(8,128)(2,1)S(1)}, u32[]{:S(2)}, u32[]{:S(2)}) %collective-permute-start.11) | collective-permute-done | bytes 393248 | tf_op jit(solution)/shard_map/ppermute | solution.py:28
  93.4 0.9 constant_dynamic-update-slice_fusion.3
  94.4 0.9 constant_dynamic-update-slice_fusion.1
  95.4 0.1 slice.425
  95.5 0.1 slice_multiply_fusion.1
  95.5 1.3 fusion.149
  96.8 1.3 fusion.147
  98.1 1.2 convolution_bitcast_fusion.2
  99.3 1.2 fusion.65
  100.6 2.8 %fusion.62 = f32[4,512,128]{1,2,0:T(8,128)} fusion(f32[4,64,512]{2,1,0:T(8,128)S(1)} %bitcast.221, bf16[4,64,512]{2,1,0:T(8,128)(2,1)} %get-tuple-element.41, bf16[4,64,512]{2,1,0:T(8,128)(2,1)} %get-tuple-element.42, bf16[4,64,512]{2,1,0:T(8,128)(2,1)} %get-tuple-element.34, bf16[4,64,512]{2,1,0:T(8,128)(2,1)} %get-tuple-element.33, ...), kind=kOutput, calls=%fused_computation.70 | convolution fusion | flops 105119744 | bytes 2818048 | tf_op jit(solution)/shard_map/bkj,bkr->bjr/dot_general | solution.py:128
  103.4 0.0 copy-start.8
  103.4 3.5 %fusion.57 = f32[8,512,128]{1,2,0:T(8,128)} fusion(f32[8,64,512]{2,1,0:T(8,128)} %bitcast.220, bf16[8,64,512]{2,1,0:T(8,128)(2,1)S(1)} %copy-done.11, bf16[8,64,512]{2,1,0:T(8,128)(2,1)S(1)} %copy-done.12, bf16[8,64,512]{2,1,0:T(8,128)(2,1)S(1)} %copy-done.10, bf16[8,64,512]{2,1,0:T(8,128)(2,1)S(1)} %copy-done.9, bf16[63,64,256]{2,1,0:T(8,128)(2,1)} %param.12, ...), kind=kOutput, calls=%fused_computation.58 | convolution fusion | flops 210239488 | bytes 5636096 | tf_op jit(solution)/shard_map/bkj,bkr->bjr/dot_general | solution.py:128
  106.9 5.2 %fusion.45 = f32[16,512,128]{1,2,0:T(8,128)} fusion(f32[16,64,512]{2,1,0:T(8,128)} %bitcast.219, bf16[16,64,512]{2,1,0:T(8,128)(2,1)} %get-tuple-element.19, bf16[16,64,512]{2,1,0:T(8,128)(2,1)} %get-tuple-element.20, bf16[16,64,512]{2,1,0:T(8,128)(2,1)} %get-tuple-element.16, bf16[16,64,512]{2,1,0:T(8,128)(2,1)} %get-tuple-element.15, ...), kind=kOutput, calls=%fused_computation.52 | convolution fusion | flops 420478976 | bytes 11272192 | tf_op jit(solution)/shard_map/bkj,bkr->bjr/dot_general | solution.py:128
  112.2 7.8 %fusion.25 = f32[32,512,128]{1,2,0:T(8,128)} fusion(bf16[32,64,128]{2,1,0:T(8,128)(2,1)S(1)} %copy-done, f32[32,64,512]{2,1,0:T(8,128)} %bitcast.218, bf16[32,64,512]{2,1,0:T(8,128)(2,1)} %get-tuple-element.11, bf16[32,64,512]{2,1,0:T(8,128)(2,1)} %get-tuple-element.12, bf16[32,64,512]{2,1,0:T(8,128)(2,1)} %get-tuple-element.8, ...), kind=kOutput, calls=%fused_computation.32 | convolution fusion | flops 840957952 | bytes 22544384 | tf_op jit(solution)/shard_map/ikp,ikr->ipr/dot_general | solution.py:138
  120.0 13.0 %fusion.8 = bf16[32,128,512]{2,1,0:T(8,128)(2,1)} fusion(f32[32,512,128]{1,2,0:T(8,128)} %fusion.25, f32[32,128,512]{2,1,0:T(8,128)} %fusion.88, f32[32,512,128]{1,2,0:T(8,128)} %fusion.11, f32[32]{0:T(128)S(1)} %copy-done.41, f32[32]{0:T(128)S(1)} %copy-done.42, f32[32]{0:T(128)S(1)} %copy-done.40, bf16[1,128,512]{2,1,0:T(8,128)(2,1)} %collective-permute-done.1, ...), kind=kOutput, calls=%fused_computation.9 | convolution fusion | flops 559939584 | bytes 34734464 | tf_op jit(solution)/shard_map/ipq,iqr->ipr/dot_general | solution.py:51
  (98 shorter events, 0.3 us)
Async XLA Ops:
  0.0 1.0 copy-start
  1.0 3.0 %copy-start.7 = (bf16[31,64,128]{2,1,0:T(8,128)(2,1)S(1)}, bf16[31,64,128]{2,1,0:T(8,128)(2,1)}, u32[]{:S(2)}) copy-start(bf16[31,64,128]{2,1,0:T(8,128)(2,1)} %param.11) | copy-start | bytes 1523716
  4.0 7.3 %copy-start.1 = (bf16[4096,512]{1,0:T(8,128)(2,1)S(1)}, bf16[4096,512]{1,0:T(8,128)(2,1)}, u32[]{:S(2)}) copy-start(bf16[4096,512]{1,0:T(8,128)(2,1)} %param.7) | copy-start | bytes 12582916
  4.5 21.3 %copy-start.2 = (bf16[16,512,64]{1,2,0:T(8,128)(2,1)}, bf16[16,512,64]{1,2,0:T(8,128)(2,1)S(1)}, u32[]{:S(2)}) copy-start(bf16[16,512,64]{1,2,0:T(8,128)(2,1)S(1)} %convolution_convert_fusion.1) | copy-start | bytes 3145732
  4.5 16.8 %copy-start.36 = (s32[63,4]{0,1:T(4,128)S(1)}, s32[63,4]{0,1:T(4,128)}, u32[]{:S(2)}) copy-start(s32[63,4]{0,1:T(4,128)} %param.13) | copy-start | bytes 3028
  4.8 20.5 %copy-start.37 = (s32[32,3]{0,1:T(4,128)S(1)}, s32[32,3]{0,1:T(4,128)}, u32[]{:S(2)}) copy-start(s32[32,3]{0,1:T(4,128)} %param.9) | copy-start | bytes 1156
  5.4 0.6 copy-start.5
  6.7 41.0 %collective-permute-start.12 = (bf16[1,3,64,512]{3,2,1,0:T(8,128)(2,1)}, bf16[1,3,64,512]{3,2,1,0:T(8,128)(2,1)}, u32[]{:S(2)}, u32[]{:S(2)}) collective-permute-start(bf16[1,3,64,512]{3,2,1,0:T(8,128)(2,1)} %maximum_bitcast_fusion.3), channel_id=1, source_target_pairs={{1,0},{2,1},{3,2},{4,3},{5,4},{6,5},{7,6},{8,7},{9,8},{10,9},{11,1... | collective-permute-start | bytes 589832 | tf_op jit(solution)/shard_map/ppermute | solution.py:28
  9.4 40.3 %collective-permute-start.10 = (bf16[1,3,64,512]{3,2,1,0:T(8,128)(2,1)}, bf16[1,3,64,512]{3,2,1,0:T(8,128)(2,1)}, u32[]{:S(2)}, u32[]{:S(2)}) collective-permute-start(bf16[1,3,64,512]{3,2,1,0:T(8,128)(2,1)} %maximum_bitcast_fusion.3), channel_id=1, source_target_pairs={{0,1},{1,2},{2,3},{3,4},{4,5},{5,6},{6,7},{7,8},{8,9},{9,10},{10,1... | collective-permute-start | bytes 589832 | tf_op jit(solution)/shard_map/ppermute | solution.py:28
  12.1 107.9 %collective-permute-start.1 = (bf16[1,128,512]{2,1,0:T(8,128)(2,1)}, bf16[1,128,512]{2,1,0:T(8,128)(2,1)}, u32[]{:S(2)}, u32[]{:S(2)}) collective-permute-start(bf16[1,128,512]{2,1,0:T(8,128)(2,1)} %get-tuple-element.5), channel_id=1, source_target_pairs={{1,0},{2,1},{3,2},{4,3},{5,4},{6,5},{7,6},{8,7},{9,8},{10,9},{11,1... | collective-permute-start | bytes 393224 | tf_op jit(solution)/shard_map/ppermute | solution.py:20
  16.6 19.3 %collective-permute-start = (bf16[1,128,512]{2,1,0:T(8,128)(2,1)}, bf16[1,128,512]{2,1,0:T(8,128)(2,1)}, u32[]{:S(2)}, u32[]{:S(2)}) collective-permute-start(bf16[1,128,512]{2,1,0:T(8,128)(2,1)} %get-tuple-element.6), channel_id=1, source_target_pairs={{0,1},{1,2},{2,3},{3,4},{4,5},{5,6},{6,7},{7,8},{8,9},{9,10},{10,1... | collective-permute-start | bytes 393224 | tf_op jit(solution)/shard_map/ppermute | solution.py:17
  19.3 36.3 %collective-permute-start.8 = (bf16[3,64,512]{2,1,0:T(8,128)(2,1)}, bf16[3,64,512]{2,1,0:T(8,128)(2,1)}, u32[]{:S(2)}, u32[]{:S(2)}) collective-permute-start(bf16[3,64,512]{2,1,0:T(8,128)(2,1)} %get-tuple-element.43), channel_id=1, source_target_pairs={{0,1},{1,2},{2,3},{3,4},{4,5},{5,6},{6,7},{7,8},{8,9},{9,10},{10,1... | collective-permute-start | bytes 589832 | tf_op jit(solution)/shard_map/ppermute | solution.py:17
  35.9 11.8 %copy-start.16 = (bf16[3,64,512]{2,1,0:T(8,128)(2,1)S(1)}, bf16[3,64,512]{2,1,0:T(8,128)(2,1)}, u32[]{:S(2)}) copy-start(bf16[3,64,512]{2,1,0:T(8,128)(2,1)} %get-tuple-element.13) | copy-start | bytes 589828
  35.9 13.9 %copy-start.15 = (bf16[3,64,512]{2,1,0:T(8,128)(2,1)S(1)}, bf16[3,64,512]{2,1,0:T(8,128)(2,1)}, u32[]{:S(2)}) copy-start(bf16[3,64,512]{2,1,0:T(8,128)(2,1)} %get-tuple-element.14) | copy-start | bytes 589828
  35.9 19.7 %copy-start.18 = (bf16[3,64,512]{2,1,0:T(8,128)(2,1)S(1)}, bf16[3,64,512]{2,1,0:T(8,128)(2,1)}, u32[]{:S(2)}) copy-start(bf16[3,64,512]{2,1,0:T(8,128)(2,1)} %get-tuple-element.31) | copy-start | bytes 589828
  35.9 21.7 %copy-start.17 = (bf16[3,64,512]{2,1,0:T(8,128)(2,1)S(1)}, bf16[3,64,512]{2,1,0:T(8,128)(2,1)}, u32[]{:S(2)}) copy-start(bf16[3,64,512]{2,1,0:T(8,128)(2,1)} %get-tuple-element.32) | copy-start | bytes 589828
  35.9 26.2 %copy-start.32 = (bf16[4]{0:T(256)(128)(2,1)S(1)}, bf16[4]{0:T(256)(128)(2,1)}, u32[]{:S(2)}) copy-start(bf16[4]{0:T(256)(128)(2,1)} %get-tuple-element.62) | copy-start | bytes 28
  35.9 26.2 %copy-start.33 = (bf16[4]{0:T(256)(128)(2,1)S(1)}, bf16[4]{0:T(256)(128)(2,1)}, u32[]{:S(2)}) copy-start(bf16[4]{0:T(256)(128)(2,1)} %get-tuple-element.63) | copy-start | bytes 28
  35.9 26.2 %copy-start.34 = (bf16[4]{0:T(256)(128)(2,1)S(1)}, bf16[4]{0:T(256)(128)(2,1)}, u32[]{:S(2)}) copy-start(bf16[4]{0:T(256)(128)(2,1)} %get-tuple-element.64) | copy-start | bytes 28
  35.9 26.2 %copy-start.35 = (bf16[4]{0:T(256)(128)(2,1)S(1)}, bf16[4]{0:T(256)(128)(2,1)}, u32[]{:S(2)}) copy-start(bf16[4]{0:T(256)(128)(2,1)} %get-tuple-element.65) | copy-start | bytes 28
  35.9 21.6 %collective-permute-start.9 = (bf16[3,64,512]{2,1,0:T(8,128)(2,1)}, bf16[3,64,512]{2,1,0:T(8,128)(2,1)S(1)}, u32[]{:S(2)}, u32[]{:S(2)}) collective-permute-start(bf16[3,64,512]{2,1,0:T(8,128)(2,1)} %get-tuple-element.44), channel_id=1, source_target_pairs={{1,0},{2,1},{3,2},{4,3},{5,4},{6,5},{7,6},{8,7},{9,8},{10,9},{11,1... | collective-permute-start | bytes 589832 | tf_op jit(solution)/shard_map/ppermute | solution.py:20
  47.6 16.6 %copy-start.14 = (bf16[3,64,512]{2,1,0:T(8,128)(2,1)S(1)}, bf16[3,64,512]{2,1,0:T(8,128)(2,1)}, u32[]{:S(2)}) copy-start(bf16[3,64,512]{2,1,0:T(8,128)(2,1)} %get-tuple-element.21) | copy-start | bytes 589828
  47.6 18.6 %copy-start.13 = (bf16[3,64,512]{2,1,0:T(8,128)(2,1)S(1)}, bf16[3,64,512]{2,1,0:T(8,128)(2,1)}, u32[]{:S(2)}) copy-start(bf16[3,64,512]{2,1,0:T(8,128)(2,1)} %get-tuple-element.22) | copy-start | bytes 589828
  47.6 23.1 %copy-start.28 = (bf16[8]{0:T(256)(128)(2,1)S(1)}, bf16[8]{0:T(256)(128)(2,1)}, u32[]{:S(2)}) copy-start(bf16[8]{0:T(256)(128)(2,1)} %get-tuple-element.58) | copy-start | bytes 52
  47.6 23.2 %copy-start.29 = (bf16[8]{0:T(256)(128)(2,1)S(1)}, bf16[8]{0:T(256)(128)(2,1)}, u32[]{:S(2)}) copy-start(bf16[8]{0:T(256)(128)(2,1)} %get-tuple-element.59) | copy-start | bytes 52
  47.6 23.2 %copy-start.30 = (bf16[8]{0:T(256)(128)(2,1)S(1)}, bf16[8]{0:T(256)(128)(2,1)}, u32[]{:S(2)}) copy-start(bf16[8]{0:T(256)(128)(2,1)} %get-tuple-element.60) | copy-start | bytes 52
  47.6 23.2 %copy-start.31 = (bf16[8]{0:T(256)(128)(2,1)S(1)}, bf16[8]{0:T(256)(128)(2,1)}, u32[]{:S(2)}) copy-start(bf16[8]{0:T(256)(128)(2,1)} %get-tuple-element.61) | copy-start | bytes 52
  47.7 26.3 %collective-permute-start.2 = (bf16[3,64,512]{2,1,0:T(8,128)(2,1)S(1)}, bf16[3,64,512]{2,1,0:T(8,128)(2,1)S(1)}, u32[]{:S(2)}, u32[]{:S(2)}) collective-permute-start(bf16[3,64,512]{2,1,0:T(8,128)(2,1)S(1)} %copy-done.16), channel_id=1, source_target_pairs={{0,1},{1,2},{2,3},{3,4},{4,5},{5,6},{6,7},{7,8},{8,9},{9,10},{10,1... | collective-permute-start | bytes 589832 | tf_op jit(solution)/shard_map/ppermute | solution.py:17
  49.8 26.1 %collective-permute-start.3 = (bf16[3,64,512]{2,1,0:T(8,128)(2,1)S(1)}, bf16[3,64,512]{2,1,0:T(8,128)(2,1)S(1)}, u32[]{:S(2)}, u32[]{:S(2)}) collective-permute-start(bf16[3,64,512]{2,1,0:T(8,128)(2,1)S(1)} %copy-done.15), channel_id=1, source_target_pairs={{1,0},{2,1},{3,2},{4,3},{5,4},{6,5},{7,6},{8,7},{9,8},{10,9},{11,1... | collective-permute-start | bytes 589832 | tf_op jit(solution)/shard_map/ppermute | solution.py:20
  55.6 8.6 %collective-permute-start.6 = (bf16[3,64,512]{2,1,0:T(8,128)(2,1)S(1)}, bf16[3,64,512]{2,1,0:T(8,128)(2,1)S(1)}, u32[]{:S(2)}, u32[]{:S(2)}) collective-permute-start(bf16[3,64,512]{2,1,0:T(8,128)(2,1)S(1)} %copy-done.18), channel_id=1, source_target_pairs={{0,1},{1,2},{2,3},{3,4},{4,5},{5,6},{6,7},{7,8},{8,9},{9,10},{10,1... | collective-permute-start | bytes 589832 | tf_op jit(solution)/shard_map/ppermute | solution.py:17
  57.6 8.6 %collective-permute-start.7 = (bf16[3,64,512]{2,1,0:T(8,128)(2,1)S(1)}, bf16[3,64,512]{2,1,0:T(8,128)(2,1)S(1)}, u32[]{:S(2)}, u32[]{:S(2)}) collective-permute-start(bf16[3,64,512]{2,1,0:T(8,128)(2,1)S(1)} %copy-done.17), channel_id=1, source_target_pairs={{1,0},{2,1},{3,2},{4,3},{5,4},{6,5},{7,6},{8,7},{9,8},{10,9},{11,1... | collective-permute-start | bytes 589832 | tf_op jit(solution)/shard_map/ppermute | solution.py:20
  62.2 10.1 %copy-start.23 = (bf16[2]{0:T(256)(128)(2,1)S(1)}, bf16[2]{0:T(256)(128)(2,1)}, u32[]{:S(2)}) copy-start(bf16[2]{0:T(256)(128)(2,1)} %get-tuple-element.68) | copy-start | bytes 16
  62.2 18.7 %copy-start.24 = (bf16[32]{0:T(256)(128)(2,1)S(1)}, bf16[32]{0:T(256)(128)(2,1)}, u32[]{:S(2)}) copy-start(bf16[32]{0:T(256)(128)(2,1)} %get-tuple-element.50) | copy-start | bytes 196
  62.2 18.7 %copy-start.25 = (bf16[32]{0:T(256)(128)(2,1)S(1)}, bf16[32]{0:T(256)(128)(2,1)}, u32[]{:S(2)}) copy-start(bf16[32]{0:T(256)(128)(2,1)} %get-tuple-element.51) | copy-start | bytes 196
  62.2 18.7 %copy-start.26 = (bf16[32]{0:T(256)(128)(2,1)S(1)}, bf16[32]{0:T(256)(128)(2,1)}, u32[]{:S(2)}) copy-start(bf16[32]{0:T(256)(128)(2,1)} %get-tuple-element.52) | copy-start | bytes 196
  62.2 18.7 %copy-start.27 = (bf16[32]{0:T(256)(128)(2,1)S(1)}, bf16[32]{0:T(256)(128)(2,1)}, u32[]{:S(2)}) copy-start(bf16[32]{0:T(256)(128)(2,1)} %get-tuple-element.53) | copy-start | bytes 196
  64.3 21.7 %collective-permute-start.4 = (bf16[3,64,512]{2,1,0:T(8,128)(2,1)S(1)}, bf16[3,64,512]{2,1,0:T(8,128)(2,1)S(1)}, u32[]{:S(2)}, u32[]{:S(2)}) collective-permute-start(bf16[3,64,512]{2,1,0:T(8,128)(2,1)S(1)} %copy-done.14), channel_id=1, source_target_pairs={{0,1},{1,2},{2,3},{3,4},{4,5},{5,6},{6,7},{7,8},{8,9},{9,10},{10,1... | collective-permute-start | bytes 589832 | tf_op jit(solution)/shard_map/ppermute | solution.py:17
  66.2 19.8 %collective-permute-start.5 = (bf16[3,64,512]{2,1,0:T(8,128)(2,1)S(1)}, bf16[3,64,512]{2,1,0:T(8,128)(2,1)S(1)}, u32[]{:S(2)}, u32[]{:S(2)}) collective-permute-start(bf16[3,64,512]{2,1,0:T(8,128)(2,1)S(1)} %copy-done.13), channel_id=1, source_target_pairs={{1,0},{2,1},{3,2},{4,3},{5,4},{6,5},{7,6},{8,7},{9,8},{10,9},{11,1... | collective-permute-start | bytes 589832 | tf_op jit(solution)/shard_map/ppermute | solution.py:20
  73.9 19.4 %collective-permute-start.11 = (bf16[2,3,64,512]{3,2,1,0:T(8,128)(2,1)S(1)}, bf16[2,3,64,512]{3,2,1,0:T(8,128)(2,1)S(1)}, u32[]{:S(2)}, u32[]{:S(2)}) collective-permute-start(bf16[2,3,64,512]{3,2,1,0:T(8,128)(2,1)S(1)} %get-tuple-element.45), channel_id=1, source_target_pairs={{0,2},{1,3},{2,4},{3,5},{4,6},{5,7},{6,8},{7,9},{8,10},{9,11},{10,... | collective-permute-start | bytes 1179656 | tf_op jit(solution)/shard_map/ppermute | solution.py:28
  75.9 19.4 %collective-permute-start.13 = (bf16[2,3,64,512]{3,2,1,0:T(8,128)(2,1)S(1)}, bf16[2,3,64,512]{3,2,1,0:T(8,128)(2,1)S(1)}, u32[]{:S(2)}, u32[]{:S(2)}) collective-permute-start(bf16[2,3,64,512]{3,2,1,0:T(8,128)(2,1)S(1)} %get-tuple-element.46), channel_id=1, source_target_pairs={{2,0},{3,1},{4,2},{5,3},{6,4},{7,5},{8,6},{9,7},{10,8},{11,9},{12,... | collective-permute-start | bytes 1179656 | tf_op jit(solution)/shard_map/ppermute | solution.py:28
  80.9 4.1 %copy-start.22 = (bf16[2]{0:T(256)(128)(2,1)S(1)}, bf16[2]{0:T(256)(128)(2,1)}, u32[]{:S(2)}) copy-start(bf16[2]{0:T(256)(128)(2,1)} %get-tuple-element.69) | copy-start | bytes 16
  80.9 5.1 %copy-start.3 = (bf16[16,512,64]{1,2,0:T(8,128)(2,1)S(1)}, bf16[16,512,64]{1,2,0:T(8,128)(2,1)}, u32[]{:S(2)}) copy-start(bf16[16,512,64]{1,2,0:T(8,128)(2,1)} %copy-done.2) | copy-start | bytes 3145732
  80.9 5.1 %copy-start.21 = (bf16[16]{0:T(256)(128)(2,1)S(1)}, bf16[16]{0:T(256)(128)(2,1)}, u32[]{:S(2)}) copy-start(bf16[16]{0:T(256)(128)(2,1)} %get-tuple-element.57) | copy-start | bytes 100
  86.0 8.3 %copy-start.6 = (bf16[1,64,512]{2,1,0:T(8,128)(2,1)S(1)}, bf16[1,64,512]{2,1,0:T(8,128)(2,1)}, u32[]{:S(2)}) copy-start(bf16[1,64,512]{2,1,0:T(8,128)(2,1)} %copy-done.5) | copy-start | bytes 196612
  93.3 2.1 %copy-start.38 = (bf16[2]{0:T(256)(128)(2,1)S(1)}, bf16[2]{0:T(256)(128)(2,1)}, u32[]{:S(2)}) copy-start(bf16[2]{0:T(256)(128)(2,1)} %get-tuple-element.66) | copy-start | bytes 16
  93.4 2.1 %copy-start.39 = (bf16[2]{0:T(256)(128)(2,1)S(1)}, bf16[2]{0:T(256)(128)(2,1)}, u32[]{:S(2)}) copy-start(bf16[2]{0:T(256)(128)(2,1)} %get-tuple-element.67) | copy-start | bytes 16
  94.3 3.7 %copy-start.20 = (bf16[2,64,64]{1,0,2:T(2,128)(2,1)S(1)}, bf16[2,64,64]{1,0,2:T(2,128)(2,1)}, u32[]{:S(2)}) copy-start(bf16[2,64,64]{1,0,2:T(2,128)(2,1)} %dot_general.110) | copy-start | bytes 49156
  95.4 3.9 %copy-start.19 = (bf16[2,64,512]{2,1,0:T(8,128)(2,1)S(1)}, bf16[2,64,512]{2,1,0:T(8,128)(2,1)}, u32[]{:S(2)}) copy-start(bf16[2,64,512]{2,1,0:T(8,128)(2,1)} %fusion.140) | copy-start | bytes 393220
  100.5 2.9 %copy-start.9 = (bf16[8,64,512]{2,1,0:T(8,128)(2,1)S(1)}, bf16[8,64,512]{2,1,0:T(8,128)(2,1)}, u32[]{:S(2)}) copy-start(bf16[8,64,512]{2,1,0:T(8,128)(2,1)} %get-tuple-element.25) | copy-start | bytes 1572868
  100.5 2.9 %copy-start.10 = (bf16[8,64,512]{2,1,0:T(8,128)(2,1)S(1)}, bf16[8,64,512]{2,1,0:T(8,128)(2,1)}, u32[]{:S(2)}) copy-start(bf16[8,64,512]{2,1,0:T(8,128)(2,1)} %get-tuple-element.26) | copy-start | bytes 1572868
  100.5 2.9 %copy-start.11 = (bf16[8,64,512]{2,1,0:T(8,128)(2,1)S(1)}, bf16[8,64,512]{2,1,0:T(8,128)(2,1)}, u32[]{:S(2)}) copy-start(bf16[8,64,512]{2,1,0:T(8,128)(2,1)} %get-tuple-element.29) | copy-start | bytes 1572868
  100.6 2.9 %copy-start.12 = (bf16[8,64,512]{2,1,0:T(8,128)(2,1)S(1)}, bf16[8,64,512]{2,1,0:T(8,128)(2,1)}, u32[]{:S(2)}) copy-start(bf16[8,64,512]{2,1,0:T(8,128)(2,1)} %get-tuple-element.30) | copy-start | bytes 1572868
  103.4 3.5 %copy-start.8 = (bf16[31,64,128]{2,1,0:T(8,128)(2,1)S(1)}, bf16[31,64,128]{2,1,0:T(8,128)(2,1)}, u32[]{:S(2)}) copy-start(bf16[31,64,128]{2,1,0:T(8,128)(2,1)} %param.11) | copy-start | bytes 1523716
  106.9 5.2 %copy-start.4 = (bf16[32,64,512]{2,1,0:T(8,128)(2,1)S(1)}, bf16[32,64,512]{2,1,0:T(8,128)(2,1)}, u32[]{:S(2)}) copy-start(bf16[32,64,512]{2,1,0:T(8,128)(2,1)} %get-tuple-element.7) | copy-start | bytes 6291460
  112.1 7.8 %copy-start.40 = (f32[32]{0:T(128)S(1)}, f32[32]{0:T(128)}, u32[]{:S(2)}) copy-start(f32[32]{0:T(128)} %get-tuple-element.47) | copy-start | bytes 388
  112.2 7.8 %copy-start.41 = (f32[32]{0:T(128)S(1)}, f32[32]{0:T(128)}, u32[]{:S(2)}) copy-start(f32[32]{0:T(128)} %get-tuple-element.48) | copy-start | bytes 388
  112.2 7.8 %copy-start.42 = (f32[32]{0:T(128)S(1)}, f32[32]{0:T(128)}, u32[]{:S(2)}) copy-start(f32[32]{0:T(128)} %get-tuple-element.49) | copy-start | bytes 388
where the time goes:
time: 135 us; the launch traced here: 133 us
  matrix products  51.7 us (38%)
  starting transfers between devices  44.1 us (33%)
  other arithmetic  17.4 us (13%)
  local copies, waits for them, and re-layouts  14.1 us (10%)
  waiting for transfers between devices  4.79 us (4%)
    dot_general x3, matrix products, body(): jnp.einsum('ipq,iqr->ipr', near_blocks[:, column], rimmed[column:column +...  25.8 us
    ppermute x5, starting transfers between devices, padded_2(): lax.ppermute(lax.slice_in_dim(block, 0, width, axis=dim), axis, backward)  22.8 us
    mul x9, other arithmetic, couple(): padded[position:position + box_count] * flags[:, column][:, None, None]  15.4 us
    dot_general x5, matrix products, body(): jnp.einsum('bkj,bkr->bjr', matrix, expansions[tree_level].astype(jnp.bflo...  13.9 us
    ppermute x4, starting transfers between devices, shifted(): return lax.ppermute(array, axis, pairs)  11.5 us
    ppermute x5, starting transfers between devices, padded_2(): lax.ppermute(lax.slice_in_dim(block, block.shape[dim] - width, None, axis...  9.72 us
    dot_general x1, matrix products, body(): jnp.einsum('ikp,ikr->ipr', leaf_basis, leaf_local, preferred_element_type...  7.8 us
    ppermute x4, waiting for transfers between devices, shifted(): return lax.ppermute(array, axis, pairs)  4.76 us
  transfers between devices with their start and end apart: 14, of which 1 were waited for; matrix products, arithmetic and copies ran while one was open for 48% of the time, Pallas kernels for 0%

commit v1 on v0

v1 whole, which is shorter than its diff:
```python
import jax
import jax.numpy as jnp
from jax import lax
from jax.experimental import pallas as pl
from jax.experimental.pallas import tpu as pltpu
from jax.sharding import PartitionSpec as P

LEVELS = 6
FULL = LEVELS - 2
BF = jnp.bfloat16
F32 = jnp.float32
MIB = 1 << 20


def resident(shape, dtype):
    return pltpu.VMEM(shape, dtype)


def keep(array):
    return pltpu.with_memory_space_constraint(array, pltpu.VMEM)


def stay(array):
    return pltpu.with_memory_space_constraint(array, pltpu.HBM)


def dot(a, b):
    return lax.dot_general(a, b, (((1,), (0,)), ((), ())), preferred_element_type=F32)


def dot_t(a, b):
    return lax.dot_general(a, b, (((0,), (0,)), ((), ())), preferred_element_type=F32)


class Plan:
    def __init__(self, leaves, panels, rank, rhs):
        self.leaves, self.panels, self.rank, self.rhs = leaves, panels, rank, rhs
        self.count = [leaves >> level for level in range(LEVELS)]
        self.first = [sum(self.count[:level]) for level in range(LEVELS)]
        self.trans = [0] + [sum(self.count[1:level]) for level in range(1, LEVELS)]
        self.padded = [sum(c + 6 for c in self.count[:level]) for level in range(FULL)]
        self.padded_boxes = sum(c + 6 for c in self.count[:FULL])
        self.inner_boxes = sum(self.count[:FULL])
        self.msg_pole = [panels + 2 * rank * level for level in range(FULL)]
        self.msg_top = panels + 2 * rank * FULL
        self.msg_trans = self.msg_top + rank
        self.msg_basis = self.msg_trans + rank
        self.basis_rows = rank * panels // rhs
        self.msg_rows = self.msg_basis + self.basis_rows


def upward_kernel(plan, chunks, charges, basis, transfers, padded_x, poles, up, down, up2, down2, top, bs, ts, sems):
    p, r = plan.panels, plan.rank
    per = plan.leaves // chunks
    copies = [
        pltpu.make_async_copy(basis, bs, sems.at[chunks]),
        pltpu.make_async_copy(transfers, ts, sems.at[chunks + 1]),
    ]
    for c in range(chunks):
        rows = per * p
        copies.append(
            pltpu.make_async_copy(
                charges.at[pl.ds(c * rows, rows)], padded_x.at[pl.ds(p + c * rows, rows)], sems.at[c]
            )
        )
    for copy in copies:
        copy.start()
    padded_x[pl.ds(0, p)] = jnp.zeros((p, plan.rhs), BF)
    padded_x[pl.ds(p * (plan.leaves + 1), p)] = jnp.zeros((p, plan.rhs), BF)
    for level in range(FULL):
        start = plan.padded[level] * r
        poles[pl.ds(start, 3 * r)] = jnp.zeros((3 * r, plan.rhs), BF)
        poles[pl.ds(start + (plan.count[level] + 3) * r, 3 * r)] = jnp.zeros((3 * r, plan.rhs), BF)
    copies[0].wait()
    copies[1].wait()

    held = {}

    def keep(level, box, value):
        held[level, box] = value
        n = plan.count[level]
        if level < FULL:
            poles[pl.ds((plan.padded[level] + 3 + box) * r, r)] = value
            if n - 3 <= box <= n - 2:
                up[pl.ds(plan.msg_pole[level] + (box - n + 3) * r, r)] = value
            if 1 <= box <= 2:
                down[pl.ds(plan.msg_pole[level] + (box - 1) * r, r)] = value
        elif level == FULL:
            if box == 0:
                up[pl.ds(plan.msg_top, r)] = value
                down2[pl.ds(0, r)] = value
            else:
                down[pl.ds(plan.msg_top, r)] = value
                up2[pl.ds(0, r)] = value
        else:
            up2[pl.ds(r, r)] = value
            down2[pl.ds(r, r)] = value
            top[...] = value

    def climb(level, box):
        pair = jnp.concatenate([held[level - 1, 2 * box], held[level - 1, 2 * box + 1]], axis=0)
        keep(level, box, dot(ts[plan.trans[level] + box], pair).astype(BF))

    for c in range(chunks):
        copies[2 + c].wait()
        for leaf in range(c * per, (c + 1) * per):
            x = padded_x[pl.ds(p * (leaf + 1), p)]
            keep(0, leaf, dot(bs[leaf], x).astype(BF))
            box = leaf
            for level in range(1, LEVELS):
                if box % 2 == 0:
                    break
                box //= 2
                climb(level, box)
    for message, leaf, last in ((up, plan.leaves - 1, True), (down, 0, False)):
        message[pl.ds(0, p)] = padded_x[pl.ds(p * (leaf + 1), p)]
        for level in range(1, FULL + 1):
            box = plan.count[level] - 1 if last else 0
            message[pl.ds(plan.msg_trans, r), pl.ds((level - 1) * p, p)] = ts[plan.trans[level] + box]
        for part in range(plan.rhs // p):
            rows = plan.basis_rows
            message[pl.ds(plan.msg_basis, rows), pl.ds(part * p, p)] = bs[leaf, pl.ds(part * rows, rows)]


def inner_kernel(
    plan, chunks, pattern, flags, padded_x, poles, near_blocks, couplings,
    near, local, masked, edge_near, nb, cb, sems,
):
    p, r = plan.panels, plan.rank
    per = plan.leaves // chunks
    coupling_copy = pltpu.make_async_copy(couplings, cb, sems.at[chunks])
    copies = [
        pltpu.make_async_copy(near_blocks.at[pl.ds(c * per, per)], nb.at[pl.ds(c * per, per)], sems.at[c])
        for c in range(chunks)
    ]
    coupling_copy.start()
    for copy in copies:
        copy.start()
    coupling_copy.wait()
    lane = lax.broadcasted_iota(jnp.int32, (r, 4 * r), 1)

    def mask(box):
        low = jnp.where(lane < r, flags[0, box], flags[1, box])
        high = jnp.where(lane < 3 * r, flags[2, box], flags[3, box])
        chosen = jnp.where(lane < 2 * r, low, high)
        value = cb[box] * chosen.astype(F32).astype(BF)
        masked[box] = value
        return value

    def couple(level):
        base = plan.padded[level]

        def one(box):
            row = (base + box) * r
            near_side = poles[pl.ds(pl.multiple_of(row, r), 2 * r)]
            far_side = poles[pl.ds(pl.multiple_of(row + 5 * r, r), 2 * r)]
            stack = jnp.concatenate([near_side, far_side], axis=0)
            index = plan.first[level] + box
            local[pl.ds(pl.multiple_of(index * r, r), r)] = dot(mask(index), stack)

        def pair(step, carry):
            for k in range(4):
                one(step * 4 + k)
            return carry

        lax.fori_loop(0, plan.count[level] // 4, pair, 0)

    for level in range(FULL):
        couple(level)
    for box in range(plan.inner_boxes, sum(plan.count)):
        mask(box)

    def side(leaf, slot):
        block = nb[leaf, slot]
        return jnp.where(pattern[slot, leaf] != 0, block, jnp.zeros_like(block))

    def near_one(leaf):
        row = pl.multiple_of(leaf * p, p)
        wide = jnp.concatenate([side(leaf, 0), nb[leaf, 1], side(leaf, 2)], axis=1)
        near[pl.ds(row, p)] = dot(wide, padded_x[pl.ds(row, 3 * p)])

    for c in range(chunks):
        copies[c].wait()

        def step(s, carry, c=c):
            for k in range(2):
                near_one(c * per + s * 2 + k)
            return carry

        lax.fori_loop(0, per // 2, step, 0)
    edge_near[0] = side(0, 0)
    edge_near[1] = side(plan.leaves - 1, 2)


def final_kernel(
    plan, near, local, masked, edge_near, bs, ts, below, above, below2, above2, below3, above3,
    out, loc, stage, sems,
):
    p, r, n = plan.panels, plan.rank, plan.leaves

    def edges(message, last):
        basis = jnp.concatenate(
            [message[pl.ds(plan.msg_basis, plan.basis_rows), pl.ds(k * p, p)] for k in range(plan.rhs // p)], axis=0
        )
        x = message[pl.ds(0, p)]
        rim = [dot(basis, x).astype(BF)]
        sent = [message[pl.ds(plan.msg_pole[level], 2 * r)] for level in range(FULL)]
        for level in range(1, FULL + 1):
            matrix = message[pl.ds(plan.msg_trans, r), pl.ds((level - 1) * p, p)]
            if last:
                pair = jnp.concatenate([sent[level - 1][r:], rim[-1]], axis=0)
            else:
                pair = jnp.concatenate([rim[-1], sent[level - 1][:r]], axis=0)
            rim.append(dot(matrix, pair).astype(BF))
        return x, rim, sent

    x_low, rim_low, sent_low = edges(below, True)
    x_high, rim_high, sent_high = edges(above, False)

    box = plan.first[LEVELS - 1]
    low = jnp.concatenate([below3[...], below2[pl.ds(r, r)]], axis=0)
    high = jnp.concatenate([above2[pl.ds(r, r)], above3[...]], axis=0)
    summit = dot(masked[box], jnp.concatenate([low, high], axis=0)).astype(BF)
    pushed = dot_t(ts[plan.trans[LEVELS - 1]], summit)
    top_low, top_high = below[pl.ds(plan.msg_top, r)], above[pl.ds(plan.msg_top, r)]
    second = []
    for k, stack in enumerate(
        (
            [below2[pl.ds(0, r)], top_low, rim_high[FULL], top_high],
            [top_low, rim_low[FULL], top_high, above2[pl.ds(0, r)]],
        )
    ):
        box = plan.first[FULL] + k
        gained = dot(masked[box], jnp.concatenate(stack, axis=0))
        second.append((gained + pushed[k * r : (k + 1) * r]).astype(BF))

    rims = []
    for level in range(FULL):
        first, m = plan.first[level], plan.count[level]
        low = jnp.concatenate([sent_low[level], rim_low[level]], axis=0)
        high = jnp.concatenate([rim_high[level], sent_high[level]], axis=0)
        gain = [
            (0, dot(masked[first, :, pl.ds(0, 2 * r)], low[: 2 * r])),
            (1, dot(masked[first + 1, :, pl.ds(0, 2 * r)], low[r:])),
            (2, dot(masked[first + 2, :, pl.ds(0, r)], low[2 * r :])),
            (m - 1, dot(masked[first + m - 1, :, pl.ds(2 * r, 2 * r)], high[r:])),
            (m - 2, dot(masked[first + m - 2, :, pl.ds(2 * r, 2 * r)], high[: 2 * r])),
            (m - 3, dot(masked[first + m - 3, :, pl.ds(3 * r, r)], high[:r])),
        ]
        sums = {}
        for place, value in gain:
            sums[place] = sums[place] + value if place in sums else value
        rims.append(sums)

    def gather(level, box, push):
        index = plan.first[level] + box
        value = local[pl.ds(index * r, r)] + push
        if box in rims[level]:
            value = value + rims[level][box]
        return value.astype(BF)

    current = second
    for level in range(FULL, 1, -1):
        lower = []
        for box, value in enumerate(current):
            push = dot_t(ts[plan.trans[level] + box], value)
            lower.append(gather(level - 1, 2 * box, push[:r]))
            lower.append(gather(level - 1, 2 * box + 1, push[r:]))
        current = lower

    writes = []
    for box, value in enumerate(current):
        push = dot_t(ts[plan.trans[1] + box], value)
        for k in range(2):
            leaf = 2 * box + k
            leaf_local = gather(0, leaf, push[k * r : (k + 1) * r])
            total = near[pl.ds(leaf * p, p)] + dot_t(bs[leaf], leaf_local)
            if leaf == 0:
                total = total + dot(edge_near[0], x_low)
            if leaf == n - 1:
                total = total + dot(edge_near[1], x_high)
            stage[pl.ds(leaf * p, p)] = total.astype(BF)
        if box % 2:
            rows = pl.ds((box - 1) * 2 * p, 4 * p)
            copy = pltpu.make_async_copy(stage.at[rows], out.at[rows], sems.at[box // 2])
            copy.start()
            writes.append(copy)
    for copy in writes:
        copy.wait()


def shifted(array, by):
    peers = lax.axis_size("slab")
    pairs = [(i, i + by) for i in range(peers) if 0 <= i + by < peers]
    return lax.ppermute(array, "slab", pairs)


def body(charges, near_blocks, near_pattern, leaf_basis, transfers, couplings, interactions):
    leaves, panels, rank, rhs = near_blocks.shape[0], near_blocks.shape[2], leaf_basis.shape[1], charges.shape[1]
    plan = Plan(leaves, panels, rank, rhs)
    hbm = pl.BlockSpec(memory_space=pltpu.HBM)
    vmem = pl.BlockSpec(memory_space=pltpu.VMEM)
    smem = pl.BlockSpec(memory_space=pltpu.SMEM)
    chunks = 8
    boxes, trans = couplings.shape[0], transfers.shape[0]

    padded_x, poles, up, down, up2, down2, top, bs, ts = pl.pallas_call(
        lambda *refs: upward_kernel(plan, chunks, *refs),
        in_specs=[hbm, hbm, hbm],
        out_specs=[vmem] * 9,
        out_shape=[
            resident(((leaves + 2) * panels, rhs), BF),
            resident((plan.padded_boxes * rank, rhs), BF),
            resident((plan.msg_rows, rhs), BF),
            resident((plan.msg_rows, rhs), BF),
            resident((2 * rank, rhs), BF),
            resident((2 * rank, rhs), BF),
            resident((rank, rhs), BF),
            resident(leaf_basis.shape, BF),
            resident(transfers.shape, BF),
        ],
        scratch_shapes=[pltpu.SemaphoreType.DMA((chunks + 2,))],
        compiler_params=pltpu.CompilerParams(vmem_limit_bytes=4 * MIB),
        name="upward",
    )(stay(charges), stay(leaf_basis), stay(transfers))

    below, above = shifted(up, 1), shifted(down, -1)
    below2, above2 = shifted(up2, 2), shifted(down2, -2)
    below3, above3 = shifted(top, 3), shifted(top, -3)

    near, local, masked, edge_near = pl.pallas_call(
        lambda *refs: inner_kernel(plan, chunks, *refs),
        in_specs=[smem, smem, vmem, vmem, hbm, hbm],
        out_specs=[vmem] * 4,
        out_shape=[
            resident((leaves * panels, rhs), F32),
            resident((plan.inner_boxes * rank, rhs), F32),
            resident(couplings.shape, BF),
            resident((2, panels, panels), BF),
        ],
        scratch_shapes=[
            pltpu.VMEM(near_blocks.shape, BF),
            pltpu.VMEM(couplings.shape, BF),
            pltpu.SemaphoreType.DMA((chunks + 1,)),
        ],
        cost_estimate=pl.CostEstimate(flops=12_000_000_000, bytes_accessed=16 * MIB, transcendentals=0),
        compiler_params=pltpu.CompilerParams(vmem_limit_bytes=12 * MIB),
        name="inner",
    )(near_pattern.T, interactions.T, keep(padded_x), keep(poles), stay(near_blocks), stay(couplings))

    return pl.pallas_call(
        lambda *refs: final_kernel(plan, *refs),
        in_specs=[vmem] * 12,
        out_specs=hbm,
        out_shape=jax.ShapeDtypeStruct((leaves * panels, rhs), BF),
        scratch_shapes=[
            pltpu.VMEM((rank, rhs), BF),
            pltpu.VMEM((leaves * panels, rhs), BF),
            pltpu.SemaphoreType.DMA((leaves // 4,)),
        ],
        compiler_params=pltpu.CompilerParams(vmem_limit_bytes=12 * MIB),
        name="final",
    )(
        keep(near), keep(local), keep(masked), keep(edge_near), keep(bs), keep(ts),
        keep(below), keep(above), keep(below2), keep(above2), keep(below3), keep(above3),
    )


def solution(mesh):
    spec = ("groups", "slab")
    in_specs = (
        P(spec, None),
        P(spec, None, None, None),
        P(spec, None),
        P(spec, None, None),
        P(spec, None, None),
        P(spec, None, None),
        P(spec, None),
    )
    return jax.shard_map(body, mesh=mesh, in_specs=in_specs, out_specs=P(spec, None), check_vma=False)
```

time: 135 us -> 49 us (0.36); the launches traced: 133 us -> 48.8 us
  matrix products: 51.7 us -> 0 us
  Pallas kernels: 0 us -> 26.2 us
  starting transfers between devices: 44.1 us -> 18.8 us
  other arithmetic: 17.4 us -> 0 us
  local copies, waits for them, and re-layouts: 14.1 us -> 0.01 us
    dot_general x15 -> x0, matrix products: 51.7 us -> none  [the longest x3 25.8 us: body(): jnp.einsum('ipq,iqr->ipr', near_blocks[:, column], rimmed[column:column +...]
    pallas_call x0 -> x3, Pallas kernels: none -> 26.2 us  [the longest x1 11.6 us: body(): pl.pallas_call(lambda *refs: inner_kernel(plan, chunks, *refs), in_specs=...]
    ppermute x14 -> x6, starting transfers between devices: 44.1 us -> 18.8 us  [shifted(): return lax.ppermute(array, 'slab', pairs)]
    mul x9 -> x0, other arithmetic: 15.4 us -> none  [couple(): padded[position:position + box_count] * flags[:, column][:, None, None]]
    slice x7 -> x0, local copies, waits for them, and re-layouts: 4.65 us -> none  [the longest x4 3.17 us: padded_2(): lax.slice_in_dim(block, block.shape[dim] - width, None, axis=dim)]
    unnamed x89 -> x4, local copies, waits for them, and re-layouts: 3.75 us -> 0.01 us
    mul x6 -> x0, local copies, waits for them, and re-layouts: 3.71 us -> none  [the longest x5 3.18 us: couple(): padded[position:position + box_count] * flags[:, column][:, None, None]]
    dot_general x2 -> x0, local copies, waits for them, and re-layouts: 2 us -> none  [body(): jnp.einsum('bkj,bkr->bjr', matrix, expansions[tree_level].astype(jnp.bflo...]
  transfers between devices with their start and end apart: 14 -> 6, of which waited for: 1 -> 1; matrix products, arithmetic and copies ran while one was open for 48% -> 0% of each run, Pallas kernels for 0% -> 24%
where the time goes in v1:
time: 49 us; the launch traced here: 48.8 us
  Pallas kernels  26.2 us (53%)
  starting transfers between devices  18.8 us (38%)
  waiting for transfers between devices  3.75 us (8%)
    ppermute x6, starting transfers between devices, shifted(): return lax.ppermute(array, 'slab', pairs)  18.8 us
    pallas_call x1, Pallas kernels, body(): pl.pallas_call(lambda *refs: inner_kernel(plan, chunks, *refs), in_specs=...  11.6 us
    pallas_call x1, Pallas kernels, body(): pl.pallas_call(lambda *refs: upward_kernel(plan, chunks, *refs), in_specs...  7.53 us
    pallas_call x1, Pallas kernels, body(): pl.pallas_call(lambda *refs: final_kernel(plan, *refs), in_specs=[vmem] *...  7.09 us
    ppermute x6, waiting for transfers between devices, shifted(): return lax.ppermute(array, 'slab', pairs)  3.75 us
  transfers between devices with their start and end apart: 6, of which 1 were waited for; matrix products, arithmetic and copies ran while one was open for 0% of the time, Pallas kernels for 24%

profile of v1, /device:TPU:16, one launch (start us, length us, event | category | flops | bytes accessed | tf_op | source)
XLA Modules:
  0.0 48.8 jit_solution(5586226398398647169)
XLA Ops:
  0.0 0.0 copy-start
  0.0 0.0 copy-start.1
  0.0 7.5 %upward.1 = (bf16[4352,512]{1,0:T(8,128)(2,1)S(1)}, bf16[5376,512]{1,0:T(8,128)(2,1)S(1)}, bf16[784,512]{1,0:T(8,128)(2,1)S(1)}, bf16[784,512]{1,0:T(8,128)(2,1)...) custom-call(bf16[4096,512]{1,0:T(8,128)(2,1)} %refs_0_.1, ...), custom_call_target="tpu_custom_call" | custom-call | tf_op jit(solution)/shard_map/upward/pallas_call | solution.py:307
  7.5 2.8 %collective-permute-start.4 = (bf16[64,512]{1,0:T(8,128)(2,1)S(1)}, bf16[64,512]{1,0:T(8,128)(2,1)S(1)}, u32[]{:S(2)}, u32[]{:S(2)}) collective-permute-start(bf16[64,512]{1,0:T(8,128)(2,1)S(1)} %get-tuple-element.30), channel_id=1, source_target_pairs={{0,3},{1,4},{2,5},{3,6},{4,7},{5,8},{6,9},{7,10},{8,11},{9,12},{10... | collective-permute-start | bytes 196616 | tf_op jit(solution)/shard_map/ppermute | solution.py:295
  10.4 2.7 %collective-permute-start.5 = (bf16[64,512]{1,0:T(8,128)(2,1)S(1)}, bf16[64,512]{1,0:T(8,128)(2,1)S(1)}, u32[]{:S(2)}, u32[]{:S(2)}) collective-permute-start(bf16[64,512]{1,0:T(8,128)(2,1)S(1)} %get-tuple-element.30), channel_id=1, source_target_pairs={{3,0},{4,1},{5,2},{6,3},{7,4},{8,5},{9,6},{10,7},{11,8},{12,9},{13... | collective-permute-start | bytes 196616 | tf_op jit(solution)/shard_map/ppermute | solution.py:295
  13.1 2.6 %collective-permute-start = (bf16[784,512]{1,0:T(8,128)(2,1)S(1)}, bf16[784,512]{1,0:T(8,128)(2,1)S(1)}, u32[]{:S(2)}, u32[]{:S(2)}) collective-permute-start(bf16[784,512]{1,0:T(8,128)(2,1)S(1)} %get-tuple-element.26), channel_id=1, source_target_pairs={{0,1},{1,2},{2,3},{3,4},{4,5},{5,6},{6,7},{7,8},{8,9},{9,10},{10,1... | collective-permute-start | bytes 2408456 | tf_op jit(solution)/shard_map/ppermute | solution.py:295
  15.8 3.8 %collective-permute-start.1 = (bf16[784,512]{1,0:T(8,128)(2,1)S(1)}, bf16[784,512]{1,0:T(8,128)(2,1)S(1)}, u32[]{:S(2)}, u32[]{:S(2)}) collective-permute-start(bf16[784,512]{1,0:T(8,128)(2,1)S(1)} %get-tuple-element.27), channel_id=1, source_target_pairs={{1,0},{2,1},{3,2},{4,3},{5,4},{6,5},{7,6},{8,7},{9,8},{10,9},{11,1... | collective-permute-start | bytes 2408456 | tf_op jit(solution)/shard_map/ppermute | solution.py:295
  19.6 2.5 %collective-permute-start.2 = (bf16[128,512]{1,0:T(8,128)(2,1)S(1)}, bf16[128,512]{1,0:T(8,128)(2,1)S(1)}, u32[]{:S(2)}, u32[]{:S(2)}) collective-permute-start(bf16[128,512]{1,0:T(8,128)(2,1)S(1)} %get-tuple-element.28), channel_id=1, source_target_pairs={{0,2},{1,3},{2,4},{3,5},{4,6},{5,7},{6,8},{7,9},{8,10},{9,11},{10,... | collective-permute-start | bytes 393224 | tf_op jit(solution)/shard_map/ppermute | solution.py:295
  22.1 0.0 collective-permute-done.4.refs_10_
  22.1 4.2 %collective-permute-start.3 = (bf16[128,512]{1,0:T(8,128)(2,1)S(1)}, bf16[128,512]{1,0:T(8,128)(2,1)S(1)}, u32[]{:S(2)}, u32[]{:S(2)}) collective-permute-start(bf16[128,512]{1,0:T(8,128)(2,1)S(1)} %get-tuple-element.29), channel_id=1, source_target_pairs={{2,0},{3,1},{4,2},{5,3},{6,4},{7,5},{8,6},{9,7},{10,8},{11,9},{12,... | collective-permute-start | bytes 393224 | tf_op jit(solution)/shard_map/ppermute | solution.py:295
  26.4 0.0 copy-done
  26.4 0.0 copy-done.1
  26.4 11.6 %inner.1 = (f32[4096,512]{1,0:T(8,128)S(1)}, f32[3840,512]{1,0:T(8,128)S(1)}, bf16[63,64,256]{2,1,0:T(8,128)(2,1)S(1)}, bf16[2,128,128]{2,1,0:T(8,128)(2,1)S(1)}) custom-call(s32[3,32]{1,0:T(4,128)S(1)} %bitcast.2, s32[4,63]{1,0:T(4,128)S(1)} %bitcast.3, bf16[4352,512]{1,0:T(8,128)(2,1)S(1)} %get-tuple-element.18.refs_2_, ...), custom_call_target="tpu_custom_call" | custom-call | flops 12000000000 | bytes 16777216 | tf_op jit(solution)/shard_map/inner/pallas_call | solution.py:331
  38.0 0.0 collective-permute-done.5.refs_11_
  38.0 0.0 collective-permute-done.2.refs_8_
  38.0 3.7 %collective-permute-done.3.refs_9_ = bf16[128,512]{1,0:T(8,128)(2,1)S(1)} collective-permute-done((bf16[128,512]{1,0:T(8,128)(2,1)S(1)}, bf16[128,512]{1,0:T(8,128)(2,1)S(1)}, u32[]{:S(2)}, u32[]{:S(2)}) %collective-permute-start.3) | collective-permute-done | bytes 131104 | tf_op jit(solution)/shard_map/ppermute | solution.py:295
  41.7 0.0 collective-permute-done.refs_6_
  41.7 0.0 collective-permute-done.1.refs_7_
  41.7 7.1 %final.1 = bf16[4096,512]{1,0:T(8,128)(2,1)} custom-call(f32[4096,512]{1,0:T(8,128)S(1)} %get-tuple-element.20.refs_0_, f32[3840,512]{1,0:T(8,128)S(1)} %get-tuple-element.21.refs_1_, bf16[63,64,256]{2,1,0:T(8,128)(2,1)S(1)} %get-tuple-element.22.refs_2_, bf16[2,128,128]{2,1,0:T(8,128)(2,1)S(1)} %get-tuple-element.23.refs_3_, ...), custom_call_target="tpu_custom_call" | custom-call | tf_op jit(solution)/shard_map/final/pallas_call | solution.py:351
Async XLA Ops:
  0.0 26.4 %copy-start = (s32[32,3]{0,1:T(4,128)S(1)}, s32[32,3]{0,1:T(4,128)}, u32[]{:S(2)}) copy-start(s32[32,3]{0,1:T(4,128)} %param.9) | copy-start | bytes 1156
  0.0 26.4 %copy-start.1 = (s32[63,4]{0,1:T(4,128)S(1)}, s32[63,4]{0,1:T(4,128)}, u32[]{:S(2)}) copy-start(s32[63,4]{0,1:T(4,128)} %param.13) | copy-start | bytes 3028
  7.5 14.6 %collective-permute-start.4 = (bf16[64,512]{1,0:T(8,128)(2,1)S(1)}, bf16[64,512]{1,0:T(8,128)(2,1)S(1)}, u32[]{:S(2)}, u32[]{:S(2)}) collective-permute-start(bf16[64,512]{1,0:T(8,128)(2,1)S(1)} %get-tuple-element.30), channel_id=1, source_target_pairs={{0,3},{1,4},{2,5},{3,6},{4,7},{5,8},{6,9},{7,10},{8,11},{9,12},{10... | collective-permute-start | bytes 196616 | tf_op jit(solution)/shard_map/ppermute | solution.py:295
  10.4 27.6 %collective-permute-start.5 = (bf16[64,512]{1,0:T(8,128)(2,1)S(1)}, bf16[64,512]{1,0:T(8,128)(2,1)S(1)}, u32[]{:S(2)}, u32[]{:S(2)}) collective-permute-start(bf16[64,512]{1,0:T(8,128)(2,1)S(1)} %get-tuple-element.30), channel_id=1, source_target_pairs={{3,0},{4,1},{5,2},{6,3},{7,4},{8,5},{9,6},{10,7},{11,8},{12,9},{13... | collective-permute-start | bytes 196616 | tf_op jit(solution)/shard_map/ppermute | solution.py:295
  13.1 28.6 %collective-permute-start = (bf16[784,512]{1,0:T(8,128)(2,1)S(1)}, bf16[784,512]{1,0:T(8,128)(2,1)S(1)}, u32[]{:S(2)}, u32[]{:S(2)}) collective-permute-start(bf16[784,512]{1,0:T(8,128)(2,1)S(1)} %get-tuple-element.26), channel_id=1, source_target_pairs={{0,1},{1,2},{2,3},{3,4},{4,5},{5,6},{6,7},{7,8},{8,9},{9,10},{10,1... | collective-permute-start | bytes 2408456 | tf_op jit(solution)/shard_map/ppermute | solution.py:295
  15.8 26.0 %collective-permute-start.1 = (bf16[784,512]{1,0:T(8,128)(2,1)S(1)}, bf16[784,512]{1,0:T(8,128)(2,1)S(1)}, u32[]{:S(2)}, u32[]{:S(2)}) collective-permute-start(bf16[784,512]{1,0:T(8,128)(2,1)S(1)} %get-tuple-element.27), channel_id=1, source_target_pairs={{1,0},{2,1},{3,2},{4,3},{5,4},{6,5},{7,6},{8,7},{9,8},{10,9},{11,1... | collective-permute-start | bytes 2408456 | tf_op jit(solution)/shard_map/ppermute | solution.py:295
  19.6 18.4 %collective-permute-start.2 = (bf16[128,512]{1,0:T(8,128)(2,1)S(1)}, bf16[128,512]{1,0:T(8,128)(2,1)S(1)}, u32[]{:S(2)}, u32[]{:S(2)}) collective-permute-start(bf16[128,512]{1,0:T(8,128)(2,1)S(1)} %get-tuple-element.28), channel_id=1, source_target_pairs={{0,2},{1,3},{2,4},{3,5},{4,6},{5,7},{6,8},{7,9},{8,10},{9,11},{10,... | collective-permute-start | bytes 393224 | tf_op jit(solution)/shard_map/ppermute | solution.py:295
  22.1 19.6 %collective-permute-start.3 = (bf16[128,512]{1,0:T(8,128)(2,1)S(1)}, bf16[128,512]{1,0:T(8,128)(2,1)S(1)}, u32[]{:S(2)}, u32[]{:S(2)}) collective-permute-start(bf16[128,512]{1,0:T(8,128)(2,1)S(1)} %get-tuple-element.29), channel_id=1, source_target_pairs={{2,0},{3,1},{4,2},{5,3},{6,4},{7,5},{8,6},{9,7},{10,8},{11,9},{12,... | collective-permute-start | bytes 393224 | tf_op jit(solution)/shard_map/ppermute | solution.py:295

commit v2 on v1

v2 whole, which is shorter than its diff:
```python
import jax
import jax.numpy as jnp
from jax import lax
from jax.experimental import pallas as pl
from jax.experimental.pallas import tpu as pltpu
from jax.sharding import PartitionSpec as P

LEVELS = 6
FULL = LEVELS - 2
BF = jnp.bfloat16
F32 = jnp.float32
MIB = 1 << 20


def resident(shape, dtype):
    return pltpu.VMEM(shape, dtype)


def keep(array):
    return pltpu.with_memory_space_constraint(array, pltpu.VMEM)


def stay(array):
    return pltpu.with_memory_space_constraint(array, pltpu.HBM)


def dot(a, b):
    return lax.dot_general(a, b, (((1,), (0,)), ((), ())), preferred_element_type=F32)


class Plan:
    def __init__(self, leaves, panels, rank, rhs):
        self.leaves, self.panels, self.rank, self.rhs = leaves, panels, rank, rhs
        self.count = [leaves >> level for level in range(LEVELS)]
        self.first = [sum(self.count[:level]) for level in range(LEVELS)]
        self.trans = [0] + [sum(self.count[1:level]) for level in range(1, LEVELS)]
        self.padded = [sum(c + 6 for c in self.count[:level]) for level in range(FULL)]
        self.padded_boxes = sum(c + 6 for c in self.count[:FULL])
        self.inner_boxes = sum(self.count[:FULL])
        self.msg_pole = [panels + 2 * rank * level for level in range(FULL)]
        self.msg_small = panels + 2 * rank * FULL
        self.msg_rows = self.msg_small + rank
        self.part_rows = rank * panels // rhs
        self.top_rows = 2 * rank + self.part_rows


def upward_kernel(plan, chunks, charges, basis, transfers, padded_x, poles, up, down, top, bs, ts, sems):
    p, r = plan.panels, plan.rank
    per = plan.leaves // chunks
    copies = []
    for c in range(chunks):
        rows = per * p
        copies.append(
            pltpu.make_async_copy(
                charges.at[pl.ds(c * rows, rows)], padded_x.at[pl.ds(p + c * rows, rows)], sems.at[c]
            )
        )
    basis_copy = pltpu.make_async_copy(basis, bs, sems.at[chunks])
    trans_copy = pltpu.make_async_copy(transfers, ts, sems.at[chunks + 1])
    basis_copy.start()
    copies[0].start()
    trans_copy.start()
    for copy in copies[1:]:
        copy.start()
    padded_x[pl.ds(0, p)] = jnp.zeros((p, plan.rhs), BF)
    padded_x[pl.ds(p * (plan.leaves + 1), p)] = jnp.zeros((p, plan.rhs), BF)
    for level in range(FULL):
        start = plan.padded[level] * r
        poles[pl.ds(start, 3 * r)] = jnp.zeros((3 * r, plan.rhs), BF)
        poles[pl.ds(start + (plan.count[level] + 3) * r, 3 * r)] = jnp.zeros((3 * r, plan.rhs), BF)
    basis_copy.wait()

    def keep(level, box, value):
        n = plan.count[level]
        if level < FULL:
            poles[pl.ds((plan.padded[level] + 3 + box) * r, r)] = value
            if n - 3 <= box <= n - 2:
                up[pl.ds(plan.msg_pole[level] + (box - n + 3) * r, r)] = value
            if 1 <= box <= 2:
                down[pl.ds(plan.msg_pole[level] + (box - 1) * r, r)] = value
        else:
            top[pl.ds(box * r, r)] = value

    def climb(level, box):
        pair = poles[pl.ds((plan.padded[level - 1] + 3 + 2 * box) * r, 2 * r)]
        keep(level, box, dot(ts[plan.trans[level] + box], pair).astype(BF))

    done = [0] * (FULL + 1)

    def climb_ready():
        ready = list(done)
        for level in range(1, FULL + 1):
            while 2 * done[level] + 2 <= ready[level - 1]:
                climb(level, done[level])
                done[level] += 1

    for c in range(chunks):
        copies[c].wait()
        if c == 0:
            trans_copy.wait()
        climb_ready()
        for leaf in range(c * per, (c + 1) * per):
            x = padded_x[pl.ds(p * (leaf + 1), p)]
            keep(0, leaf, dot(bs[leaf], x).astype(BF))
        done[0] = (c + 1) * per
    while done[FULL] < plan.count[FULL]:
        climb_ready()
    for message, leaf, last in ((up, plan.leaves - 1, True), (down, 0, False)):
        message[pl.ds(0, p)] = padded_x[pl.ds(p * (leaf + 1), p)]
        message[pl.ds(plan.msg_small, r), pl.ds(0, p)] = bs[leaf]
        for level in range(1, FULL):
            box = plan.count[level] - 1 if last else 0
            message[pl.ds(plan.msg_small, r), pl.ds(level * p, p)] = ts[plan.trans[level] + box]
    rows = plan.part_rows
    for part in range(plan.rhs // p):
        top[pl.ds(2 * r, rows), pl.ds(part * p, p)] = ts[plan.trans[LEVELS - 1], pl.ds(part * rows, rows)]


def inner_kernel(
    plan, chunks, pattern, flags, padded_x, poles, bs, ts, near_blocks, couplings,
    near, local, masked, edge_near, bs_t, ts_t, nb, sems,
):
    p, r = plan.panels, plan.rank
    per = plan.leaves // chunks
    half = couplings.shape[0] // 2
    coupling_copies = [
        pltpu.make_async_copy(couplings.at[pl.ds(a, n)], masked.at[pl.ds(a, n)], sems.at[chunks + k])
        for k, (a, n) in enumerate(((0, half), (half, couplings.shape[0] - half)))
    ]
    copies = [
        pltpu.make_async_copy(near_blocks.at[pl.ds(c * per, per)], nb.at[pl.ds(c * per, per)], sems.at[c])
        for c in range(chunks)
    ]
    for copy in coupling_copies + copies:
        copy.start()
    for box in range(ts.shape[0]):
        ts_t[box] = ts[box].T
    for leaf in range(bs.shape[0]):
        bs_t[leaf] = bs[leaf].T
    lane = lax.broadcasted_iota(jnp.int32, (r, 4 * r), 1)

    def mask(box):
        low = jnp.where(lane < r, flags[0, box], flags[1, box])
        high = jnp.where(lane < 3 * r, flags[2, box], flags[3, box])
        chosen = jnp.where(lane < 2 * r, low, high)
        value = masked[box] * chosen.astype(F32).astype(BF)
        masked[box] = value
        return value

    def couple(level, box):
        row = (plan.padded[level] + box) * r
        stack = jnp.concatenate([poles[pl.ds(row, 2 * r)], poles[pl.ds(row + 5 * r, 2 * r)]], axis=0)
        index = plan.first[level] + box
        local[pl.ds(index * r, r)] = dot(mask(index), stack)

    for copy in coupling_copies:
        copy.wait()
    for level in range(FULL):
        for box in range(plan.count[level]):
            couple(level, box)
    for box in range(plan.inner_boxes, sum(plan.count)):
        mask(box)

    def side(leaf, slot):
        block = nb[leaf, slot]
        return jnp.where(pattern[slot, leaf] != 0, block, jnp.zeros_like(block))

    def near_one(leaf):
        wide = jnp.concatenate([side(leaf, 0), nb[leaf, 1], side(leaf, 2)], axis=1)
        near[pl.ds(leaf * p, p)] = dot(wide, padded_x[pl.ds(leaf * p, 3 * p)]).astype(BF)

    for c in range(chunks):
        copies[c].wait()
    for leaf in range(plan.leaves):
        near_one(leaf)
    edge_near[0] = side(0, 0)
    edge_near[1] = side(plan.leaves - 1, 2)


def top_kernel(plan, peers, gathered, local, masked, ts, ts_t, third, held, sems):
    r, p = plan.rank, plan.panels
    me = lax.axis_index("slab")
    copies = {}
    for k, by in enumerate((-3, -2, -1, 1, 2, 3)):
        source = jnp.clip(me + by, 0, peers - 1)
        copies[by] = pltpu.make_async_copy(gathered.at[source], held.at[k], sems.at[k])
        copies[by].start()
    pair, fifth = {}, {}
    for k, by in enumerate((-3, -2, -1, 1, 2, 3)):
        copies[by].wait()
        inside = (me + by >= 0) if by < 0 else (me + by < peers)
        value = held[k, pl.ds(0, 2 * r)]
        pair[by] = jnp.where(inside, value, jnp.zeros_like(value))
        if abs(by) > 1:
            rows = plan.part_rows
            matrix = jnp.concatenate(
                [held[k, pl.ds(2 * r, rows), pl.ds(part * p, p)] for part in range(plan.rhs // p)], axis=0
            )
            fifth[by] = dot(matrix, pair[by]).astype(BF)
    box = plan.first[LEVELS - 1]
    stack = jnp.concatenate([fifth[-3], fifth[-2], fifth[2], fifth[3]], axis=0)
    summit = dot(masked[box], stack).astype(BF)
    pushed = dot(ts_t[plan.trans[LEVELS - 1]], summit)
    stacks = (
        [pair[-2][r:], pair[-1][:r], pair[1]],
        [pair[-1], pair[1][r:], pair[2][:r]],
    )
    for k, stack in enumerate(stacks):
        gained = dot(masked[plan.first[FULL] + k], jnp.concatenate(stack, axis=0))
        value = (gained + pushed[k * r : (k + 1) * r]).astype(BF)
        index = (plan.first[FULL - 1] + 2 * k) * r
        third[pl.ds(2 * k * r, 2 * r)] = local[pl.ds(index, 2 * r)] + dot(ts_t[plan.trans[FULL] + k], value)


def final_kernel(plan, near, local, third, masked, edge_near, bs_t, ts_t, below, above, out, stage, sems):
    p, r, n = plan.panels, plan.rank, plan.leaves

    def edges(message, last):
        x = message[pl.ds(0, p)]
        small = pl.ds(plan.msg_small, r)
        rim = [dot(message[small, pl.ds(0, p)], x).astype(BF)]
        sent = [message[pl.ds(plan.msg_pole[level], 2 * r)] for level in range(FULL)]
        for level in range(1, FULL):
            if last:
                pair = jnp.concatenate([sent[level - 1][r:], rim[-1]], axis=0)
            else:
                pair = jnp.concatenate([rim[-1], sent[level - 1][:r]], axis=0)
            rim.append(dot(message[small, pl.ds(level * p, p)], pair).astype(BF))
        return x, rim, sent

    x_low, rim_low, sent_low = edges(below, True)
    x_high, rim_high, sent_high = edges(above, False)

    rims = []
    for level in range(FULL):
        first, m = plan.first[level], plan.count[level]
        low = jnp.concatenate([sent_low[level], rim_low[level]], axis=0)
        high = jnp.concatenate([rim_high[level], sent_high[level]], axis=0)
        gain = [
            (0, dot(masked[first, :, pl.ds(0, 2 * r)], low[: 2 * r])),
            (1, dot(masked[first + 1, :, pl.ds(0, 2 * r)], low[r:])),
            (2, dot(masked[first + 2, :, pl.ds(0, r)], low[2 * r :])),
            (m - 1, dot(masked[first + m - 1, :, pl.ds(2 * r, 2 * r)], high[r:])),
            (m - 2, dot(masked[first + m - 2, :, pl.ds(2 * r, 2 * r)], high[: 2 * r])),
            (m - 3, dot(masked[first + m - 3, :, pl.ds(3 * r, r)], high[:r])),
        ]
        sums = {}
        for place, value in gain:
            sums[place] = sums[place] + value if place in sums else value
        rims.append(sums)

    def settled(level, box, value):
        if box in rims[level]:
            value = value + rims[level][box]
        return value.astype(BF)

    current = [settled(FULL - 1, box, third[pl.ds(box * r, r)]) for box in range(plan.count[FULL - 1])]
    for level in range(FULL - 1, 1, -1):
        lower = []
        for box, value in enumerate(current):
            push = dot(ts_t[plan.trans[level] + box], value)
            for k in range(2):
                index = (plan.first[level - 1] + 2 * box + k) * r
                lower.append(settled(level - 1, 2 * box + k, local[pl.ds(index, r)] + push[k * r : (k + 1) * r]))
        current = lower

    writes = []
    for box, value in enumerate(current):
        push = dot(ts_t[plan.trans[1] + box], value)
        for k in range(2):
            leaf = 2 * box + k
            leaf_local = settled(0, leaf, local[pl.ds(leaf * r, r)] + push[k * r : (k + 1) * r])
            total = near[pl.ds(leaf * p, p)].astype(F32) + dot(bs_t[leaf], leaf_local)
            if leaf == 0:
                total = total + dot(edge_near[0], x_low)
            if leaf == n - 1:
                total = total + dot(edge_near[1], x_high)
            stage[pl.ds(leaf * p, p)] = total.astype(BF)
        if box % 2:
            rows = pl.ds((box - 1) * 2 * p, 4 * p)
            copy = pltpu.make_async_copy(stage.at[rows], out.at[rows], sems.at[box // 2])
            copy.start()
            writes.append(copy)
    for copy in writes:
        copy.wait()


def shifted(array, by):
    peers = lax.axis_size("slab")
    pairs = [(i, i + by) for i in range(peers) if 0 <= i + by < peers]
    return lax.ppermute(array, "slab", pairs)


def body(charges, near_blocks, near_pattern, leaf_basis, transfers, couplings, interactions):
    leaves, panels, rank, rhs = near_blocks.shape[0], near_blocks.shape[2], leaf_basis.shape[1], charges.shape[1]
    plan = Plan(leaves, panels, rank, rhs)
    hbm = pl.BlockSpec(memory_space=pltpu.HBM)
    vmem = pl.BlockSpec(memory_space=pltpu.VMEM)
    smem = pl.BlockSpec(memory_space=pltpu.SMEM)
    chunks = 8

    padded_x, poles, up, down, top, bs, ts = pl.pallas_call(
        lambda *refs: upward_kernel(plan, chunks, *refs),
        in_specs=[hbm, hbm, hbm],
        out_specs=[vmem] * 7,
        out_shape=[
            resident(((leaves + 2) * panels, rhs), BF),
            resident((plan.padded_boxes * rank, rhs), BF),
            resident((plan.msg_rows, rhs), BF),
            resident((plan.msg_rows, rhs), BF),
            resident((plan.top_rows, rhs), BF),
            resident(leaf_basis.shape, BF),
            resident(transfers.shape, BF),
        ],
        scratch_shapes=[pltpu.SemaphoreType.DMA((chunks + 2,))],
        compiler_params=pltpu.CompilerParams(vmem_limit_bytes=6 * MIB),
        name="upward",
    )(stay(charges), stay(leaf_basis), stay(transfers))

    gathered = lax.all_gather(top, "slab")
    below, above = shifted(up, 1), shifted(down, -1)

    near, local, masked, edge_near, bs_t, ts_t = pl.pallas_call(
        lambda *refs: inner_kernel(plan, 4, *refs),
        in_specs=[smem, smem, vmem, vmem, vmem, vmem, hbm, hbm],
        out_specs=[vmem] * 6,
        out_shape=[
            resident((leaves * panels, rhs), BF),
            resident((plan.inner_boxes * rank, rhs), F32),
            resident(couplings.shape, BF),
            resident((2, panels, panels), BF),
            resident((leaves, panels, rank), BF),
            resident((transfers.shape[0], panels, rank), BF),
        ],
        scratch_shapes=[
            pltpu.VMEM(near_blocks.shape, BF),
            pltpu.SemaphoreType.DMA((6,)),
        ],
        compiler_params=pltpu.CompilerParams(vmem_limit_bytes=12 * MIB),
        cost_estimate=pl.CostEstimate(flops=12_000_000_000, bytes_accessed=16 * MIB, transcendentals=0),
        name="inner",
    )(
        near_pattern.T, interactions.T, keep(padded_x), keep(poles), keep(bs), keep(ts),
        stay(near_blocks), stay(couplings),
    )

    third = pl.pallas_call(
        lambda *refs: top_kernel(plan, gathered.shape[0], *refs),
        in_specs=[hbm, vmem, vmem, vmem, vmem],
        out_specs=vmem,
        out_shape=resident((plan.count[FULL - 1] * rank, rhs), F32),
        scratch_shapes=[
            pltpu.VMEM((6, plan.top_rows, rhs), BF),
            pltpu.SemaphoreType.DMA((6,)),
        ],
        compiler_params=pltpu.CompilerParams(vmem_limit_bytes=6 * MIB),
        name="top",
    )(stay(gathered), keep(local), keep(masked), keep(ts), keep(ts_t))

    return pl.pallas_call(
        lambda *refs: final_kernel(plan, *refs),
        in_specs=[vmem] * 9,
        out_specs=hbm,
        out_shape=jax.ShapeDtypeStruct((leaves * panels, rhs), BF),
        scratch_shapes=[
            pltpu.VMEM((leaves * panels, rhs), BF),
            pltpu.SemaphoreType.DMA((leaves // 4,)),
        ],
        compiler_params=pltpu.CompilerParams(vmem_limit_bytes=12 * MIB),
        name="final",
    )(
        keep(near), keep(local), keep(third), keep(masked), keep(edge_near), keep(bs_t), keep(ts_t),
        keep(below), keep(above),
    )


def solution(mesh):
    spec = ("groups", "slab")
    in_specs = (
        P(spec, None),
        P(spec, None, None, None),
        P(spec, None),
        P(spec, None, None),
        P(spec, None, None),
        P(spec, None, None),
        P(spec, None),
    )
    return jax.shard_map(body, mesh=mesh, in_specs=in_specs, out_specs=P(spec, None), check_vma=False)
```

time: 49 us -> 91.8 us (1.87)
  the two profiles are of different devices: /device:TPU:16 before, /device:TPU:0 now
where the time goes in v2:
time: 91.8 us; the launch traced here: 91.4 us
  local copies, waits for them, and re-layouts  26 us (28%)
  waiting for transfers between devices  24.4 us (27%)
  Pallas kernels  23.1 us (25%)
  between operations  13.5 us (15%)
  starting transfers between devices  4.48 us (5%)
    unnamed x36, local copies, waits for them, and re-layouts  26 us
    all_gather x1, waiting for transfers between devices, body(): gathered = lax.all_gather(top, 'slab')  24.3 us
    pallas_call x1, Pallas kernels, body(): pl.pallas_call(lambda *refs: final_kernel(plan, *refs), in_specs=[vmem] *...  7.73 us
    pallas_call x1, Pallas kernels, body(): pl.pallas_call(lambda *refs: inner_kernel(plan, 4, *refs), in_specs=[smem...  7.66 us
    pallas_call x1, Pallas kernels, body(): pl.pallas_call(lambda *refs: upward_kernel(plan, chunks, *refs), in_specs...  5.28 us
    ppermute x2, starting transfers between devices, shifted(): return lax.ppermute(array, 'slab', pairs)  4.48 us
    pallas_call x1, Pallas kernels, body(): pl.pallas_call(lambda *refs: top_kernel(plan, gathered.shape[0], *refs),...  2.41 us
  transfers between devices with their start and end apart: 3, of which 1 were waited for; matrix products, arithmetic and copies ran while one was open for 0% of the time, Pallas kernels for 11%

profile of v2, /device:TPU:0, one launch (start us, length us, event | category | flops | bytes accessed | tf_op | source)
XLA Modules:
  0.0 91.4 jit_solution(15785187332278506852)
XLA Ops:
  6.5 0.0 copy-start.16
  6.5 0.0 copy-start.17
  6.5 0.0 all-gather.3.cloned.1.call-start
  6.5 5.3 %upward.1 = (bf16[4352,512]{1,0:T(8,128)(2,1)S(1)}, bf16[5376,512]{1,0:T(8,128)(2,1)S(1)}, bf16[704,512]{1,0:T(8,128)(2,1)}, bf16[704,512]{1,0:T(8,128)(2,1)}, b...) custom-call(bf16[4096,512]{1,0:T(8,128)(2,1)} %refs_0_.1, ...), custom_call_target="tpu_custom_call" | custom-call | tf_op jit(solution)/shard_map/upward/pallas_call | solution.py:302
  11.8 0.0 copy-start.7
  11.8 0.8 copy-done.7
  12.6 0.0 copy-start.10
  12.6 2.4 %copy-done.10 = bf16[5376,512]{1,0:T(8,128)(2,1)} copy-done((bf16[5376,512]{1,0:T(8,128)(2,1)}, bf16[5376,512]{1,0:T(8,128)(2,1)S(1)}, u32[]{:S(2)}) %copy-start.10) | copy-done | bytes 5505048
  15.0 0.0 copy-start.12
  15.0 2.1 %copy-done.12 = bf16[4352,512]{1,0:T(8,128)(2,1)} copy-done((bf16[4352,512]{1,0:T(8,128)(2,1)}, bf16[4352,512]{1,0:T(8,128)(2,1)S(1)}, u32[]{:S(2)}) %copy-start.12) | copy-done | bytes 4456472
  17.1 0.0 copy-start.14
  17.1 0.8 copy-done.14
  17.9 0.0 all-gather.3.cloned.1.call-update
  17.9 3.2 %collective-permute-start = (bf16[704,512]{1,0:T(8,128)(2,1)}, bf16[704,512]{1,0:T(8,128)(2,1)}, u32[]{:S(2)}, u32[]{:S(2)}) collective-permute-start(bf16[704,512]{1,0:T(8,128)(2,1)} %get-tuple-element.29), channel_id=1, source_target_pairs={{0,1},{1,2},{2,3},{3,4},{4,5},{5,6},{6,7},{7,8},{8,9},{9,10},{10,1... | collective-permute-start | bytes 2162696 | tf_op jit(solution)/shard_map/ppermute | solution.py:291
  21.1 1.3 %collective-permute-start.1 = (bf16[704,512]{1,0:T(8,128)(2,1)}, bf16[704,512]{1,0:T(8,128)(2,1)}, u32[]{:S(2)}, u32[]{:S(2)}) collective-permute-start(bf16[704,512]{1,0:T(8,128)(2,1)} %get-tuple-element.30), channel_id=1, source_target_pairs={{1,0},{2,1},{3,2},{4,3},{5,4},{6,5},{7,6},{8,7},{9,8},{10,9},{11,1... | collective-permute-start | bytes 2162696 | tf_op jit(solution)/shard_map/ppermute | solution.py:291
  22.4 0.0 copy-done.16
  22.4 0.0 copy-done.17
  22.5 0.0 copy-start.8
  22.5 1.0 %copy-done.8 = bf16[31,64,128]{2,1,0:T(8,128)(2,1)S(1)} copy-done((bf16[31,64,128]{2,1,0:T(8,128)(2,1)S(1)}, bf16[31,64,128]{2,1,0:T(8,128)(2,1)}, u32[]{:S(2)}) %copy-start.8) | copy-done | bytes 507928
  23.5 0.0 copy-start.11
  23.5 2.6 %copy-done.11 = bf16[5376,512]{1,0:T(8,128)(2,1)S(1)} copy-done((bf16[5376,512]{1,0:T(8,128)(2,1)S(1)}, bf16[5376,512]{1,0:T(8,128)(2,1)}, u32[]{:S(2)}) %copy-start.11) | copy-done | bytes 5505048
  26.1 0.0 copy-start.13
  26.1 2.3 %copy-done.13 = bf16[4352,512]{1,0:T(8,128)(2,1)S(1)} copy-done((bf16[4352,512]{1,0:T(8,128)(2,1)S(1)}, bf16[4352,512]{1,0:T(8,128)(2,1)}, u32[]{:S(2)}) %copy-start.13) | copy-done | bytes 4456472
  28.4 0.0 copy-start.15
  28.4 1.0 %copy-done.15 = bf16[32,64,128]{2,1,0:T(8,128)(2,1)S(1)} copy-done((bf16[32,64,128]{2,1,0:T(8,128)(2,1)S(1)}, bf16[32,64,128]{2,1,0:T(8,128)(2,1)}, u32[]{:S(2)}) %copy-start.15) | copy-done | bytes 524312
  29.4 7.7 %inner.1 = (bf16[4096,512]{1,0:T(8,128)(2,1)S(1)}, f32[3840,512]{1,0:T(8,128)S(1)}, bf16[63,64,256]{2,1,0:T(8,128)(2,1)S(1)}, bf16[2,128,128]{2,1,0:T(8,128)(2,1...) custom-call(s32[3,32]{1,0:T(4,128)S(1)} %bitcast.3, s32[4,63]{1,0:T(4,128)S(1)} %bitcast.4, ...), custom_call_target="tpu_custom_call" | custom-call | flops 12000000000 | bytes 16777216 | tf_op jit(solution)/shard_map/inner/pallas_call | solution.py:323
  37.1 0.0 copy-start
  37.1 3.0 %copy-done = f32[3840,512]{1,0:T(8,128)} copy-done((f32[3840,512]{1,0:T(8,128)}, f32[3840,512]{1,0:T(8,128)S(1)}, u32[]{:S(2)}) %copy-start) | copy-done | bytes 7864344
  40.1 0.0 copy-start.3
  40.1 2.0 %copy-done.3 = bf16[4096,512]{1,0:T(8,128)(2,1)} copy-done((bf16[4096,512]{1,0:T(8,128)(2,1)}, bf16[4096,512]{1,0:T(8,128)(2,1)S(1)}, u32[]{:S(2)}) %copy-start.3) | copy-done | bytes 4194328
  42.1 0.0 copy-start.5
  42.1 1.1 %copy-done.5 = bf16[32,128,64]{2,1,0:T(8,128)(2,1)} copy-done((bf16[32,128,64]{2,1,0:T(8,128)(2,1)}, bf16[32,128,64]{2,1,0:T(8,128)(2,1)S(1)}, u32[]{:S(2)}) %copy-start.5) | copy-done | bytes 524312
  43.2 24.3 %all-gather.3.cloned.1.call-done = bf16[2304,512]{1,0:T(8,128)(2,1)} async-done(((bf16[144,512]{1,0:T(8,128)(2,1)}), bf16[2304,512]{1,0:T(8,128)(2,1)}) %all-gather.3.cloned.1.call-update) | async-done | bytes 2359312 | tf_op jit(solution)/shard_map/all_gather | solution.py:320
  67.5 0.0 copy-start.1
  67.5 3.2 %copy-done.1 = f32[3840,512]{1,0:T(8,128)S(1)} copy-done((f32[3840,512]{1,0:T(8,128)S(1)}, f32[3840,512]{1,0:T(8,128)}, u32[]{:S(2)}) %copy-start.1) | copy-done | bytes 7864344
  70.8 0.0 copy-start.9
  70.8 1.0 %copy-done.9 = bf16[31,64,128]{2,1,0:T(8,128)(2,1)S(1)} copy-done((bf16[31,64,128]{2,1,0:T(8,128)(2,1)S(1)}, bf16[31,64,128]{2,1,0:T(8,128)(2,1)}, u32[]{:S(2)}) %copy-start.9) | copy-done | bytes 507928
  71.8 0.0 copy-start.2
  71.8 0.0 copy-start.4
  71.8 0.0 copy-start.6
  71.8 2.4 %top.1.refs_2_ = f32[256,512]{1,0:T(8,128)S(1)} custom-call(bf16[16,144,512]{2,1,0:T(8,128)(2,1)} %bitcast.5, f32[3840,512]{1,0:T(8,128)S(1)} %copy-done.1, bf16[63,64,256]{2,1,0:T(8,128)(2,1)S(1)} %get-tuple-element.25.refs_2_.refs_3_, bf16[31,64,128]{2,1,0:T(8,128)(2,1)S(1)} %copy-done.9, bf16[31,128,64]{2,1,0:T(8,128)(2,1)S(1)} %get-tuple-element.26.refs_4_.refs_6_), custom_call_target="tpu_custom_call" | custom-call | tf_op jit(solution)/shard_map/top/pallas_call | solution.py:347
  74.2 0.0 collective-permute-done.refs_7_
  74.2 0.0 collective-permute-done.1.refs_8_
  74.2 1.2 %copy-done.2 = f32[3840,512]{1,0:T(8,128)S(1)} copy-done((f32[3840,512]{1,0:T(8,128)S(1)}, f32[3840,512]{1,0:T(8,128)}, u32[]{:S(2)}) %copy-start.2) | copy-done | bytes 7864344
  75.4 1.2 %copy-done.4 = bf16[4096,512]{1,0:T(8,128)(2,1)S(1)} copy-done((bf16[4096,512]{1,0:T(8,128)(2,1)S(1)}, bf16[4096,512]{1,0:T(8,128)(2,1)}, u32[]{:S(2)}) %copy-start.4) | copy-done | bytes 4194328
  76.6 0.2 copy-done.6
  76.8 7.7 %final.1 = bf16[4096,512]{1,0:T(8,128)(2,1)} custom-call(bf16[4096,512]{1,0:T(8,128)(2,1)S(1)} %copy-done.4, f32[3840,512]{1,0:T(8,128)S(1)} %copy-done.2, f32[256,512]{1,0:T(8,128)S(1)} %top.1.refs_2_, bf16[63,64,256]{2,1,0:T(8,128)(2,1)S(1)} %get-tuple-element.25.refs_2_.refs_3_, bf16[2,128,128]{2,1,0:T(8,128)(2,1)S(1)} %get-tuple-element.27.refs_4_, ...), custom_call_target="tpu_custom_call" | custom-call | tf_op jit(solution)/shard_map/final/pallas_call | solution.py:360
Async XLA Ops:
  6.5 15.9 %copy-start.16 = (s32[32,3]{0,1:T(4,128)S(1)}, s32[32,3]{0,1:T(4,128)}, u32[]{:S(2)}) copy-start(s32[32,3]{0,1:T(4,128)} %param.9) | copy-start | bytes 1156
  6.5 15.9 %copy-start.17 = (s32[63,4]{0,1:T(4,128)S(1)}, s32[63,4]{0,1:T(4,128)}, u32[]{:S(2)}) copy-start(s32[63,4]{0,1:T(4,128)} %param.13) | copy-start | bytes 3028
  6.5 61.0 %all-gather.3.cloned.1.call-start = ((), (), s32[]{:S(2)}) async-start(), calls=%async_computation | async-start | bytes 2506752 | tf_op jit(solution)/shard_map/all_gather | solution.py:320
  11.8 0.8 copy-start.7
  12.6 2.4 %copy-start.10 = (bf16[5376,512]{1,0:T(8,128)(2,1)}, bf16[5376,512]{1,0:T(8,128)(2,1)S(1)}, u32[]{:S(2)}) copy-start(bf16[5376,512]{1,0:T(8,128)(2,1)S(1)} %get-tuple-element.19.refs_3_) | copy-start | bytes 16515076
  15.0 2.1 %copy-start.12 = (bf16[4352,512]{1,0:T(8,128)(2,1)}, bf16[4352,512]{1,0:T(8,128)(2,1)S(1)}, u32[]{:S(2)}) copy-start(bf16[4352,512]{1,0:T(8,128)(2,1)S(1)} %get-tuple-element.18.refs_2_) | copy-start | bytes 13369348
  17.1 0.8 copy-start.14
  17.9 56.3 %collective-permute-start = (bf16[704,512]{1,0:T(8,128)(2,1)}, bf16[704,512]{1,0:T(8,128)(2,1)}, u32[]{:S(2)}, u32[]{:S(2)}) collective-permute-start(bf16[704,512]{1,0:T(8,128)(2,1)} %get-tuple-element.29), channel_id=1, source_target_pairs={{0,1},{1,2},{2,3},{3,4},{4,5},{5,6},{6,7},{7,8},{8,9},{9,10},{10,1... | collective-permute-start | bytes 2162696 | tf_op jit(solution)/shard_map/ppermute | solution.py:291
  21.1 53.1 %collective-permute-start.1 = (bf16[704,512]{1,0:T(8,128)(2,1)}, bf16[704,512]{1,0:T(8,128)(2,1)}, u32[]{:S(2)}, u32[]{:S(2)}) collective-permute-start(bf16[704,512]{1,0:T(8,128)(2,1)} %get-tuple-element.30), channel_id=1, source_target_pairs={{1,0},{2,1},{3,2},{4,3},{5,4},{6,5},{7,6},{8,7},{9,8},{10,9},{11,1... | collective-permute-start | bytes 2162696 | tf_op jit(solution)/shard_map/ppermute | solution.py:291
  22.5 1.0 %copy-start.8 = (bf16[31,64,128]{2,1,0:T(8,128)(2,1)S(1)}, bf16[31,64,128]{2,1,0:T(8,128)(2,1)}, u32[]{:S(2)}) copy-start(bf16[31,64,128]{2,1,0:T(8,128)(2,1)} %copy-done.7) | copy-start | bytes 1523716
  23.5 2.6 %copy-start.11 = (bf16[5376,512]{1,0:T(8,128)(2,1)S(1)}, bf16[5376,512]{1,0:T(8,128)(2,1)}, u32[]{:S(2)}) copy-start(bf16[5376,512]{1,0:T(8,128)(2,1)} %copy-done.10) | copy-start | bytes 16515076
  26.1 2.3 %copy-start.13 = (bf16[4352,512]{1,0:T(8,128)(2,1)S(1)}, bf16[4352,512]{1,0:T(8,128)(2,1)}, u32[]{:S(2)}) copy-start(bf16[4352,512]{1,0:T(8,128)(2,1)} %copy-done.12) | copy-start | bytes 13369348
  28.4 1.0 %copy-start.15 = (bf16[32,64,128]{2,1,0:T(8,128)(2,1)S(1)}, bf16[32,64,128]{2,1,0:T(8,128)(2,1)}, u32[]{:S(2)}) copy-start(bf16[32,64,128]{2,1,0:T(8,128)(2,1)} %copy-done.14) | copy-start | bytes 1572868
  37.1 3.0 %copy-start = (f32[3840,512]{1,0:T(8,128)}, f32[3840,512]{1,0:T(8,128)S(1)}, u32[]{:S(2)}) copy-start(f32[3840,512]{1,0:T(8,128)S(1)} %get-tuple-element.23.refs_1_) | copy-start | bytes 23592964
  40.1 2.0 %copy-start.3 = (bf16[4096,512]{1,0:T(8,128)(2,1)}, bf16[4096,512]{1,0:T(8,128)(2,1)S(1)}, u32[]{:S(2)}) copy-start(bf16[4096,512]{1,0:T(8,128)(2,1)S(1)} %get-tuple-element.22.refs_0_) | copy-start | bytes 12582916
  42.1 1.1 %copy-start.5 = (bf16[32,128,64]{2,1,0:T(8,128)(2,1)}, bf16[32,128,64]{2,1,0:T(8,128)(2,1)S(1)}, u32[]{:S(2)}) copy-start(bf16[32,128,64]{2,1,0:T(8,128)(2,1)S(1)} %get-tuple-element.28.refs_5_) | copy-start | bytes 1572868
  67.5 3.2 %copy-start.1 = (f32[3840,512]{1,0:T(8,128)S(1)}, f32[3840,512]{1,0:T(8,128)}, u32[]{:S(2)}) copy-start(f32[3840,512]{1,0:T(8,128)} %copy-done) | copy-start | bytes 23592964
  70.8 1.0 %copy-start.9 = (bf16[31,64,128]{2,1,0:T(8,128)(2,1)S(1)}, bf16[31,64,128]{2,1,0:T(8,128)(2,1)}, u32[]{:S(2)}) copy-start(bf16[31,64,128]{2,1,0:T(8,128)(2,1)} %copy-done.7) | copy-start | bytes 1523716
  71.8 3.6 %copy-start.2 = (f32[3840,512]{1,0:T(8,128)S(1)}, f32[3840,512]{1,0:T(8,128)}, u32[]{:S(2)}) copy-start(f32[3840,512]{1,0:T(8,128)} %copy-done) | copy-start | bytes 23592964
  71.8 4.8 %copy-start.4 = (bf16[4096,512]{1,0:T(8,128)(2,1)S(1)}, bf16[4096,512]{1,0:T(8,128)(2,1)}, u32[]{:S(2)}) copy-start(bf16[4096,512]{1,0:T(8,128)(2,1)} %copy-done.3) | copy-start | bytes 12582916
  71.8 5.0 %copy-start.6 = (bf16[32,128,64]{2,1,0:T(8,128)(2,1)S(1)}, bf16[32,128,64]{2,1,0:T(8,128)(2,1)}, u32[]{:S(2)}) copy-start(bf16[32,128,64]{2,1,0:T(8,128)(2,1)} %copy-done.5) | copy-start | bytes 1572868
Sparse Core Ops, SparseCore 0:
  18.1 49.4 all-gather.2

commit v3 on v2

v3 whole, which is shorter than its diff:
```python
import jax
import jax.numpy as jnp
from jax import lax
from jax.experimental import pallas as pl
from jax.experimental.pallas import tpu as pltpu
from jax.sharding import PartitionSpec as P

LEVELS = 6
FULL = LEVELS - 2
BF = jnp.bfloat16
F32 = jnp.float32
MIB = 1 << 20


def resident(shape, dtype):
    return pltpu.VMEM(shape, dtype)


def keep(array):
    return pltpu.with_memory_space_constraint(array, pltpu.VMEM)


def stay(array):
    return pltpu.with_memory_space_constraint(array, pltpu.HBM)


def dot(a, b):
    return lax.dot_general(a, b, (((1,), (0,)), ((), ())), preferred_element_type=F32)


class Plan:
    def __init__(self, leaves, panels, rank, rhs):
        self.leaves, self.panels, self.rank, self.rhs = leaves, panels, rank, rhs
        self.count = [leaves >> level for level in range(LEVELS)]
        self.first = [sum(self.count[:level]) for level in range(LEVELS)]
        self.trans = [0] + [sum(self.count[1:level]) for level in range(1, LEVELS)]
        self.padded = [sum(c + 6 for c in self.count[:level]) for level in range(FULL)]
        self.padded_boxes = sum(c + 6 for c in self.count[:FULL])
        self.inner_boxes = sum(self.count[:FULL])
        self.msg_pole = [panels + 2 * rank * level for level in range(FULL)]
        self.msg_top = panels + 2 * rank * FULL
        self.msg_small = self.msg_top + rank
        self.msg_last = self.msg_small + rank
        self.part_rows = rank * panels // rhs
        self.msg_rows = self.msg_last + self.part_rows


def upward_kernel(plan, chunks, charges, basis, transfers, padded_x, poles, up, down, up2, down2, top, bs, ts, pair4, sems):
    p, r = plan.panels, plan.rank
    per = plan.leaves // chunks
    copies = []
    for c in range(chunks):
        rows = per * p
        copies.append(
            pltpu.make_async_copy(
                charges.at[pl.ds(c * rows, rows)], padded_x.at[pl.ds(p + c * rows, rows)], sems.at[c]
            )
        )
    basis_copy = pltpu.make_async_copy(basis, bs, sems.at[chunks])
    trans_copy = pltpu.make_async_copy(transfers, ts, sems.at[chunks + 1])
    basis_copy.start()
    copies[0].start()
    trans_copy.start()
    for copy in copies[1:]:
        copy.start()
    padded_x[pl.ds(0, p)] = jnp.zeros((p, plan.rhs), BF)
    padded_x[pl.ds(p * (plan.leaves + 1), p)] = jnp.zeros((p, plan.rhs), BF)
    for level in range(FULL):
        start = plan.padded[level] * r
        poles[pl.ds(start, 3 * r)] = jnp.zeros((3 * r, plan.rhs), BF)
        poles[pl.ds(start + (plan.count[level] + 3) * r, 3 * r)] = jnp.zeros((3 * r, plan.rhs), BF)
    basis_copy.wait()

    def keep(level, box, value):
        n = plan.count[level]
        if level < FULL:
            poles[pl.ds((plan.padded[level] + 3 + box) * r, r)] = value
            if n - 3 <= box <= n - 2:
                up[pl.ds(plan.msg_pole[level] + (box - n + 3) * r, r)] = value
            if 1 <= box <= 2:
                down[pl.ds(plan.msg_pole[level] + (box - 1) * r, r)] = value
        elif level == FULL:
            (up if box == 0 else down)[pl.ds(plan.msg_top, r)] = value
            (down2 if box == 0 else up2)[pl.ds(0, r)] = value
            pair4[pl.ds(box * r, r)] = value
        else:
            for message in (up2, down2):
                message[pl.ds(r, r)] = value
            top[...] = value

    def climb(level, box):
        if level <= FULL:
            pair = poles[pl.ds((plan.padded[level - 1] + 3 + 2 * box) * r, 2 * r)]
        else:
            pair = pair4[...]
        keep(level, box, dot(ts[plan.trans[level] + box], pair).astype(BF))

    done = [0] * LEVELS

    def climb_ready():
        ready = list(done)
        for level in range(1, LEVELS):
            while 2 * done[level] + 2 <= ready[level - 1]:
                climb(level, done[level])
                done[level] += 1

    for c in range(chunks):
        copies[c].wait()
        if c == 0:
            trans_copy.wait()
        climb_ready()
        for leaf in range(c * per, (c + 1) * per):
            x = padded_x[pl.ds(p * (leaf + 1), p)]
            keep(0, leaf, dot(bs[leaf], x).astype(BF))
        done[0] = (c + 1) * per
    while done[LEVELS - 1] < plan.count[LEVELS - 1]:
        climb_ready()
    for message, leaf, last in ((up, plan.leaves - 1, True), (down, 0, False)):
        message[pl.ds(0, p)] = padded_x[pl.ds(p * (leaf + 1), p)]
        message[pl.ds(plan.msg_small, r), pl.ds(0, p)] = bs[leaf]
        for level in range(1, FULL):
            box = plan.count[level] - 1 if last else 0
            message[pl.ds(plan.msg_small, r), pl.ds(level * p, p)] = ts[plan.trans[level] + box]
        matrix = plan.trans[FULL] + (plan.count[FULL] - 1 if last else 0)
        rows = plan.part_rows
        for part in range(plan.rhs // p):
            message[pl.ds(plan.msg_last, rows), pl.ds(part * p, p)] = ts[matrix, pl.ds(part * rows, rows)]


def inner_kernel(
    plan, chunks, pattern, flags, padded_x, poles, bs, ts, near_blocks, couplings,
    near, local, masked, edge_near, bs_t, ts_t, nb, sems,
):
    p, r = plan.panels, plan.rank
    per = plan.leaves // chunks
    half = couplings.shape[0] // 2
    coupling_copies = [
        pltpu.make_async_copy(couplings.at[pl.ds(a, n)], masked.at[pl.ds(a, n)], sems.at[chunks + k])
        for k, (a, n) in enumerate(((0, half), (half, couplings.shape[0] - half)))
    ]
    copies = [
        pltpu.make_async_copy(near_blocks.at[pl.ds(c * per, per)], nb.at[pl.ds(c * per, per)], sems.at[c])
        for c in range(chunks)
    ]
    for copy in coupling_copies + copies:
        copy.start()
    for box in range(ts.shape[0]):
        ts_t[box] = ts[box].T
    for leaf in range(bs.shape[0]):
        bs_t[leaf] = bs[leaf].T
    lane = lax.broadcasted_iota(jnp.int32, (r, 4 * r), 1)

    def mask(box):
        low = jnp.where(lane < r, flags[0, box], flags[1, box])
        high = jnp.where(lane < 3 * r, flags[2, box], flags[3, box])
        chosen = jnp.where(lane < 2 * r, low, high)
        value = masked[box] * chosen.astype(F32).astype(BF)
        masked[box] = value
        return value

    def couple(level, box):
        row = (plan.padded[level] + box) * r
        stack = jnp.concatenate([poles[pl.ds(row, 2 * r)], poles[pl.ds(row + 5 * r, 2 * r)]], axis=0)
        index = plan.first[level] + box
        local[pl.ds(index * r, r)] = dot(mask(index), stack)

    for copy in coupling_copies:
        copy.wait()
    for level in range(FULL):
        for box in range(plan.count[level]):
            couple(level, box)
    for box in range(plan.inner_boxes, sum(plan.count)):
        mask(box)

    def side(leaf, slot):
        block = nb[leaf, slot]
        return jnp.where(pattern[slot, leaf] != 0, block, jnp.zeros_like(block))

    def near_one(leaf):
        wide = jnp.concatenate([side(leaf, 0), nb[leaf, 1], side(leaf, 2)], axis=1)
        near[pl.ds(leaf * p, p)] = dot(wide, padded_x[pl.ds(leaf * p, 3 * p)]).astype(BF)

    for c in range(chunks):
        copies[c].wait()
    for leaf in range(plan.leaves):
        near_one(leaf)
    edge_near[0] = side(0, 0)
    edge_near[1] = side(plan.leaves - 1, 2)


def final_kernel(
    plan, near, local, masked, edge_near, bs_t, ts_t, below, above, below2, above2, below3, above3,
    out, loc, stage, sems,
):
    p, r, n = plan.panels, plan.rank, plan.leaves
    small = pl.ds(plan.msg_small, r)
    messages = (below, above)

    sent = [[message[pl.ds(plan.msg_pole[level], 2 * r)] for level in range(FULL)] for message in messages]
    rim = [[dot(message[small, pl.ds(0, p)], message[pl.ds(0, p)]).astype(BF)] for message in messages]
    for level in range(1, FULL + 1):
        for k, message in enumerate(messages):
            if level < FULL:
                matrix = message[small, pl.ds(level * p, p)]
            else:
                rows = pl.ds(plan.msg_last, plan.part_rows)
                matrix = jnp.concatenate([message[rows, pl.ds(part * p, p)] for part in range(plan.rhs // p)], axis=0)
            children = [sent[k][level - 1][r:], rim[k][-1]] if k == 0 else [rim[k][-1], sent[k][level - 1][:r]]
            rim[k].append(dot(matrix, jnp.concatenate(children, axis=0)).astype(BF))

    def place(level, box):
        return pl.ds((plan.first[level] + box) * r, r)

    stack = jnp.concatenate([below3[...], below2[pl.ds(r, r)], above2[pl.ds(r, r)], above3[...]], axis=0)
    summit = dot(masked[plan.first[LEVELS - 1]], stack).astype(BF)
    pushed = dot(ts_t[plan.trans[LEVELS - 1]], summit)
    low, high = below[pl.ds(plan.msg_top, r)], above[pl.ds(plan.msg_top, r)]
    stacks = ([below2[pl.ds(0, r)], low, rim[1][FULL], high], [low, rim[0][FULL], high, above2[pl.ds(0, r)]])
    for k, stack in enumerate(stacks):
        gained = dot(masked[plan.first[FULL] + k], jnp.concatenate(stack, axis=0))
        loc[place(FULL, k)] = (gained + pushed[k * r : (k + 1) * r]).astype(BF)

    def rim_gain(level, box):
        first, m = plan.first[level], plan.count[level]
        low = [sent[0][level][:r], sent[0][level][r:], rim[0][level]]
        high = [rim[1][level], sent[1][level][:r], sent[1][level][r:]]
        gain = None
        if box < 3:
            used = low[box : box + 2]
            gain = dot(masked[first + box, :, pl.ds(0, len(used) * r)], jnp.concatenate(used, axis=0))
        if box >= m - 3:
            from_end = box - (m - 3)
            used = high[max(from_end - 1, 0) : from_end + 1]
            start = (4 - len(used)) * r if from_end == 0 else 2 * r
            value = dot(masked[first + box, :, pl.ds(start, len(used) * r)], jnp.concatenate(used, axis=0))
            gain = value if gain is None else gain + value
        return gain

    for level in range(FULL, 0, -1):
        for box in range(plan.count[level]):
            push = dot(ts_t[plan.trans[level] + box], loc[place(level, box)])
            for k in range(2):
                child = 2 * box + k
                value = local[place(level - 1, child)] + push[k * r : (k + 1) * r]
                gain = rim_gain(level - 1, child)
                loc[place(level - 1, child)] = (value if gain is None else value + gain).astype(BF)

    writes = []
    per = n // sems.shape[0]
    for leaf in range(n):
        total = near[pl.ds(leaf * p, p)].astype(F32) + dot(bs_t[leaf], loc[place(0, leaf)])
        if leaf == 0:
            total = total + dot(edge_near[0], below[pl.ds(0, p)])
        if leaf == n - 1:
            total = total + dot(edge_near[1], above[pl.ds(0, p)])
        stage[pl.ds(leaf * p, p)] = total.astype(BF)
        if (leaf + 1) % per == 0:
            rows = pl.ds((leaf + 1 - per) * p, per * p)
            copy = pltpu.make_async_copy(stage.at[rows], out.at[rows], sems.at[leaf // per])
            copy.start()
            writes.append(copy)
    for copy in writes:
        copy.wait()


def shifted(array, by):
    peers = lax.axis_size("slab")
    pairs = [(i, i + by) for i in range(peers) if 0 <= i + by < peers]
    return lax.ppermute(array, "slab", pairs)


def body(charges, near_blocks, near_pattern, leaf_basis, transfers, couplings, interactions):
    leaves, panels, rank, rhs = near_blocks.shape[0], near_blocks.shape[2], leaf_basis.shape[1], charges.shape[1]
    plan = Plan(leaves, panels, rank, rhs)
    hbm = pl.BlockSpec(memory_space=pltpu.HBM)
    vmem = pl.BlockSpec(memory_space=pltpu.VMEM)
    smem = pl.BlockSpec(memory_space=pltpu.SMEM)
    chunks = 8

    padded_x, poles, up, down, up2, down2, top, bs, ts = pl.pallas_call(
        lambda *refs: upward_kernel(plan, chunks, *refs),
        in_specs=[hbm, hbm, hbm],
        out_specs=[vmem] * 9,
        out_shape=[
            resident(((leaves + 2) * panels, rhs), BF),
            resident((plan.padded_boxes * rank, rhs), BF),
            resident((plan.msg_rows, rhs), BF),
            resident((plan.msg_rows, rhs), BF),
            resident((2 * rank, rhs), BF),
            resident((2 * rank, rhs), BF),
            resident((rank, rhs), BF),
            resident(leaf_basis.shape, BF),
            resident(transfers.shape, BF),
        ],
        scratch_shapes=[pltpu.VMEM((2 * rank, rhs), BF), pltpu.SemaphoreType.DMA((chunks + 2,))],
        compiler_params=pltpu.CompilerParams(vmem_limit_bytes=6 * MIB),
        name="upward",
    )(stay(charges), stay(leaf_basis), stay(transfers))

    below, above = shifted(up, 1), shifted(down, -1)
    below2, above2 = shifted(up2, 2), shifted(down2, -2)
    below3, above3 = shifted(top, 3), shifted(top, -3)

    near, local, masked, edge_near, bs_t, ts_t = pl.pallas_call(
        lambda *refs: inner_kernel(plan, 4, *refs),
        in_specs=[smem, smem, vmem, vmem, vmem, vmem, hbm, hbm],
        out_specs=[vmem] * 6,
        out_shape=[
            resident((leaves * panels, rhs), BF),
            resident((plan.inner_boxes * rank, rhs), F32),
            resident(couplings.shape, BF),
            resident((2, panels, panels), BF),
            resident((leaves, panels, rank), BF),
            resident((transfers.shape[0], panels, rank), BF),
        ],
        scratch_shapes=[
            pltpu.VMEM(near_blocks.shape, BF),
            pltpu.SemaphoreType.DMA((6,)),
        ],
        compiler_params=pltpu.CompilerParams(vmem_limit_bytes=12 * MIB),
        cost_estimate=pl.CostEstimate(flops=12_000_000_000, bytes_accessed=16 * MIB, transcendentals=0),
        name="inner",
    )(
        near_pattern.T, interactions.T, keep(padded_x), keep(poles), keep(bs), keep(ts),
        stay(near_blocks), stay(couplings),
    )

    return pl.pallas_call(
        lambda *refs: final_kernel(plan, *refs),
        in_specs=[vmem] * 12,
        out_specs=hbm,
        out_shape=jax.ShapeDtypeStruct((leaves * panels, rhs), BF),
        scratch_shapes=[
            pltpu.VMEM((couplings.shape[0] * rank, rhs), BF),
            pltpu.VMEM((leaves * panels, rhs), BF),
            pltpu.SemaphoreType.DMA((leaves // 4,)),
        ],
        compiler_params=pltpu.CompilerParams(vmem_limit_bytes=14 * MIB),
        name="final",
    )(
        keep(near), keep(local), keep(masked), keep(edge_near), keep(bs_t), keep(ts_t),
        keep(below), keep(above), keep(below2), keep(above2), keep(below3), keep(above3),
    )


def solution(mesh):
    spec = ("groups", "slab")
    in_specs = (
        P(spec, None),
        P(spec, None, None, None),
        P(spec, None),
        P(spec, None, None),
        P(spec, None, None),
        P(spec, None, None),
        P(spec, None),
    )
    return jax.shard_map(body, mesh=mesh, in_specs=in_specs, out_specs=P(spec, None), check_vma=False)
```

time: 91.8 us -> 43.7 us (0.48)
  the two profiles are of different devices: /device:TPU:0 before, /device:TPU:16 now
where the time goes in v3:
time: 43.7 us; the launch traced here: 43.5 us
  starting transfers between devices  18.8 us (43%)
  Pallas kernels  17 us (39%)
  waiting for transfers between devices  7.66 us (18%)
    ppermute x6, starting transfers between devices, shifted(): return lax.ppermute(array, 'slab', pairs)  18.8 us
    pallas_call x1, Pallas kernels, body(): pl.pallas_call(lambda *refs: inner_kernel(plan, 4, *refs), in_specs=[smem...  7.67 us
    ppermute x6, waiting for transfers between devices, shifted(): return lax.ppermute(array, 'slab', pairs)  7.66 us
    pallas_call x1, Pallas kernels, body(): pl.pallas_call(lambda *refs: final_kernel(plan, *refs), in_specs=[vmem] *...  4.87 us
    pallas_call x1, Pallas kernels, body(): pl.pallas_call(lambda *refs: upward_kernel(plan, chunks, *refs), in_specs...  4.43 us
  transfers between devices with their start and end apart: 6, of which 2 were waited for; matrix products, arithmetic and copies ran while one was open for 0% of the time, Pallas kernels for 18%

profile of v3, /device:TPU:16, one launch (start us, length us, event | category | flops | bytes accessed | tf_op | source)
XLA Modules:
  0.0 43.5 jit_solution(3714250942409684645)
XLA Ops:
  0.0 0.0 copy-start
  0.0 0.0 copy-start.1
  0.0 4.4 %upward.1 = (bf16[4352,512]{1,0:T(8,128)(2,1)S(1)}, bf16[5376,512]{1,0:T(8,128)(2,1)S(1)}, bf16[784,512]{1,0:T(8,128)(2,1)S(1)}, bf16[784,512]{1,0:T(8,128)(2,1)...) custom-call(bf16[4096,512]{1,0:T(8,128)(2,1)} %refs_0_.1, ...), custom_call_target="tpu_custom_call" | custom-call | tf_op jit(solution)/shard_map/upward/pallas_call | solution.py:280
  4.4 2.8 %collective-permute-start.4 = (bf16[64,512]{1,0:T(8,128)(2,1)S(1)}, bf16[64,512]{1,0:T(8,128)(2,1)S(1)}, u32[]{:S(2)}, u32[]{:S(2)}) collective-permute-start(bf16[64,512]{1,0:T(8,128)(2,1)S(1)} %get-tuple-element.34), channel_id=1, source_target_pairs={{0,3},{1,4},{2,5},{3,6},{4,7},{5,8},{6,9},{7,10},{8,11},{9,12},{10... | collective-permute-start | bytes 196616 | tf_op jit(solution)/shard_map/ppermute | solution.py:269
  7.3 2.7 %collective-permute-start.5 = (bf16[64,512]{1,0:T(8,128)(2,1)S(1)}, bf16[64,512]{1,0:T(8,128)(2,1)S(1)}, u32[]{:S(2)}, u32[]{:S(2)}) collective-permute-start(bf16[64,512]{1,0:T(8,128)(2,1)S(1)} %get-tuple-element.34), channel_id=1, source_target_pairs={{3,0},{4,1},{5,2},{6,3},{7,4},{8,5},{9,6},{10,7},{11,8},{12,9},{13... | collective-permute-start | bytes 196616 | tf_op jit(solution)/shard_map/ppermute | solution.py:269
  10.0 2.6 %collective-permute-start = (bf16[784,512]{1,0:T(8,128)(2,1)S(1)}, bf16[784,512]{1,0:T(8,128)(2,1)S(1)}, u32[]{:S(2)}, u32[]{:S(2)}) collective-permute-start(bf16[784,512]{1,0:T(8,128)(2,1)S(1)} %get-tuple-element.30), channel_id=1, source_target_pairs={{0,1},{1,2},{2,3},{3,4},{4,5},{5,6},{6,7},{7,8},{8,9},{9,10},{10,1... | collective-permute-start | bytes 2408456 | tf_op jit(solution)/shard_map/ppermute | solution.py:269
  12.7 3.8 %collective-permute-start.1 = (bf16[784,512]{1,0:T(8,128)(2,1)S(1)}, bf16[784,512]{1,0:T(8,128)(2,1)S(1)}, u32[]{:S(2)}, u32[]{:S(2)}) collective-permute-start(bf16[784,512]{1,0:T(8,128)(2,1)S(1)} %get-tuple-element.31), channel_id=1, source_target_pairs={{1,0},{2,1},{3,2},{4,3},{5,4},{6,5},{7,6},{8,7},{9,8},{10,9},{11,1... | collective-permute-start | bytes 2408456 | tf_op jit(solution)/shard_map/ppermute | solution.py:269
  16.5 2.5 %collective-permute-start.2 = (bf16[128,512]{1,0:T(8,128)(2,1)S(1)}, bf16[128,512]{1,0:T(8,128)(2,1)S(1)}, u32[]{:S(2)}, u32[]{:S(2)}) collective-permute-start(bf16[128,512]{1,0:T(8,128)(2,1)S(1)} %get-tuple-element.32), channel_id=1, source_target_pairs={{0,2},{1,3},{2,4},{3,5},{4,6},{5,7},{6,8},{7,9},{8,10},{9,11},{10,... | collective-permute-start | bytes 393224 | tf_op jit(solution)/shard_map/ppermute | solution.py:269
  19.0 0.0 collective-permute-done.4.refs_10_
  19.0 4.2 %collective-permute-start.3 = (bf16[128,512]{1,0:T(8,128)(2,1)S(1)}, bf16[128,512]{1,0:T(8,128)(2,1)S(1)}, u32[]{:S(2)}, u32[]{:S(2)}) collective-permute-start(bf16[128,512]{1,0:T(8,128)(2,1)S(1)} %get-tuple-element.33), channel_id=1, source_target_pairs={{2,0},{3,1},{4,2},{5,3},{6,4},{7,5},{8,6},{9,7},{10,8},{11,9},{12,... | collective-permute-start | bytes 393224 | tf_op jit(solution)/shard_map/ppermute | solution.py:269
  23.3 0.0 copy-done
  23.3 0.0 copy-done.1
  23.3 7.7 %inner.1 = (bf16[4096,512]{1,0:T(8,128)(2,1)S(1)}, f32[3840,512]{1,0:T(8,128)S(1)}, bf16[63,64,256]{2,1,0:T(8,128)(2,1)S(1)}, bf16[2,128,128]{2,1,0:T(8,128)(2,1...) custom-call(s32[3,32]{1,0:T(4,128)S(1)} %bitcast.2, s32[4,63]{1,0:T(4,128)S(1)} %bitcast.3, ...), custom_call_target="tpu_custom_call" | custom-call | flops 12000000000 | bytes 16777216 | tf_op jit(solution)/shard_map/inner/pallas_call | solution.py:304
  31.0 0.0 collective-permute-done.5.refs_11_
  31.0 2.0 %collective-permute-done.2.refs_8_ = bf16[128,512]{1,0:T(8,128)(2,1)S(1)} collective-permute-done((bf16[128,512]{1,0:T(8,128)(2,1)S(1)}, bf16[128,512]{1,0:T(8,128)(2,1)S(1)}, u32[]{:S(2)}, u32[]{:S(2)}) %collective-permute-start.2) | collective-permute-done | bytes 131104 | tf_op jit(solution)/shard_map/ppermute | solution.py:269
  32.9 5.7 %collective-permute-done.3.refs_9_ = bf16[128,512]{1,0:T(8,128)(2,1)S(1)} collective-permute-done((bf16[128,512]{1,0:T(8,128)(2,1)S(1)}, bf16[128,512]{1,0:T(8,128)(2,1)S(1)}, u32[]{:S(2)}, u32[]{:S(2)}) %collective-permute-start.3) | collective-permute-done | bytes 131104 | tf_op jit(solution)/shard_map/ppermute | solution.py:269
  38.6 0.0 collective-permute-done.refs_6_
  38.6 0.0 collective-permute-done.1.refs_7_
  38.6 4.9 %final.1 = bf16[4096,512]{1,0:T(8,128)(2,1)} custom-call(bf16[4096,512]{1,0:T(8,128)(2,1)S(1)} %get-tuple-element.24.refs_0_, f32[3840,512]{1,0:T(8,128)S(1)} %get-tuple-element.25.refs_1_, bf16[63,64,256]{2,1,0:T(8,128)(2,1)S(1)} %get-tuple-element.26.refs_2_, bf16[2,128,128]{2,1,0:T(8,128)(2,1)S(1)} %get-tuple-element.27.refs_3_, ...), custom_call_target="tpu_custom_call" | custom-call | tf_op jit(solution)/shard_map/final/pallas_call | solution.py:328
Async XLA Ops:
  0.0 23.3 %copy-start = (s32[32,3]{0,1:T(4,128)S(1)}, s32[32,3]{0,1:T(4,128)}, u32[]{:S(2)}) copy-start(s32[32,3]{0,1:T(4,128)} %param.9) | copy-start | bytes 1156
  0.0 23.3 %copy-start.1 = (s32[63,4]{0,1:T(4,128)S(1)}, s32[63,4]{0,1:T(4,128)}, u32[]{:S(2)}) copy-start(s32[63,4]{0,1:T(4,128)} %param.13) | copy-start | bytes 3028
  4.4 14.6 %collective-permute-start.4 = (bf16[64,512]{1,0:T(8,128)(2,1)S(1)}, bf16[64,512]{1,0:T(8,128)(2,1)S(1)}, u32[]{:S(2)}, u32[]{:S(2)}) collective-permute-start(bf16[64,512]{1,0:T(8,128)(2,1)S(1)} %get-tuple-element.34), channel_id=1, source_target_pairs={{0,3},{1,4},{2,5},{3,6},{4,7},{5,8},{6,9},{7,10},{8,11},{9,12},{10... | collective-permute-start | bytes 196616 | tf_op jit(solution)/shard_map/ppermute | solution.py:269
  7.3 23.7 %collective-permute-start.5 = (bf16[64,512]{1,0:T(8,128)(2,1)S(1)}, bf16[64,512]{1,0:T(8,128)(2,1)S(1)}, u32[]{:S(2)}, u32[]{:S(2)}) collective-permute-start(bf16[64,512]{1,0:T(8,128)(2,1)S(1)} %get-tuple-element.34), channel_id=1, source_target_pairs={{3,0},{4,1},{5,2},{6,3},{7,4},{8,5},{9,6},{10,7},{11,8},{12,9},{13... | collective-permute-start | bytes 196616 | tf_op jit(solution)/shard_map/ppermute | solution.py:269
  10.0 28.6 %collective-permute-start = (bf16[784,512]{1,0:T(8,128)(2,1)S(1)}, bf16[784,512]{1,0:T(8,128)(2,1)S(1)}, u32[]{:S(2)}, u32[]{:S(2)}) collective-permute-start(bf16[784,512]{1,0:T(8,128)(2,1)S(1)} %get-tuple-element.30), channel_id=1, source_target_pairs={{0,1},{1,2},{2,3},{3,4},{4,5},{5,6},{6,7},{7,8},{8,9},{9,10},{10,1... | collective-permute-start | bytes 2408456 | tf_op jit(solution)/shard_map/ppermute | solution.py:269
  12.7 26.0 %collective-permute-start.1 = (bf16[784,512]{1,0:T(8,128)(2,1)S(1)}, bf16[784,512]{1,0:T(8,128)(2,1)S(1)}, u32[]{:S(2)}, u32[]{:S(2)}) collective-permute-start(bf16[784,512]{1,0:T(8,128)(2,1)S(1)} %get-tuple-element.31), channel_id=1, source_target_pairs={{1,0},{2,1},{3,2},{4,3},{5,4},{6,5},{7,6},{8,7},{9,8},{10,9},{11,1... | collective-permute-start | bytes 2408456 | tf_op jit(solution)/shard_map/ppermute | solution.py:269
  16.5 16.4 %collective-permute-start.2 = (bf16[128,512]{1,0:T(8,128)(2,1)S(1)}, bf16[128,512]{1,0:T(8,128)(2,1)S(1)}, u32[]{:S(2)}, u32[]{:S(2)}) collective-permute-start(bf16[128,512]{1,0:T(8,128)(2,1)S(1)} %get-tuple-element.32), channel_id=1, source_target_pairs={{0,2},{1,3},{2,4},{3,5},{4,6},{5,7},{6,8},{7,9},{8,10},{9,11},{10,... | collective-permute-start | bytes 393224 | tf_op jit(solution)/shard_map/ppermute | solution.py:269
  19.0 19.6 %collective-permute-start.3 = (bf16[128,512]{1,0:T(8,128)(2,1)S(1)}, bf16[128,512]{1,0:T(8,128)(2,1)S(1)}, u32[]{:S(2)}, u32[]{:S(2)}) collective-permute-start(bf16[128,512]{1,0:T(8,128)(2,1)S(1)} %get-tuple-element.33), channel_id=1, source_target_pairs={{2,0},{3,1},{4,2},{5,3},{6,4},{7,5},{8,6},{9,7},{10,8},{11,9},{12,... | collective-permute-start | bytes 393224 | tf_op jit(solution)/shard_map/ppermute | solution.py:269

commit v4 on v3

--- a/solution.py
+++ b/solution.py
@@ -45,7 +45,7 @@
         self.msg_rows = self.msg_last + self.part_rows
 
 
-def upward_kernel(plan, chunks, charges, basis, transfers, padded_x, poles, up, down, up2, down2, top, bs, ts, pair4, sems):
+def upward_kernel(plan, chunks, charges, basis, transfers, padded_x, poles, up, down, top, pair4, bs, ts, sems):
     p, r = plan.panels, plan.rank
     per = plan.leaves // chunks
     copies = []
@@ -81,11 +81,8 @@
                 down[pl.ds(plan.msg_pole[level] + (box - 1) * r, r)] = value
         elif level == FULL:
             (up if box == 0 else down)[pl.ds(plan.msg_top, r)] = value
-            (down2 if box == 0 else up2)[pl.ds(0, r)] = value
             pair4[pl.ds(box * r, r)] = value
         else:
-            for message in (up2, down2):
-                message[pl.ds(r, r)] = value
             top[...] = value
 
     def climb(level, box):
@@ -127,23 +124,23 @@
             message[pl.ds(plan.msg_last, rows), pl.ds(part * p, p)] = ts[matrix, pl.ds(part * rows, rows)]
 
 
-def inner_kernel(
-    plan, chunks, pattern, flags, padded_x, poles, bs, ts, near_blocks, couplings,
-    near, local, masked, edge_near, bs_t, ts_t, nb, sems,
+def couple_kernel(
+    plan, flags, poles, bs, ts, top, pair_top, couplings,
+    local, masked, bs_t, ts_t, up2, down2, top_out, sems,
 ):
     p, r = plan.panels, plan.rank
-    per = plan.leaves // chunks
     half = couplings.shape[0] // 2
-    coupling_copies = [
-        pltpu.make_async_copy(couplings.at[pl.ds(a, n)], masked.at[pl.ds(a, n)], sems.at[chunks + k])
+    copies = [
+        pltpu.make_async_copy(couplings.at[pl.ds(a, n)], masked.at[pl.ds(a, n)], sems.at[k])
         for k, (a, n) in enumerate(((0, half), (half, couplings.shape[0] - half)))
     ]
-    copies = [
-        pltpu.make_async_copy(near_blocks.at[pl.ds(c * per, per)], nb.at[pl.ds(c * per, per)], sems.at[c])
-        for c in range(chunks)
-    ]
-    for copy in coupling_copies + copies:
+    for copy in copies:
         copy.start()
+    up2[pl.ds(0, r)] = pair_top[pl.ds(r, r)]
+    down2[pl.ds(0, r)] = pair_top[pl.ds(0, r)]
+    for message in (up2, down2):
+        message[pl.ds(r, r)] = top[...]
+    top_out[...] = top[...]
     for box in range(ts.shape[0]):
         ts_t[box] = ts[box].T
     for leaf in range(bs.shape[0]):
@@ -158,32 +155,37 @@
         masked[box] = value
         return value
 
-    def couple(level, box):
-        row = (plan.padded[level] + box) * r
-        stack = jnp.concatenate([poles[pl.ds(row, 2 * r)], poles[pl.ds(row + 5 * r, 2 * r)]], axis=0)
-        index = plan.first[level] + box
-        local[pl.ds(index * r, r)] = dot(mask(index), stack)
-
-    for copy in coupling_copies:
+    for copy in copies:
         copy.wait()
     for level in range(FULL):
         for box in range(plan.count[level]):
-            couple(level, box)
+            row = (plan.padded[level] + box) * r
+            stack = jnp.concatenate([poles[pl.ds(row, 2 * r)], poles[pl.ds(row + 5 * r, 2 * r)]], axis=0)
+            index = plan.first[level] + box
+            local[pl.ds(index * r, r)] = dot(mask(index), stack)
     for box in range(plan.inner_boxes, sum(plan.count)):
         mask(box)
+
+
+def near_kernel(plan, chunks, pattern, padded_x, near_blocks, near, edge_near, nb, sems):
+    p = plan.panels
+    per = plan.leaves // chunks
+    copies = [
+        pltpu.make_async_copy(near_blocks.at[pl.ds(c * per, per)], nb.at[pl.ds(c * per, per)], sems.at[c])
+        for c in range(chunks)
+    ]
+    for copy in copies:
+        copy.start()
 
     def side(leaf, slot):
         block = nb[leaf, slot]
         return jnp.where(pattern[slot, leaf] != 0, block, jnp.zeros_like(block))
 
-    def near_one(leaf):
-        wide = jnp.concatenate([side(leaf, 0), nb[leaf, 1], side(leaf, 2)], axis=1)
-        near[pl.ds(leaf * p, p)] = dot(wide, padded_x[pl.ds(leaf * p, 3 * p)]).astype(BF)
-
     for c in range(chunks):
         copies[c].wait()
-    for leaf in range(plan.leaves):
-        near_one(leaf)
+        for leaf in range(c * per, (c + 1) * per):
+            wide = jnp.concatenate([side(leaf, 0), nb[leaf, 1], side(leaf, 2)], axis=1)
+            near[pl.ds(leaf * p, p)] = dot(wide, padded_x[pl.ds(leaf * p, 3 * p)]).astype(BF)
     edge_near[0] = side(0, 0)
     edge_near[1] = side(plan.leaves - 1, 2)
 
@@ -277,53 +279,62 @@
     smem = pl.BlockSpec(memory_space=pltpu.SMEM)
     chunks = 8
 
-    padded_x, poles, up, down, up2, down2, top, bs, ts = pl.pallas_call(
+    padded_x, poles, up, down, top, pair_top, bs, ts = pl.pallas_call(
         lambda *refs: upward_kernel(plan, chunks, *refs),
         in_specs=[hbm, hbm, hbm],
-        out_specs=[vmem] * 9,
+        out_specs=[vmem] * 8,
         out_shape=[
             resident(((leaves + 2) * panels, rhs), BF),
             resident((plan.padded_boxes * rank, rhs), BF),
             resident((plan.msg_rows, rhs), BF),
             resident((plan.msg_rows, rhs), BF),
+            resident((rank, rhs), BF),
+            resident((2 * rank, rhs), BF),
+            resident(leaf_basis.shape, BF),
+            resident(transfers.shape, BF),
+        ],
+        scratch_shapes=[pltpu.SemaphoreType.DMA((chunks + 2,))],
+        compiler_params=pltpu.CompilerParams(vmem_limit_bytes=6 * MIB),
+        name="upward",
+    )(stay(charges), stay(leaf_basis), stay(transfers))
+
+    below, above = shifted(up, 1), shifted(down, -1)
+
+    local, masked, bs_t, ts_t, up2, down2, top = pl.pallas_call(
+        lambda *refs: couple_kernel(plan, *refs),
+        in_specs=[smem, vmem, vmem, vmem, vmem, vmem, hbm],
+        out_specs=[vmem] * 7,
+        out_shape=[
+            resident((plan.inner_boxes * rank, rhs), F32),
+            resident(couplings.shape, BF),
+            resident((leaves, panels, rank), BF),
+            resident((transfers.shape[0], panels, rank), BF),
             resident((2 * rank, rhs), BF),
             resident((2 * rank, rhs), BF),
             resident((rank, rhs), BF),
-            resident(leaf_basis.shape, BF),
-            resident(transfers.shape, BF),
         ],
-        scratch_shapes=[pltpu.VMEM((2 * rank, rhs), BF), pltpu.SemaphoreType.DMA((chunks + 2,))],
-        compiler_params=pltpu.CompilerParams(vmem_limit_bytes=6 * MIB),
-        name="upward",
-    )(stay(charges), stay(leaf_basis), stay(transfers))
-
-    below, above = shifted(up, 1), shifted(down, -1)
+        scratch_shapes=[pltpu.SemaphoreType.DMA((2,))],
+        compiler_params=pltpu.CompilerParams(vmem_limit_bytes=8 * MIB),
+        cost_estimate=pl.CostEstimate(flops=6_000_000_000, bytes_accessed=8 * MIB, transcendentals=0),
+        name="couple",
+    )(interactions.T, keep(poles), keep(bs), keep(ts), keep(top), keep(pair_top), stay(couplings))
+
     below2, above2 = shifted(up2, 2), shifted(down2, -2)
     below3, above3 = shifted(top, 3), shifted(top, -3)
 
-    near, local, masked, edge_near, bs_t, ts_t = pl.pallas_call(
-        lambda *refs: inner_kernel(plan, 4, *refs),
-        in_specs=[smem, smem, vmem, vmem, vmem, vmem, hbm, hbm],
-        out_specs=[vmem] * 6,
+    near, edge_near = pl.pallas_call(
+        lambda *refs: near_kernel(plan, 4, *refs),
+        in_specs=[smem, vmem, hbm],
+        out_specs=[vmem] * 2,
         out_shape=[
             resident((leaves * panels, rhs), BF),
-            resident((plan.inner_boxes * rank, rhs), F32),
-            resident(couplings.shape, BF),
             resident((2, panels, panels), BF),
-            resident((leaves, panels, rank), BF),
-            resident((transfers.shape[0], panels, rank), BF),
         ],
-        scratch_shapes=[
-            pltpu.VMEM(near_blocks.shape, BF),
-            pltpu.SemaphoreType.DMA((6,)),
-        ],
-        compiler_params=pltpu.CompilerParams(vmem_limit_bytes=12 * MIB),
-        cost_estimate=pl.CostEstimate(flops=12_000_000_000, bytes_accessed=16 * MIB, transcendentals=0),
-        name="inner",
-    )(
-        near_pattern.T, interactions.T, keep(padded_x), keep(poles), keep(bs), keep(ts),
-        stay(near_blocks), stay(couplings),
-    )
+        scratch_shapes=[pltpu.VMEM(near_blocks.shape, BF), pltpu.SemaphoreType.DMA((4,))],
+        compiler_params=pltpu.CompilerParams(vmem_limit_bytes=10 * MIB),
+        cost_estimate=pl.CostEstimate(flops=6_000_000_000, bytes_accessed=8 * MIB, transcendentals=0),
+        name="near",
+    )(near_pattern.T, keep(padded_x), stay(near_blocks))
 
     return pl.pallas_call(
         lambda *refs: final_kernel(plan, *refs),

time: 43.7 us -> 39.6 us (0.906)
  waiting for transfers between devices: 7.66 us -> 1.35 us
  Pallas kernels: 17 us -> 19.1 us
    ppermute x6, waiting for transfers between devices: 7.66 us -> 1.35 us  [shifted(): return lax.ppermute(array, 'slab', pairs)]
    pallas_call x1 -> x2, Pallas kernels: 7.67 us -> 9.78 us  [the longest x1 5.16 us: body(): pl.pallas_call(lambda *refs: couple_kernel(plan, *refs), in_specs=[smem,...]
  transfers between devices with their start and end apart: 6 -> 6, of which waited for: 2 -> 1; matrix products, arithmetic and copies ran while one was open for 0% -> 0% of each run, Pallas kernels for 18% -> 25%
where the time goes in v4:
time: 39.6 us; the launch traced here: 39.3 us
  Pallas kernels  19.1 us (48%)
  starting transfers between devices  18.8 us (47%)
  waiting for transfers between devices  1.35 us (3%)
    ppermute x6, starting transfers between devices, shifted(): return lax.ppermute(array, 'slab', pairs)  18.8 us
    pallas_call x1, Pallas kernels, body(): pl.pallas_call(lambda *refs: couple_kernel(plan, *refs), in_specs=[smem,...  5.16 us
    pallas_call x1, Pallas kernels, body(): pl.pallas_call(lambda *refs: final_kernel(plan, *refs), in_specs=[vmem] *...  4.89 us
    pallas_call x1, Pallas kernels, body(): pl.pallas_call(lambda *refs: near_kernel(plan, 4, *refs), in_specs=[smem,...  4.63 us
    pallas_call x1, Pallas kernels, body(): pl.pallas_call(lambda *refs: upward_kernel(plan, chunks, *refs), in_specs...  4.41 us
    ppermute x6, waiting for transfers between devices, shifted(): return lax.ppermute(array, 'slab', pairs)  1.35 us
  transfers between devices with their start and end apart: 6, of which 1 were waited for; matrix products, arithmetic and copies ran while one was open for 0% of the time, Pallas kernels for 25%

profile of v4, /device:TPU:16, one launch (start us, length us, event | category | flops | bytes accessed | tf_op | source)
XLA Modules:
  0.0 39.3 jit_solution(18272817418689018367)
XLA Ops:
  0.0 0.0 copy-start
  0.0 4.4 %upward.1 = (bf16[4352,512]{1,0:T(8,128)(2,1)S(1)}, bf16[5376,512]{1,0:T(8,128)(2,1)S(1)}, bf16[784,512]{1,0:T(8,128)(2,1)S(1)}, bf16[784,512]{1,0:T(8,128)(2,1)...) custom-call(bf16[4096,512]{1,0:T(8,128)(2,1)} %refs_0_.1, ...), custom_call_target="tpu_custom_call" | custom-call | tf_op jit(solution)/shard_map/upward/pallas_call | solution.py:282
  4.4 1.9 %collective-permute-start = (bf16[784,512]{1,0:T(8,128)(2,1)S(1)}, bf16[784,512]{1,0:T(8,128)(2,1)S(1)}, u32[]{:S(2)}, u32[]{:S(2)}) collective-permute-start(bf16[784,512]{1,0:T(8,128)(2,1)S(1)} %get-tuple-element.34), channel_id=1, source_target_pairs={{0,1},{1,2},{2,3},{3,4},{4,5},{5,6},{6,7},{7,8},{8,9},{9,10},{10,1... | collective-permute-start | bytes 2408456 | tf_op jit(solution)/shard_map/ppermute | solution.py:271
  6.3 4.5 %collective-permute-start.1 = (bf16[784,512]{1,0:T(8,128)(2,1)S(1)}, bf16[784,512]{1,0:T(8,128)(2,1)S(1)}, u32[]{:S(2)}, u32[]{:S(2)}) collective-permute-start(bf16[784,512]{1,0:T(8,128)(2,1)S(1)} %get-tuple-element.35), channel_id=1, source_target_pairs={{1,0},{2,1},{3,2},{4,3},{5,4},{6,5},{7,6},{8,7},{9,8},{10,9},{11,1... | collective-permute-start | bytes 2408456 | tf_op jit(solution)/shard_map/ppermute | solution.py:271
  10.9 0.0 copy-done
  10.9 0.0 copy-start.1
  10.9 5.2 %couple.1 = (f32[3840,512]{1,0:T(8,128)S(1)}, bf16[63,64,256]{2,1,0:T(8,128)(2,1)S(1)}, bf16[32,128,64]{2,1,0:T(8,128)(2,1)S(1)}, bf16[31,128,64]{2,1,0:T(8,128)...) custom-call(s32[4,63]{1,0:T(4,128)S(1)} %bitcast.2, ...), custom_call_target="tpu_custom_call" | custom-call | flops 6000000000 | bytes 8388608 | tf_op jit(solution)/shard_map/couple/pallas_call | solution.py:303
  16.1 1.9 %collective-permute-start.5 = (bf16[64,512]{1,0:T(8,128)(2,1)S(1)}, bf16[64,512]{1,0:T(8,128)(2,1)S(1)}, u32[]{:S(2)}, u32[]{:S(2)}) collective-permute-start(bf16[64,512]{1,0:T(8,128)(2,1)S(1)} %get-tuple-element.38), channel_id=1, source_target_pairs={{3,0},{4,1},{5,2},{6,3},{7,4},{8,5},{9,6},{10,7},{11,8},{12,9},{13... | collective-permute-start | bytes 196616 | tf_op jit(solution)/shard_map/ppermute | solution.py:271
  18.0 3.6 %collective-permute-start.4 = (bf16[64,512]{1,0:T(8,128)(2,1)S(1)}, bf16[64,512]{1,0:T(8,128)(2,1)S(1)}, u32[]{:S(2)}, u32[]{:S(2)}) collective-permute-start(bf16[64,512]{1,0:T(8,128)(2,1)S(1)} %get-tuple-element.38), channel_id=1, source_target_pairs={{0,3},{1,4},{2,5},{3,6},{4,7},{5,8},{6,9},{7,10},{8,11},{9,12},{10... | collective-permute-start | bytes 196616 | tf_op jit(solution)/shard_map/ppermute | solution.py:271
  21.7 3.4 %collective-permute-start.2 = (bf16[128,512]{1,0:T(8,128)(2,1)S(1)}, bf16[128,512]{1,0:T(8,128)(2,1)S(1)}, u32[]{:S(2)}, u32[]{:S(2)}) collective-permute-start(bf16[128,512]{1,0:T(8,128)(2,1)S(1)} %get-tuple-element.36), channel_id=1, source_target_pairs={{0,2},{1,3},{2,4},{3,5},{4,6},{5,7},{6,8},{7,9},{8,10},{9,11},{10,... | collective-permute-start | bytes 393224 | tf_op jit(solution)/shard_map/ppermute | solution.py:271
  25.1 0.0 collective-permute-done.5.refs_11_
  25.1 3.3 %collective-permute-start.3 = (bf16[128,512]{1,0:T(8,128)(2,1)S(1)}, bf16[128,512]{1,0:T(8,128)(2,1)S(1)}, u32[]{:S(2)}, u32[]{:S(2)}) collective-permute-start(bf16[128,512]{1,0:T(8,128)(2,1)S(1)} %get-tuple-element.37), channel_id=1, source_target_pairs={{2,0},{3,1},{4,2},{5,3},{6,4},{7,5},{8,6},{9,7},{10,8},{11,9},{12,... | collective-permute-start | bytes 393224 | tf_op jit(solution)/shard_map/ppermute | solution.py:271
  28.4 0.0 copy-done.1
  28.4 4.6 %near.1 = (bf16[4096,512]{1,0:T(8,128)(2,1)S(1)}, bf16[2,128,128]{2,1,0:T(8,128)(2,1)S(1)}) custom-call(s32[3,32]{1,0:T(4,128)S(1)} %bitcast.3, bf16[4352,512]{1,0:T(8,128)(2,1)S(1)} %get-tuple-element.22.refs_1_, bf16[32,3,128,128]{3,2,1,0:T(8,128)(2,1)} %refs_2_.3), custom_call_target="tpu_custom_call" | custom-call | flops 6000000000 | bytes 8388608 | tf_op jit(solution)/shard_map/near/pallas_call | solution.py:325
  33.1 0.0 collective-permute-done.4.refs_10_
  33.1 0.0 collective-permute-done.2.refs_8_
  33.1 1.3 %collective-permute-done.3.refs_9_ = bf16[128,512]{1,0:T(8,128)(2,1)S(1)} collective-permute-done((bf16[128,512]{1,0:T(8,128)(2,1)S(1)}, bf16[128,512]{1,0:T(8,128)(2,1)S(1)}, u32[]{:S(2)}, u32[]{:S(2)}) %collective-permute-start.3) | collective-permute-done | bytes 131104 | tf_op jit(solution)/shard_map/ppermute | solution.py:271
  34.4 0.0 collective-permute-done.refs_6_
  34.4 0.0 collective-permute-done.1.refs_7_
  34.4 4.9 %final.1 = bf16[4096,512]{1,0:T(8,128)(2,1)} custom-call(bf16[4096,512]{1,0:T(8,128)(2,1)S(1)} %get-tuple-element.23.refs_0_, f32[3840,512]{1,0:T(8,128)S(1)} %get-tuple-element.29.refs_1_, bf16[63,64,256]{2,1,0:T(8,128)(2,1)S(1)} %get-tuple-element.30.refs_2_, bf16[2,128,128]{2,1,0:T(8,128)(2,1)S(1)} %get-tuple-element.31.refs_3_, ...), custom_call_target="tpu_custom_call" | custom-call | tf_op jit(solution)/shard_map/final/pallas_call | solution.py:339
Async XLA Ops:
  0.0 10.9 %copy-start = (s32[63,4]{0,1:T(4,128)S(1)}, s32[63,4]{0,1:T(4,128)}, u32[]{:S(2)}) copy-start(s32[63,4]{0,1:T(4,128)} %param.13) | copy-start | bytes 3028
  4.4 30.0 %collective-permute-start = (bf16[784,512]{1,0:T(8,128)(2,1)S(1)}, bf16[784,512]{1,0:T(8,128)(2,1)S(1)}, u32[]{:S(2)}, u32[]{:S(2)}) collective-permute-start(bf16[784,512]{1,0:T(8,128)(2,1)S(1)} %get-tuple-element.34), channel_id=1, source_target_pairs={{0,1},{1,2},{2,3},{3,4},{4,5},{5,6},{6,7},{7,8},{8,9},{9,10},{10,1... | collective-permute-start | bytes 2408456 | tf_op jit(solution)/shard_map/ppermute | solution.py:271
  6.3 28.1 %collective-permute-start.1 = (bf16[784,512]{1,0:T(8,128)(2,1)S(1)}, bf16[784,512]{1,0:T(8,128)(2,1)S(1)}, u32[]{:S(2)}, u32[]{:S(2)}) collective-permute-start(bf16[784,512]{1,0:T(8,128)(2,1)S(1)} %get-tuple-element.35), channel_id=1, source_target_pairs={{1,0},{2,1},{3,2},{4,3},{5,4},{6,5},{7,6},{8,7},{9,8},{10,9},{11,1... | collective-permute-start | bytes 2408456 | tf_op jit(solution)/shard_map/ppermute | solution.py:271
  10.9 17.5 %copy-start.1 = (s32[32,3]{0,1:T(4,128)S(1)}, s32[32,3]{0,1:T(4,128)}, u32[]{:S(2)}) copy-start(s32[32,3]{0,1:T(4,128)} %param.9) | copy-start | bytes 1156
  16.1 9.0 %collective-permute-start.5 = (bf16[64,512]{1,0:T(8,128)(2,1)S(1)}, bf16[64,512]{1,0:T(8,128)(2,1)S(1)}, u32[]{:S(2)}, u32[]{:S(2)}) collective-permute-start(bf16[64,512]{1,0:T(8,128)(2,1)S(1)} %get-tuple-element.38), channel_id=1, source_target_pairs={{3,0},{4,1},{5,2},{6,3},{7,4},{8,5},{9,6},{10,7},{11,8},{12,9},{13... | collective-permute-start | bytes 196616 | tf_op jit(solution)/shard_map/ppermute | solution.py:271
  18.0 15.1 %collective-permute-start.4 = (bf16[64,512]{1,0:T(8,128)(2,1)S(1)}, bf16[64,512]{1,0:T(8,128)(2,1)S(1)}, u32[]{:S(2)}, u32[]{:S(2)}) collective-permute-start(bf16[64,512]{1,0:T(8,128)(2,1)S(1)} %get-tuple-element.38), channel_id=1, source_target_pairs={{0,3},{1,4},{2,5},{3,6},{4,7},{5,8},{6,9},{7,10},{8,11},{9,12},{10... | collective-permute-start | bytes 196616 | tf_op jit(solution)/shard_map/ppermute | solution.py:271
  21.7 11.4 %collective-permute-start.2 = (bf16[128,512]{1,0:T(8,128)(2,1)S(1)}, bf16[128,512]{1,0:T(8,128)(2,1)S(1)}, u32[]{:S(2)}, u32[]{:S(2)}) collective-permute-start(bf16[128,512]{1,0:T(8,128)(2,1)S(1)} %get-tuple-element.36), channel_id=1, source_target_pairs={{0,2},{1,3},{2,4},{3,5},{4,6},{5,7},{6,8},{7,9},{8,10},{9,11},{10,... | collective-permute-start | bytes 393224 | tf_op jit(solution)/shard_map/ppermute | solution.py:271
  25.1 9.3 %collective-permute-start.3 = (bf16[128,512]{1,0:T(8,128)(2,1)S(1)}, bf16[128,512]{1,0:T(8,128)(2,1)S(1)}, u32[]{:S(2)}, u32[]{:S(2)}) collective-permute-start(bf16[128,512]{1,0:T(8,128)(2,1)S(1)} %get-tuple-element.37), channel_id=1, source_target_pairs={{2,0},{3,1},{4,2},{5,3},{6,4},{7,5},{8,6},{9,7},{10,8},{11,9},{12,... | collective-permute-start | bytes 393224 | tf_op jit(solution)/shard_map/ppermute | solution.py:271

commit v5 on v4

--- a/solution.py
+++ b/solution.py
@@ -45,7 +45,7 @@
         self.msg_rows = self.msg_last + self.part_rows
 
 
-def upward_kernel(plan, chunks, charges, basis, transfers, padded_x, poles, up, down, top, pair4, bs, ts, sems):
+def upward_kernel(plan, chunks, charges, basis, transfers, padded_x, poles, up, down, up2, down2, top, bs, ts, pair4, sems):
     p, r = plan.panels, plan.rank
     per = plan.leaves // chunks
     copies = []
@@ -81,8 +81,11 @@
                 down[pl.ds(plan.msg_pole[level] + (box - 1) * r, r)] = value
         elif level == FULL:
             (up if box == 0 else down)[pl.ds(plan.msg_top, r)] = value
+            (down2 if box == 0 else up2)[pl.ds(0, r)] = value
             pair4[pl.ds(box * r, r)] = value
         else:
+            for message in (up2, down2):
+                message[pl.ds(r, r)] = value
             top[...] = value
 
     def climb(level, box):
@@ -125,21 +128,10 @@
 
 
 def couple_kernel(
-    plan, flags, poles, bs, ts, top, pair_top, couplings,
-    local, masked, bs_t, ts_t, up2, down2, top_out, sems,
+    plan, flags, poles, bs, ts, top, couplings,
+    local, masked, bs_t, ts_t, top_out,
 ):
     p, r = plan.panels, plan.rank
-    half = couplings.shape[0] // 2
-    copies = [
-        pltpu.make_async_copy(couplings.at[pl.ds(a, n)], masked.at[pl.ds(a, n)], sems.at[k])
-        for k, (a, n) in enumerate(((0, half), (half, couplings.shape[0] - half)))
-    ]
-    for copy in copies:
-        copy.start()
-    up2[pl.ds(0, r)] = pair_top[pl.ds(r, r)]
-    down2[pl.ds(0, r)] = pair_top[pl.ds(0, r)]
-    for message in (up2, down2):
-        message[pl.ds(r, r)] = top[...]
     top_out[...] = top[...]
     for box in range(ts.shape[0]):
         ts_t[box] = ts[box].T
@@ -151,12 +143,10 @@
         low = jnp.where(lane < r, flags[0, box], flags[1, box])
         high = jnp.where(lane < 3 * r, flags[2, box], flags[3, box])
         chosen = jnp.where(lane < 2 * r, low, high)
-        value = masked[box] * chosen.astype(F32).astype(BF)
+        value = couplings[box] * chosen.astype(F32).astype(BF)
         masked[box] = value
         return value
 
-    for copy in copies:
-        copy.wait()
     for level in range(FULL):
         for box in range(plan.count[level]):
             row = (plan.padded[level] + box) * r
@@ -167,25 +157,19 @@
         mask(box)
 
 
-def near_kernel(plan, chunks, pattern, padded_x, near_blocks, near, edge_near, nb, sems):
+def near_kernel(plan, pattern, padded_x, near_blocks, near, edge_near):
     p = plan.panels
-    per = plan.leaves // chunks
-    copies = [
-        pltpu.make_async_copy(near_blocks.at[pl.ds(c * per, per)], nb.at[pl.ds(c * per, per)], sems.at[c])
-        for c in range(chunks)
-    ]
-    for copy in copies:
-        copy.start()
 
     def side(leaf, slot):
-        block = nb[leaf, slot]
+        block = near_blocks[leaf, slot]
         return jnp.where(pattern[slot, leaf] != 0, block, jnp.zeros_like(block))
 
-    for c in range(chunks):
-        copies[c].wait()
-        for leaf in range(c * per, (c + 1) * per):
-            wide = jnp.concatenate([side(leaf, 0), nb[leaf, 1], side(leaf, 2)], axis=1)
-            near[pl.ds(leaf * p, p)] = dot(wide, padded_x[pl.ds(leaf * p, 3 * p)]).astype(BF)
+    zero = jnp.zeros((p, p), BF)
+    for leaf in range(0, plan.leaves, 2):
+        upper = jnp.concatenate([side(leaf, 0), near_blocks[leaf, 1], side(leaf, 2), zero], axis=1)
+        lower = jnp.concatenate([zero, side(leaf + 1, 0), near_blocks[leaf + 1, 1], side(leaf + 1, 2)], axis=1)
+        both = jnp.concatenate([upper, lower], axis=0)
+        near[pl.ds(leaf * p, 2 * p)] = dot(both, padded_x[pl.ds(leaf * p, 4 * p)]).astype(BF)
     edge_near[0] = side(0, 0)
     edge_near[1] = side(plan.leaves - 1, 2)
 
@@ -279,62 +263,59 @@
     smem = pl.BlockSpec(memory_space=pltpu.SMEM)
     chunks = 8
 
-    padded_x, poles, up, down, top, pair_top, bs, ts = pl.pallas_call(
+    padded_x, poles, up, down, up2, down2, top, bs, ts = pl.pallas_call(
         lambda *refs: upward_kernel(plan, chunks, *refs),
         in_specs=[hbm, hbm, hbm],
-        out_specs=[vmem] * 8,
+        out_specs=[vmem] * 9,
         out_shape=[
             resident(((leaves + 2) * panels, rhs), BF),
             resident((plan.padded_boxes * rank, rhs), BF),
             resident((plan.msg_rows, rhs), BF),
             resident((plan.msg_rows, rhs), BF),
+            resident((2 * rank, rhs), BF),
+            resident((2 * rank, rhs), BF),
             resident((rank, rhs), BF),
-            resident((2 * rank, rhs), BF),
             resident(leaf_basis.shape, BF),
             resident(transfers.shape, BF),
         ],
-        scratch_shapes=[pltpu.SemaphoreType.DMA((chunks + 2,))],
+        scratch_shapes=[pltpu.VMEM((2 * rank, rhs), BF), pltpu.SemaphoreType.DMA((chunks + 2,))],
         compiler_params=pltpu.CompilerParams(vmem_limit_bytes=6 * MIB),
         name="upward",
     )(stay(charges), stay(leaf_basis), stay(transfers))
 
     below, above = shifted(up, 1), shifted(down, -1)
-
-    local, masked, bs_t, ts_t, up2, down2, top = pl.pallas_call(
+    below2, above2 = shifted(up2, 2), shifted(down2, -2)
+
+    local, masked, bs_t, ts_t, top = pl.pallas_call(
         lambda *refs: couple_kernel(plan, *refs),
-        in_specs=[smem, vmem, vmem, vmem, vmem, vmem, hbm],
-        out_specs=[vmem] * 7,
+        in_specs=[smem, vmem, vmem, vmem, vmem, vmem],
+        out_specs=[vmem] * 5,
         out_shape=[
             resident((plan.inner_boxes * rank, rhs), F32),
             resident(couplings.shape, BF),
             resident((leaves, panels, rank), BF),
             resident((transfers.shape[0], panels, rank), BF),
-            resident((2 * rank, rhs), BF),
-            resident((2 * rank, rhs), BF),
             resident((rank, rhs), BF),
         ],
-        scratch_shapes=[pltpu.SemaphoreType.DMA((2,))],
         compiler_params=pltpu.CompilerParams(vmem_limit_bytes=8 * MIB),
         cost_estimate=pl.CostEstimate(flops=6_000_000_000, bytes_accessed=8 * MIB, transcendentals=0),
         name="couple",
-    )(interactions.T, keep(poles), keep(bs), keep(ts), keep(top), keep(pair_top), stay(couplings))
-
-    below2, above2 = shifted(up2, 2), shifted(down2, -2)
+    )(interactions.T, keep(poles), keep(bs), keep(ts), keep(top), keep(couplings))
+
     below3, above3 = shifted(top, 3), shifted(top, -3)
 
     near, edge_near = pl.pallas_call(
-        lambda *refs: near_kernel(plan, 4, *refs),
-        in_specs=[smem, vmem, hbm],
+        lambda *refs: near_kernel(plan, *refs),
+        in_specs=[smem, vmem, vmem],
         out_specs=[vmem] * 2,
         out_shape=[
             resident((leaves * panels, rhs), BF),
             resident((2, panels, panels), BF),
         ],
-        scratch_shapes=[pltpu.VMEM(near_blocks.shape, BF), pltpu.SemaphoreType.DMA((4,))],
-        compiler_params=pltpu.CompilerParams(vmem_limit_bytes=10 * MIB),
+        compiler_params=pltpu.CompilerParams(vmem_limit_bytes=8 * MIB),
         cost_estimate=pl.CostEstimate(flops=6_000_000_000, bytes_accessed=8 * MIB, transcendentals=0),
         name="near",
-    )(near_pattern.T, keep(padded_x), stay(near_blocks))
+    )(near_pattern.T, keep(padded_x), keep(near_blocks))
 
     return pl.pallas_call(
         lambda *refs: final_kernel(plan, *refs),

time: 39.6 us -> 39.7 us (level)
  waiting for transfers between devices: 1.35 us -> 4.69 us
  Pallas kernels: 19.1 us -> 15.8 us
    ppermute x6, waiting for transfers between devices: 1.35 us -> 4.69 us  [shifted(): return lax.ppermute(array, 'slab', pairs)]
    pallas_call x1, Pallas kernels: 4.63 us -> 2.91 us  [body(): pl.pallas_call(lambda *refs: near_kernel(plan, *refs), in_specs=[smem, vm...]
    pallas_call x1, Pallas kernels: 5.16 us -> 3.5 us  [body(): pl.pallas_call(lambda *refs: couple_kernel(plan, *refs), in_specs=[smem,...]
  transfers between devices with their start and end apart: 6 -> 6, of which waited for: 1 -> 1; matrix products, arithmetic and copies ran while one was open for 0% -> 0% of each run, Pallas kernels for 25% -> 16%
where the time goes in v5:
time: 39.7 us; the launch traced here: 39.5 us
  starting transfers between devices  18.8 us (47%)
  Pallas kernels  15.8 us (40%)
  waiting for transfers between devices  4.69 us (12%)
    ppermute x6, starting transfers between devices, shifted(): return lax.ppermute(array, 'slab', pairs)  18.8 us
    pallas_call x1, Pallas kernels, body(): pl.pallas_call(lambda *refs: final_kernel(plan, *refs), in_specs=[vmem] *...  4.89 us
    ppermute x6, waiting for transfers between devices, shifted(): return lax.ppermute(array, 'slab', pairs)  4.69 us
    pallas_call x1, Pallas kernels, body(): pl.pallas_call(lambda *refs: upward_kernel(plan, chunks, *refs), in_specs...  4.55 us
    pallas_call x1, Pallas kernels, body(): pl.pallas_call(lambda *refs: couple_kernel(plan, *refs), in_specs=[smem,...  3.5 us
    pallas_call x1, Pallas kernels, body(): pl.pallas_call(lambda *refs: near_kernel(plan, *refs), in_specs=[smem, vm...  2.91 us
  transfers between devices with their start and end apart: 6, of which 1 were waited for; matrix products, arithmetic and copies ran while one was open for 0% of the time, Pallas kernels for 16%

profile of v5, /device:TPU:16, one launch (start us, length us, event | category | flops | bytes accessed | tf_op | source)
XLA Modules:
  0.0 39.5 jit_solution(13186188793716584818)
XLA Ops:
  0.0 0.0 copy-start.2
  0.0 0.0 copy-start.1
  0.0 4.5 %upward.1 = (bf16[4352,512]{1,0:T(8,128)(2,1)S(1)}, bf16[5376,512]{1,0:T(8,128)(2,1)S(1)}, bf16[784,512]{1,0:T(8,128)(2,1)S(1)}, bf16[784,512]{1,0:T(8,128)(2,1)...) custom-call(bf16[4096,512]{1,0:T(8,128)(2,1)} %refs_0_.1, ...), custom_call_target="tpu_custom_call" | custom-call | tf_op jit(solution)/shard_map/upward/pallas_call | solution.py:266
  4.6 1.9 %collective-permute-start = (bf16[784,512]{1,0:T(8,128)(2,1)S(1)}, bf16[784,512]{1,0:T(8,128)(2,1)S(1)}, u32[]{:S(2)}, u32[]{:S(2)}) collective-permute-start(bf16[784,512]{1,0:T(8,128)(2,1)S(1)} %get-tuple-element.32), channel_id=1, source_target_pairs={{0,1},{1,2},{2,3},{3,4},{4,5},{5,6},{6,7},{7,8},{8,9},{9,10},{10,1... | collective-permute-start | bytes 2408456 | tf_op jit(solution)/shard_map/ppermute | solution.py:255
  6.5 4.5 %collective-permute-start.1 = (bf16[784,512]{1,0:T(8,128)(2,1)S(1)}, bf16[784,512]{1,0:T(8,128)(2,1)S(1)}, u32[]{:S(2)}, u32[]{:S(2)}) collective-permute-start(bf16[784,512]{1,0:T(8,128)(2,1)S(1)} %get-tuple-element.33), channel_id=1, source_target_pairs={{1,0},{2,1},{3,2},{4,3},{5,4},{6,5},{7,6},{8,7},{9,8},{10,9},{11,1... | collective-permute-start | bytes 2408456 | tf_op jit(solution)/shard_map/ppermute | solution.py:255
  11.0 0.0 copy-done.2
  11.0 0.0 copy-done.1
  11.1 0.0 copy-start
  11.1 0.0 copy-start.3
  11.1 3.5 %couple.1 = (f32[3840,512]{1,0:T(8,128)S(1)}, bf16[63,64,256]{2,1,0:T(8,128)(2,1)S(1)}, bf16[32,128,64]{2,1,0:T(8,128)(2,1)S(1)}, bf16[31,128,64]{2,1,0:T(8,128)(2,1)S(1)}, bf16[64,512]{1,0:T(8,128)(2,1)S(1)}) custom-call(s32[4,63]{1,0:T(4,128)S(1)} %bitcast.2, bf16[5376,512]{1,0:T(8,128)(2,1)S(1)} %get-tuple-element.23.refs_1_, ...), custom_call_target="tpu_custom_call" | custom-call | flops 6000000000 | bytes 8388608 | tf_op jit(solution)/shard_map/couple/pallas_call | solution.py:289
  14.6 1.9 %collective-permute-start.5 = (bf16[64,512]{1,0:T(8,128)(2,1)S(1)}, bf16[64,512]{1,0:T(8,128)(2,1)S(1)}, u32[]{:S(2)}, u32[]{:S(2)}) collective-permute-start(bf16[64,512]{1,0:T(8,128)(2,1)S(1)} %get-tuple-element.36), channel_id=1, source_target_pairs={{3,0},{4,1},{5,2},{6,3},{7,4},{8,5},{9,6},{10,7},{11,8},{12,9},{13... | collective-permute-start | bytes 196616 | tf_op jit(solution)/shard_map/ppermute | solution.py:255
  16.5 3.6 %collective-permute-start.4 = (bf16[64,512]{1,0:T(8,128)(2,1)S(1)}, bf16[64,512]{1,0:T(8,128)(2,1)S(1)}, u32[]{:S(2)}, u32[]{:S(2)}) collective-permute-start(bf16[64,512]{1,0:T(8,128)(2,1)S(1)} %get-tuple-element.36), channel_id=1, source_target_pairs={{0,3},{1,4},{2,5},{3,6},{4,7},{5,8},{6,9},{7,10},{8,11},{9,12},{10... | collective-permute-start | bytes 196616 | tf_op jit(solution)/shard_map/ppermute | solution.py:255
  20.2 3.4 %collective-permute-start.2 = (bf16[128,512]{1,0:T(8,128)(2,1)S(1)}, bf16[128,512]{1,0:T(8,128)(2,1)S(1)}, u32[]{:S(2)}, u32[]{:S(2)}) collective-permute-start(bf16[128,512]{1,0:T(8,128)(2,1)S(1)} %get-tuple-element.34), channel_id=1, source_target_pairs={{0,2},{1,3},{2,4},{3,5},{4,6},{5,7},{6,8},{7,9},{8,10},{9,11},{10,... | collective-permute-start | bytes 393224 | tf_op jit(solution)/shard_map/ppermute | solution.py:255
  23.6 0.0 collective-permute-done.5.refs_11_
  23.6 3.3 %collective-permute-start.3 = (bf16[128,512]{1,0:T(8,128)(2,1)S(1)}, bf16[128,512]{1,0:T(8,128)(2,1)S(1)}, u32[]{:S(2)}, u32[]{:S(2)}) collective-permute-start(bf16[128,512]{1,0:T(8,128)(2,1)S(1)} %get-tuple-element.35), channel_id=1, source_target_pairs={{2,0},{3,1},{4,2},{5,3},{6,4},{7,5},{8,6},{9,7},{10,8},{11,9},{12,... | collective-permute-start | bytes 393224 | tf_op jit(solution)/shard_map/ppermute | solution.py:255
  26.9 0.0 copy-done
  26.9 0.0 copy-done.3
  27.0 2.9 %near.1 = (bf16[4096,512]{1,0:T(8,128)(2,1)S(1)}, bf16[2,128,128]{2,1,0:T(8,128)(2,1)S(1)}) custom-call(s32[3,32]{1,0:T(4,128)S(1)} %bitcast.3, bf16[4352,512]{1,0:T(8,128)(2,1)S(1)} %get-tuple-element.21.refs_1_, bf16[32,3,128,128]{3,2,1,0:T(8,128)(2,1)S(1)} %copy-done), custom_call_target="tpu_custom_call" | custom-call | flops 6000000000 | bytes 8388608 | tf_op jit(solution)/shard_map/near/pallas_call | solution.py:307
  29.9 0.0 collective-permute-done.4.refs_10_
  29.9 0.0 collective-permute-done.2.refs_8_
  29.9 4.7 %collective-permute-done.3.refs_9_ = bf16[128,512]{1,0:T(8,128)(2,1)S(1)} collective-permute-done((bf16[128,512]{1,0:T(8,128)(2,1)S(1)}, bf16[128,512]{1,0:T(8,128)(2,1)S(1)}, u32[]{:S(2)}, u32[]{:S(2)}) %collective-permute-start.3) | collective-permute-done | bytes 131104 | tf_op jit(solution)/shard_map/ppermute | solution.py:255
  34.6 0.0 collective-permute-done.refs_6_
  34.6 0.0 collective-permute-done.1.refs_7_
  34.6 4.9 %final.1 = bf16[4096,512]{1,0:T(8,128)(2,1)} custom-call(bf16[4096,512]{1,0:T(8,128)(2,1)S(1)} %get-tuple-element.22.refs_0_, f32[3840,512]{1,0:T(8,128)S(1)} %get-tuple-element.27.refs_1_, bf16[63,64,256]{2,1,0:T(8,128)(2,1)S(1)} %get-tuple-element.28.refs_2_, bf16[2,128,128]{2,1,0:T(8,128)(2,1)S(1)} %get-tuple-element.29.refs_3_, ...), custom_call_target="tpu_custom_call" | custom-call | tf_op jit(solution)/shard_map/final/pallas_call | solution.py:320
Async XLA Ops:
  0.0 11.0 %copy-start.2 = (s32[63,4]{0,1:T(4,128)S(1)}, s32[63,4]{0,1:T(4,128)}, u32[]{:S(2)}) copy-start(s32[63,4]{0,1:T(4,128)} %param.13) | copy-start | bytes 3028
  0.0 11.0 %copy-start.1 = (bf16[63,64,256]{2,1,0:T(8,128)(2,1)S(1)}, bf16[63,64,256]{2,1,0:T(8,128)(2,1)}, u32[]{:S(2)}) copy-start(bf16[63,64,256]{2,1,0:T(8,128)(2,1)} %refs_5_.1) | copy-start | bytes 6193156
  4.6 30.0 %collective-permute-start = (bf16[784,512]{1,0:T(8,128)(2,1)S(1)}, bf16[784,512]{1,0:T(8,128)(2,1)S(1)}, u32[]{:S(2)}, u32[]{:S(2)}) collective-permute-start(bf16[784,512]{1,0:T(8,128)(2,1)S(1)} %get-tuple-element.32), channel_id=1, source_target_pairs={{0,1},{1,2},{2,3},{3,4},{4,5},{5,6},{6,7},{7,8},{8,9},{9,10},{10,1... | collective-permute-start | bytes 2408456 | tf_op jit(solution)/shard_map/ppermute | solution.py:255
  6.5 28.1 %collective-permute-start.1 = (bf16[784,512]{1,0:T(8,128)(2,1)S(1)}, bf16[784,512]{1,0:T(8,128)(2,1)S(1)}, u32[]{:S(2)}, u32[]{:S(2)}) collective-permute-start(bf16[784,512]{1,0:T(8,128)(2,1)S(1)} %get-tuple-element.33), channel_id=1, source_target_pairs={{1,0},{2,1},{3,2},{4,3},{5,4},{6,5},{7,6},{8,7},{9,8},{10,9},{11,1... | collective-permute-start | bytes 2408456 | tf_op jit(solution)/shard_map/ppermute | solution.py:255
  11.1 15.9 %copy-start = (bf16[32,3,128,128]{3,2,1,0:T(8,128)(2,1)S(1)}, bf16[32,3,128,128]{3,2,1,0:T(8,128)(2,1)}, u32[]{:S(2)}) copy-start(bf16[32,3,128,128]{3,2,1,0:T(8,128)(2,1)} %refs_2_.3) | copy-start | bytes 9437188
  11.1 15.9 %copy-start.3 = (s32[32,3]{0,1:T(4,128)S(1)}, s32[32,3]{0,1:T(4,128)}, u32[]{:S(2)}) copy-start(s32[32,3]{0,1:T(4,128)} %param.9) | copy-start | bytes 1156
  14.6 9.0 %collective-permute-start.5 = (bf16[64,512]{1,0:T(8,128)(2,1)S(1)}, bf16[64,512]{1,0:T(8,128)(2,1)S(1)}, u32[]{:S(2)}, u32[]{:S(2)}) collective-permute-start(bf16[64,512]{1,0:T(8,128)(2,1)S(1)} %get-tuple-element.36), channel_id=1, source_target_pairs={{3,0},{4,1},{5,2},{6,3},{7,4},{8,5},{9,6},{10,7},{11,8},{12,9},{13... | collective-permute-start | bytes 196616 | tf_op jit(solution)/shard_map/ppermute | solution.py:255
  16.5 13.4 %collective-permute-start.4 = (bf16[64,512]{1,0:T(8,128)(2,1)S(1)}, bf16[64,512]{1,0:T(8,128)(2,1)S(1)}, u32[]{:S(2)}, u32[]{:S(2)}) collective-permute-start(bf16[64,512]{1,0:T(8,128)(2,1)S(1)} %get-tuple-element.36), channel_id=1, source_target_pairs={{0,3},{1,4},{2,5},{3,6},{4,7},{5,8},{6,9},{7,10},{8,11},{9,12},{10... | collective-permute-start | bytes 196616 | tf_op jit(solution)/shard_map/ppermute | solution.py:255
  20.2 9.7 %collective-permute-start.2 = (bf16[128,512]{1,0:T(8,128)(2,1)S(1)}, bf16[128,512]{1,0:T(8,128)(2,1)S(1)}, u32[]{:S(2)}, u32[]{:S(2)}) collective-permute-start(bf16[128,512]{1,0:T(8,128)(2,1)S(1)} %get-tuple-element.34), channel_id=1, source_target_pairs={{0,2},{1,3},{2,4},{3,5},{4,6},{5,7},{6,8},{7,9},{8,10},{9,11},{10,... | collective-permute-start | bytes 393224 | tf_op jit(solution)/shard_map/ppermute | solution.py:255
  23.6 11.0 %collective-permute-start.3 = (bf16[128,512]{1,0:T(8,128)(2,1)S(1)}, bf16[128,512]{1,0:T(8,128)(2,1)S(1)}, u32[]{:S(2)}, u32[]{:S(2)}) collective-permute-start(bf16[128,512]{1,0:T(8,128)(2,1)S(1)} %get-tuple-element.35), channel_id=1, source_target_pairs={{2,0},{3,1},{4,2},{5,3},{6,4},{7,5},{8,6},{9,7},{10,8},{11,9},{12,... | collective-permute-start | bytes 393224 | tf_op jit(solution)/shard_map/ppermute | solution.py:255

commit v6 on v5

--- a/solution.py
+++ b/solution.py
@@ -128,11 +128,10 @@
 
 
 def couple_kernel(
-    plan, flags, poles, bs, ts, top, couplings,
-    local, masked, bs_t, ts_t, top_out,
+    plan, flags, poles, bs, ts, couplings,
+    local, masked, bs_t, ts_t,
 ):
     p, r = plan.panels, plan.rank
-    top_out[...] = top[...]
     for box in range(ts.shape[0]):
         ts_t[box] = ts[box].T
     for leaf in range(bs.shape[0]):
@@ -175,7 +174,7 @@
 
 
 def final_kernel(
-    plan, near, local, masked, edge_near, bs_t, ts_t, below, above, below2, above2, below3, above3,
+    plan, near, local, masked, edge_near, bs_t, ts_t, below3, above3, below2, above2, below, above,
     out, loc, stage, sems,
 ):
     p, r, n = plan.panels, plan.rank, plan.leaves
@@ -285,24 +284,23 @@
 
     below, above = shifted(up, 1), shifted(down, -1)
     below2, above2 = shifted(up2, 2), shifted(down2, -2)
-
-    local, masked, bs_t, ts_t, top = pl.pallas_call(
+    below3, above3 = shifted(top, 3), shifted(top, -3)
+
+    local, masked, bs_t, ts_t = pl.pallas_call(
         lambda *refs: couple_kernel(plan, *refs),
-        in_specs=[smem, vmem, vmem, vmem, vmem, vmem],
-        out_specs=[vmem] * 5,
+        in_specs=[smem, vmem, vmem, vmem, vmem],
+        out_specs=[vmem] * 4,
         out_shape=[
             resident((plan.inner_boxes * rank, rhs), F32),
             resident(couplings.shape, BF),
             resident((leaves, panels, rank), BF),
             resident((transfers.shape[0], panels, rank), BF),
-            resident((rank, rhs), BF),
         ],
         compiler_params=pltpu.CompilerParams(vmem_limit_bytes=8 * MIB),
         cost_estimate=pl.CostEstimate(flops=6_000_000_000, bytes_accessed=8 * MIB, transcendentals=0),
         name="couple",
-    )(interactions.T, keep(poles), keep(bs), keep(ts), keep(top), keep(couplings))
-
-    below3, above3 = shifted(top, 3), shifted(top, -3)
+    )(interactions.T, keep(poles), keep(bs), keep(ts), keep(couplings))
+
 
     near, edge_near = pl.pallas_call(
         lambda *refs: near_kernel(plan, *refs),
@@ -313,7 +311,7 @@
             resident((2, panels, panels), BF),
         ],
         compiler_params=pltpu.CompilerParams(vmem_limit_bytes=8 * MIB),
-        cost_estimate=pl.CostEstimate(flops=6_000_000_000, bytes_accessed=8 * MIB, transcendentals=0),
+        cost_estimate=pl.CostEstimate(flops=100_000_000, bytes_accessed=MIB // 4, transcendentals=0),
         name="near",
     )(near_pattern.T, keep(padded_x), keep(near_blocks))
 
@@ -331,7 +329,7 @@
         name="final",
     )(
         keep(near), keep(local), keep(masked), keep(edge_near), keep(bs_t), keep(ts_t),
-        keep(below), keep(above), keep(below2), keep(above2), keep(below3), keep(above3),
+        keep(below3), keep(above3), keep(below2), keep(above2), keep(below), keep(above),
     )
 
 

time: 39.7 us -> 39.9 us (level)
  starting transfers between devices: 18.8 us -> 16.4 us
  waiting for transfers between devices: 4.69 us -> 7.07 us
    ppermute x6, waiting for transfers between devices: 4.69 us -> 7.07 us  [shifted(): return lax.ppermute(array, 'slab', pairs)]
    ppermute x6, starting transfers between devices: 18.8 us -> 16.4 us  [shifted(): return lax.ppermute(array, 'slab', pairs)]
  transfers between devices with their start and end apart: 6 -> 6, of which waited for: 1 -> 2; matrix products, arithmetic and copies ran while one was open for 0% -> 0% of each run, Pallas kernels for 16% -> 16%
where the time goes in v6:
time: 39.9 us; the launch traced here: 39.5 us
  starting transfers between devices  16.4 us (41%)
  Pallas kernels  15.8 us (40%)
  waiting for transfers between devices  7.07 us (18%)
    ppermute x6, starting transfers between devices, shifted(): return lax.ppermute(array, 'slab', pairs)  16.4 us
    ppermute x6, waiting for transfers between devices, shifted(): return lax.ppermute(array, 'slab', pairs)  7.07 us
    pallas_call x1, Pallas kernels, body(): pl.pallas_call(lambda *refs: final_kernel(plan, *refs), in_specs=[vmem] *...  4.88 us
    pallas_call x1, Pallas kernels, body(): pl.pallas_call(lambda *refs: upward_kernel(plan, chunks, *refs), in_specs...  4.55 us
    pallas_call x1, Pallas kernels, body(): pl.pallas_call(lambda *refs: couple_kernel(plan, *refs), in_specs=[smem,...  3.45 us
    pallas_call x1, Pallas kernels, body(): pl.pallas_call(lambda *refs: near_kernel(plan, *refs), in_specs=[smem, vm...  2.91 us
  transfers between devices with their start and end apart: 6, of which 2 were waited for; matrix products, arithmetic and copies ran while one was open for 0% of the time, Pallas kernels for 16%

profile of v6, /device:TPU:16, one launch (start us, length us, event | category | flops | bytes accessed | tf_op | source)
XLA Modules:
  0.0 39.5 jit_solution(1467294864458851745)
XLA Ops:
  0.0 0.0 copy-start.3
  0.0 0.0 copy-start.2
  0.0 4.5 %upward.1 = (bf16[4352,512]{1,0:T(8,128)(2,1)S(1)}, bf16[5376,512]{1,0:T(8,128)(2,1)S(1)}, bf16[784,512]{1,0:T(8,128)(2,1)S(1)}, bf16[784,512]{1,0:T(8,128)(2,1)...) custom-call(bf16[4096,512]{1,0:T(8,128)(2,1)} %refs_0_.1, ...), custom_call_target="tpu_custom_call" | custom-call | tf_op jit(solution)/shard_map/upward/pallas_call | solution.py:265
  4.6 1.9 %collective-permute-start.4 = (bf16[784,512]{1,0:T(8,128)(2,1)S(1)}, bf16[784,512]{1,0:T(8,128)(2,1)S(1)}, u32[]{:S(2)}, u32[]{:S(2)}) collective-permute-start(bf16[784,512]{1,0:T(8,128)(2,1)S(1)} %get-tuple-element.33), channel_id=1, source_target_pairs={{0,1},{1,2},{2,3},{3,4},{4,5},{5,6},{6,7},{7,8},{8,9},{9,10},{10,1... | collective-permute-start | bytes 2408456 | tf_op jit(solution)/shard_map/ppermute | solution.py:254
  6.5 4.5 %collective-permute-start.5 = (bf16[784,512]{1,0:T(8,128)(2,1)S(1)}, bf16[784,512]{1,0:T(8,128)(2,1)S(1)}, u32[]{:S(2)}, u32[]{:S(2)}) collective-permute-start(bf16[784,512]{1,0:T(8,128)(2,1)S(1)} %get-tuple-element.34), channel_id=1, source_target_pairs={{1,0},{2,1},{3,2},{4,3},{5,4},{6,5},{7,6},{8,7},{9,8},{10,9},{11,1... | collective-permute-start | bytes 2408456 | tf_op jit(solution)/shard_map/ppermute | solution.py:254
  11.0 2.0 %collective-permute-start = (bf16[64,512]{1,0:T(8,128)(2,1)S(1)}, bf16[64,512]{1,0:T(8,128)(2,1)S(1)}, u32[]{:S(2)}, u32[]{:S(2)}) collective-permute-start(bf16[64,512]{1,0:T(8,128)(2,1)S(1)} %get-tuple-element.30), channel_id=1, source_target_pairs={{0,3},{1,4},{2,5},{3,6},{4,7},{5,8},{6,9},{7,10},{8,11},{9,12},{10... | collective-permute-start | bytes 196616 | tf_op jit(solution)/shard_map/ppermute | solution.py:254
  13.1 3.5 %collective-permute-start.1 = (bf16[64,512]{1,0:T(8,128)(2,1)S(1)}, bf16[64,512]{1,0:T(8,128)(2,1)S(1)}, u32[]{:S(2)}, u32[]{:S(2)}) collective-permute-start(bf16[64,512]{1,0:T(8,128)(2,1)S(1)} %get-tuple-element.30), channel_id=1, source_target_pairs={{3,0},{4,1},{5,2},{6,3},{7,4},{8,5},{9,6},{10,7},{11,8},{12,9},{13... | collective-permute-start | bytes 196616 | tf_op jit(solution)/shard_map/ppermute | solution.py:254
  16.6 2.5 %collective-permute-start.2 = (bf16[128,512]{1,0:T(8,128)(2,1)S(1)}, bf16[128,512]{1,0:T(8,128)(2,1)S(1)}, u32[]{:S(2)}, u32[]{:S(2)}) collective-permute-start(bf16[128,512]{1,0:T(8,128)(2,1)S(1)} %get-tuple-element.31), channel_id=1, source_target_pairs={{0,2},{1,3},{2,4},{3,5},{4,6},{5,7},{6,8},{7,9},{8,10},{9,11},{10,... | collective-permute-start | bytes 393224 | tf_op jit(solution)/shard_map/ppermute | solution.py:254
  19.1 4.8 %collective-permute-done.refs_6_ = bf16[64,512]{1,0:T(8,128)(2,1)S(1)} collective-permute-done((bf16[64,512]{1,0:T(8,128)(2,1)S(1)}, bf16[64,512]{1,0:T(8,128)(2,1)S(1)}, u32[]{:S(2)}, u32[]{:S(2)}) %collective-permute-start) | collective-permute-done | bytes 65568 | tf_op jit(solution)/shard_map/ppermute | solution.py:254
  24.0 1.9 %collective-permute-start.3 = (bf16[128,512]{1,0:T(8,128)(2,1)S(1)}, bf16[128,512]{1,0:T(8,128)(2,1)S(1)}, u32[]{:S(2)}, u32[]{:S(2)}) collective-permute-start(bf16[128,512]{1,0:T(8,128)(2,1)S(1)} %get-tuple-element.32), channel_id=1, source_target_pairs={{2,0},{3,1},{4,2},{5,3},{6,4},{7,5},{8,6},{9,7},{10,8},{11,9},{12,... | collective-permute-start | bytes 393224 | tf_op jit(solution)/shard_map/ppermute | solution.py:254
  25.9 0.0 copy-done.3
  25.9 0.0 copy-done.2
  25.9 0.0 copy-start
  25.9 0.0 copy-start.1
  25.9 3.4 %couple.1 = (f32[3840,512]{1,0:T(8,128)S(1)}, bf16[63,64,256]{2,1,0:T(8,128)(2,1)S(1)}, bf16[32,128,64]{2,1,0:T(8,128)(2,1)S(1)}, bf16[31,128,64]{2,1,0:T(8,128)(2,1)S(1)}) custom-call(s32[4,63]{1,0:T(4,128)S(1)} %bitcast.3, bf16[5376,512]{1,0:T(8,128)(2,1)S(1)} %get-tuple-element.22.refs_1_, bf16[32,64,128]{2,1,0:T(8,128)(2,1)S(1)} %get-tuple-element.23.refs_2_, ...), custom_call_target="tpu_custom_call" | custom-call | flops 6000000000 | bytes 8388608 | tf_op jit(solution)/shard_map/couple/pallas_call | solution.py:289
  29.4 0.0 copy-done
  29.4 0.0 copy-done.1
  29.4 2.9 %near.1 = (bf16[4096,512]{1,0:T(8,128)(2,1)S(1)}, bf16[2,128,128]{2,1,0:T(8,128)(2,1)S(1)}) custom-call(s32[3,32]{1,0:T(4,128)S(1)} %bitcast.2, bf16[4352,512]{1,0:T(8,128)(2,1)S(1)} %get-tuple-element.20.refs_1_, bf16[32,3,128,128]{3,2,1,0:T(8,128)(2,1)S(1)} %copy-done), custom_call_target="tpu_custom_call" | custom-call | flops 100000000 | bytes 262144 | tf_op jit(solution)/shard_map/near/pallas_call | solution.py:305
  32.3 0.0 collective-permute-done.1.refs_7_
  32.3 0.0 collective-permute-done.2.refs_8_
  32.4 2.2 %collective-permute-done.3.refs_9_ = bf16[128,512]{1,0:T(8,128)(2,1)S(1)} collective-permute-done((bf16[128,512]{1,0:T(8,128)(2,1)S(1)}, bf16[128,512]{1,0:T(8,128)(2,1)S(1)}, u32[]{:S(2)}, u32[]{:S(2)}) %collective-permute-start.3) | collective-permute-done | bytes 131104 | tf_op jit(solution)/shard_map/ppermute | solution.py:254
  34.6 0.0 collective-permute-done.4.refs_10_
  34.6 0.0 collective-permute-done.5.refs_11_
  34.6 4.9 %final.1 = bf16[4096,512]{1,0:T(8,128)(2,1)} custom-call(bf16[4096,512]{1,0:T(8,128)(2,1)S(1)} %get-tuple-element.21.refs_0_, f32[3840,512]{1,0:T(8,128)S(1)} %get-tuple-element.25.refs_1_, bf16[63,64,256]{2,1,0:T(8,128)(2,1)S(1)} %get-tuple-element.26.refs_2_, bf16[2,128,128]{2,1,0:T(8,128)(2,1)S(1)} %get-tuple-element.27.refs_3_, ...), custom_call_target="tpu_custom_call" | custom-call | tf_op jit(solution)/shard_map/final/pallas_call | solution.py:318
Async XLA Ops:
  0.0 25.9 %copy-start.3 = (s32[63,4]{0,1:T(4,128)S(1)}, s32[63,4]{0,1:T(4,128)}, u32[]{:S(2)}) copy-start(s32[63,4]{0,1:T(4,128)} %param.13) | copy-start | bytes 3028
  0.0 25.9 %copy-start.2 = (bf16[63,64,256]{2,1,0:T(8,128)(2,1)S(1)}, bf16[63,64,256]{2,1,0:T(8,128)(2,1)}, u32[]{:S(2)}) copy-start(bf16[63,64,256]{2,1,0:T(8,128)(2,1)} %refs_4_.1) | copy-start | bytes 6193156
  4.6 30.0 %collective-permute-start.4 = (bf16[784,512]{1,0:T(8,128)(2,1)S(1)}, bf16[784,512]{1,0:T(8,128)(2,1)S(1)}, u32[]{:S(2)}, u32[]{:S(2)}) collective-permute-start(bf16[784,512]{1,0:T(8,128)(2,1)S(1)} %get-tuple-element.33), channel_id=1, source_target_pairs={{0,1},{1,2},{2,3},{3,4},{4,5},{5,6},{6,7},{7,8},{8,9},{9,10},{10,1... | collective-permute-start | bytes 2408456 | tf_op jit(solution)/shard_map/ppermute | solution.py:254
  6.5 28.1 %collective-permute-start.5 = (bf16[784,512]{1,0:T(8,128)(2,1)S(1)}, bf16[784,512]{1,0:T(8,128)(2,1)S(1)}, u32[]{:S(2)}, u32[]{:S(2)}) collective-permute-start(bf16[784,512]{1,0:T(8,128)(2,1)S(1)} %get-tuple-element.34), channel_id=1, source_target_pairs={{1,0},{2,1},{3,2},{4,3},{5,4},{6,5},{7,6},{8,7},{9,8},{10,9},{11,1... | collective-permute-start | bytes 2408456 | tf_op jit(solution)/shard_map/ppermute | solution.py:254
  11.0 12.9 %collective-permute-start = (bf16[64,512]{1,0:T(8,128)(2,1)S(1)}, bf16[64,512]{1,0:T(8,128)(2,1)S(1)}, u32[]{:S(2)}, u32[]{:S(2)}) collective-permute-start(bf16[64,512]{1,0:T(8,128)(2,1)S(1)} %get-tuple-element.30), channel_id=1, source_target_pairs={{0,3},{1,4},{2,5},{3,6},{4,7},{5,8},{6,9},{7,10},{8,11},{9,12},{10... | collective-permute-start | bytes 196616 | tf_op jit(solution)/shard_map/ppermute | solution.py:254
  13.1 19.3 %collective-permute-start.1 = (bf16[64,512]{1,0:T(8,128)(2,1)S(1)}, bf16[64,512]{1,0:T(8,128)(2,1)S(1)}, u32[]{:S(2)}, u32[]{:S(2)}) collective-permute-start(bf16[64,512]{1,0:T(8,128)(2,1)S(1)} %get-tuple-element.30), channel_id=1, source_target_pairs={{3,0},{4,1},{5,2},{6,3},{7,4},{8,5},{9,6},{10,7},{11,8},{12,9},{13... | collective-permute-start | bytes 196616 | tf_op jit(solution)/shard_map/ppermute | solution.py:254
  16.6 15.7 %collective-permute-start.2 = (bf16[128,512]{1,0:T(8,128)(2,1)S(1)}, bf16[128,512]{1,0:T(8,128)(2,1)S(1)}, u32[]{:S(2)}, u32[]{:S(2)}) collective-permute-start(bf16[128,512]{1,0:T(8,128)(2,1)S(1)} %get-tuple-element.31), channel_id=1, source_target_pairs={{0,2},{1,3},{2,4},{3,5},{4,6},{5,7},{6,8},{7,9},{8,10},{9,11},{10,... | collective-permute-start | bytes 393224 | tf_op jit(solution)/shard_map/ppermute | solution.py:254
  24.0 10.6 %collective-permute-start.3 = (bf16[128,512]{1,0:T(8,128)(2,1)S(1)}, bf16[128,512]{1,0:T(8,128)(2,1)S(1)}, u32[]{:S(2)}, u32[]{:S(2)}) collective-permute-start(bf16[128,512]{1,0:T(8,128)(2,1)S(1)} %get-tuple-element.32), channel_id=1, source_target_pairs={{2,0},{3,1},{4,2},{5,3},{6,4},{7,5},{8,6},{9,7},{10,8},{11,9},{12,... | collective-permute-start | bytes 393224 | tf_op jit(solution)/shard_map/ppermute | solution.py:254
  25.9 3.5 %copy-start = (bf16[32,3,128,128]{3,2,1,0:T(8,128)(2,1)S(1)}, bf16[32,3,128,128]{3,2,1,0:T(8,128)(2,1)}, u32[]{:S(2)}) copy-start(bf16[32,3,128,128]{3,2,1,0:T(8,128)(2,1)} %refs_2_.3) | copy-start | bytes 9437188
  25.9 3.5 %copy-start.1 = (s32[32,3]{0,1:T(4,128)S(1)}, s32[32,3]{0,1:T(4,128)}, u32[]{:S(2)}) copy-start(s32[32,3]{0,1:T(4,128)} %param.9) | copy-start | bytes 1156

commit v7 on v5

--- a/solution.py
+++ b/solution.py
@@ -45,7 +45,7 @@
         self.msg_rows = self.msg_last + self.part_rows
 
 
-def upward_kernel(plan, chunks, charges, basis, transfers, padded_x, poles, up, down, up2, down2, top, bs, ts, pair4, sems):
+def upward_kernel(plan, chunks, charges, basis, transfers, padded_x, poles, up, down, pair4, bs, ts, sems):
     p, r = plan.panels, plan.rank
     per = plan.leaves // chunks
     copies = []
@@ -81,39 +81,31 @@
                 down[pl.ds(plan.msg_pole[level] + (box - 1) * r, r)] = value
         elif level == FULL:
             (up if box == 0 else down)[pl.ds(plan.msg_top, r)] = value
-            (down2 if box == 0 else up2)[pl.ds(0, r)] = value
             pair4[pl.ds(box * r, r)] = value
-        else:
-            for message in (up2, down2):
-                message[pl.ds(r, r)] = value
-            top[...] = value
 
     def climb(level, box):
-        if level <= FULL:
-            pair = poles[pl.ds((plan.padded[level - 1] + 3 + 2 * box) * r, 2 * r)]
-        else:
-            pair = pair4[...]
+        pair = poles[pl.ds((plan.padded[level - 1] + 3 + 2 * box) * r, 2 * r)]
         keep(level, box, dot(ts[plan.trans[level] + box], pair).astype(BF))
 
-    done = [0] * LEVELS
+    done = [0] * (FULL + 1)
 
     def climb_ready():
         ready = list(done)
-        for level in range(1, LEVELS):
+        for level in range(1, FULL + 1):
             while 2 * done[level] + 2 <= ready[level - 1]:
                 climb(level, done[level])
                 done[level] += 1
 
     for c in range(chunks):
         copies[c].wait()
-        if c == 0:
+        if c == 1:
             trans_copy.wait()
         climb_ready()
         for leaf in range(c * per, (c + 1) * per):
             x = padded_x[pl.ds(p * (leaf + 1), p)]
             keep(0, leaf, dot(bs[leaf], x).astype(BF))
         done[0] = (c + 1) * per
-    while done[LEVELS - 1] < plan.count[LEVELS - 1]:
+    while done[FULL] < plan.count[FULL]:
         climb_ready()
     for message, leaf, last in ((up, plan.leaves - 1, True), (down, 0, False)):
         message[pl.ds(0, p)] = padded_x[pl.ds(p * (leaf + 1), p)]
@@ -128,11 +120,16 @@
 
 
 def couple_kernel(
-    plan, flags, poles, bs, ts, top, couplings,
-    local, masked, bs_t, ts_t, top_out,
+    plan, flags, poles, bs, ts, pair4, couplings,
+    local, masked, bs_t, ts_t, up2, down2, top,
 ):
     p, r = plan.panels, plan.rank
-    top_out[...] = top[...]
+    summit = dot(ts[plan.trans[LEVELS - 1]], pair4[...]).astype(BF)
+    up2[pl.ds(0, r)] = pair4[pl.ds(r, r)]
+    down2[pl.ds(0, r)] = pair4[pl.ds(0, r)]
+    for message in (up2, down2):
+        message[pl.ds(r, r)] = summit
+    top[...] = summit
     for box in range(ts.shape[0]):
         ts_t[box] = ts[box].T
     for leaf in range(bs.shape[0]):
@@ -222,29 +219,41 @@
             gain = value if gain is None else gain + value
         return gain
 
-    for level in range(FULL, 0, -1):
+    def descend(level, box):
+        push = dot(ts_t[plan.trans[level] + box], loc[place(level, box)])
+        for k in range(2):
+            child = 2 * box + k
+            value = local[place(level - 1, child)] + push[k * r : (k + 1) * r]
+            gain = rim_gain(level - 1, child)
+            loc[place(level - 1, child)] = (value if gain is None else value + gain).astype(BF)
+
+    for level in range(FULL, 1, -1):
         for box in range(plan.count[level]):
-            push = dot(ts_t[plan.trans[level] + box], loc[place(level, box)])
-            for k in range(2):
-                child = 2 * box + k
-                value = local[place(level - 1, child)] + push[k * r : (k + 1) * r]
-                gain = rim_gain(level - 1, child)
-                loc[place(level - 1, child)] = (value if gain is None else value + gain).astype(BF)
+            descend(level, box)
 
     writes = []
-    per = n // sems.shape[0]
-    for leaf in range(n):
-        total = near[pl.ds(leaf * p, p)].astype(F32) + dot(bs_t[leaf], loc[place(0, leaf)])
-        if leaf == 0:
-            total = total + dot(edge_near[0], below[pl.ds(0, p)])
-        if leaf == n - 1:
-            total = total + dot(edge_near[1], above[pl.ds(0, p)])
-        stage[pl.ds(leaf * p, p)] = total.astype(BF)
-        if (leaf + 1) % per == 0:
-            rows = pl.ds((leaf + 1 - per) * p, per * p)
-            copy = pltpu.make_async_copy(stage.at[rows], out.at[rows], sems.at[leaf // per])
-            copy.start()
-            writes.append(copy)
+    groups = sems.shape[0]
+    per = n // groups
+
+    def descend_group(group):
+        for box in range(group * per // 2, (group + 1) * per // 2):
+            descend(1, box)
+
+    descend_group(0)
+    for group in range(groups):
+        if group + 1 < groups:
+            descend_group(group + 1)
+        for leaf in range(group * per, (group + 1) * per):
+            total = near[pl.ds(leaf * p, p)].astype(F32) + dot(bs_t[leaf], loc[place(0, leaf)])
+            if leaf == 0:
+                total = total + dot(edge_near[0], below[pl.ds(0, p)])
+            if leaf == n - 1:
+                total = total + dot(edge_near[1], above[pl.ds(0, p)])
+            stage[pl.ds(leaf * p, p)] = total.astype(BF)
+        rows = pl.ds(group * per * p, per * p)
+        copy = pltpu.make_async_copy(stage.at[rows], out.at[rows], sems.at[group])
+        copy.start()
+        writes.append(copy)
     for copy in writes:
         copy.wait()
 
@@ -263,45 +272,45 @@
     smem = pl.BlockSpec(memory_space=pltpu.SMEM)
     chunks = 8
 
-    padded_x, poles, up, down, up2, down2, top, bs, ts = pl.pallas_call(
+    padded_x, poles, up, down, pair4, bs, ts = pl.pallas_call(
         lambda *refs: upward_kernel(plan, chunks, *refs),
         in_specs=[hbm, hbm, hbm],
-        out_specs=[vmem] * 9,
+        out_specs=[vmem] * 7,
         out_shape=[
             resident(((leaves + 2) * panels, rhs), BF),
             resident((plan.padded_boxes * rank, rhs), BF),
             resident((plan.msg_rows, rhs), BF),
             resident((plan.msg_rows, rhs), BF),
             resident((2 * rank, rhs), BF),
-            resident((2 * rank, rhs), BF),
-            resident((rank, rhs), BF),
             resident(leaf_basis.shape, BF),
             resident(transfers.shape, BF),
         ],
-        scratch_shapes=[pltpu.VMEM((2 * rank, rhs), BF), pltpu.SemaphoreType.DMA((chunks + 2,))],
+        scratch_shapes=[pltpu.SemaphoreType.DMA((chunks + 2,))],
         compiler_params=pltpu.CompilerParams(vmem_limit_bytes=6 * MIB),
         name="upward",
     )(stay(charges), stay(leaf_basis), stay(transfers))
 
     below, above = shifted(up, 1), shifted(down, -1)
-    below2, above2 = shifted(up2, 2), shifted(down2, -2)
-
-    local, masked, bs_t, ts_t, top = pl.pallas_call(
+
+    local, masked, bs_t, ts_t, up2, down2, top = pl.pallas_call(
         lambda *refs: couple_kernel(plan, *refs),
         in_specs=[smem, vmem, vmem, vmem, vmem, vmem],
-        out_specs=[vmem] * 5,
+        out_specs=[vmem] * 7,
         out_shape=[
             resident((plan.inner_boxes * rank, rhs), F32),
             resident(couplings.shape, BF),
             resident((leaves, panels, rank), BF),
             resident((transfers.shape[0], panels, rank), BF),
+            resident((2 * rank, rhs), BF),
+            resident((2 * rank, rhs), BF),
             resident((rank, rhs), BF),
         ],
         compiler_params=pltpu.CompilerParams(vmem_limit_bytes=8 * MIB),
         cost_estimate=pl.CostEstimate(flops=6_000_000_000, bytes_accessed=8 * MIB, transcendentals=0),
         name="couple",
-    )(interactions.T, keep(poles), keep(bs), keep(ts), keep(top), keep(couplings))
-
+    )(interactions.T, keep(poles), keep(bs), keep(ts), keep(pair4), keep(couplings))
+
+    below2, above2 = shifted(up2, 2), shifted(down2, -2)
     below3, above3 = shifted(top, 3), shifted(top, -3)
 
     near, edge_near = pl.pallas_call(

time: 39.7 us -> 39.3 us (0.990)
  no operation moved by 1% of the time
where the time goes in v7:
time: 39.3 us; the launch traced here: 39.1 us
  starting transfers between devices  18.8 us (48%)
  Pallas kernels  15.5 us (39%)
  waiting for transfers between devices  4.65 us (12%)
    ppermute x6, starting transfers between devices, shifted(): return lax.ppermute(array, 'slab', pairs)  18.8 us
    pallas_call x1, Pallas kernels, body(): pl.pallas_call(lambda *refs: final_kernel(plan, *refs), in_specs=[vmem] *...  4.67 us
    ppermute x6, waiting for transfers between devices, shifted(): return lax.ppermute(array, 'slab', pairs)  4.65 us
    pallas_call x1, Pallas kernels, body(): pl.pallas_call(lambda *refs: upward_kernel(plan, chunks, *refs), in_specs...  4.36 us
    pallas_call x1, Pallas kernels, body(): pl.pallas_call(lambda *refs: couple_kernel(plan, *refs), in_specs=[smem,...  3.54 us
    pallas_call x1, Pallas kernels, body(): pl.pallas_call(lambda *refs: near_kernel(plan, *refs), in_specs=[smem, vm...  2.91 us
  transfers between devices with their start and end apart: 6, of which 1 were waited for; matrix products, arithmetic and copies ran while one was open for 0% of the time, Pallas kernels for 16%

profile of v7, /device:TPU:16, one launch (start us, length us, event | category | flops | bytes accessed | tf_op | source)
XLA Modules:
  0.0 39.1 jit_solution(13718167340343076343)
XLA Ops:
  0.0 0.0 copy-start.2
  0.0 0.0 copy-start.1
  0.0 4.4 %upward.1 = (bf16[4352,512]{1,0:T(8,128)(2,1)S(1)}, bf16[5376,512]{1,0:T(8,128)(2,1)S(1)}, bf16[784,512]{1,0:T(8,128)(2,1)S(1)}, bf16[784,512]{1,0:T(8,128)(2,1)...) custom-call(bf16[4096,512]{1,0:T(8,128)(2,1)} %refs_0_.1, ...), custom_call_target="tpu_custom_call" | custom-call | tf_op jit(solution)/shard_map/upward/pallas_call | solution.py:275
  4.4 1.9 %collective-permute-start = (bf16[784,512]{1,0:T(8,128)(2,1)S(1)}, bf16[784,512]{1,0:T(8,128)(2,1)S(1)}, u32[]{:S(2)}, u32[]{:S(2)}) collective-permute-start(bf16[784,512]{1,0:T(8,128)(2,1)S(1)} %get-tuple-element.32), channel_id=1, source_target_pairs={{0,1},{1,2},{2,3},{3,4},{4,5},{5,6},{6,7},{7,8},{8,9},{9,10},{10,1... | collective-permute-start | bytes 2408456 | tf_op jit(solution)/shard_map/ppermute | solution.py:264
  6.3 4.5 %collective-permute-start.1 = (bf16[784,512]{1,0:T(8,128)(2,1)S(1)}, bf16[784,512]{1,0:T(8,128)(2,1)S(1)}, u32[]{:S(2)}, u32[]{:S(2)}) collective-permute-start(bf16[784,512]{1,0:T(8,128)(2,1)S(1)} %get-tuple-element.33), channel_id=1, source_target_pairs={{1,0},{2,1},{3,2},{4,3},{5,4},{6,5},{7,6},{8,7},{9,8},{10,9},{11,1... | collective-permute-start | bytes 2408456 | tf_op jit(solution)/shard_map/ppermute | solution.py:264
  10.8 0.0 copy-done.2
  10.9 0.0 copy-done.1
  10.9 0.0 copy-start
  10.9 0.0 copy-start.3
  10.9 3.5 %couple.1 = (f32[3840,512]{1,0:T(8,128)S(1)}, bf16[63,64,256]{2,1,0:T(8,128)(2,1)S(1)}, bf16[32,128,64]{2,1,0:T(8,128)(2,1)S(1)}, bf16[31,128,64]{2,1,0:T(8,128)...) custom-call(s32[4,63]{1,0:T(4,128)S(1)} %bitcast.2, ...), custom_call_target="tpu_custom_call" | custom-call | flops 6000000000 | bytes 8388608 | tf_op jit(solution)/shard_map/couple/pallas_call | solution.py:295
  14.4 1.9 %collective-permute-start.5 = (bf16[64,512]{1,0:T(8,128)(2,1)S(1)}, bf16[64,512]{1,0:T(8,128)(2,1)S(1)}, u32[]{:S(2)}, u32[]{:S(2)}) collective-permute-start(bf16[64,512]{1,0:T(8,128)(2,1)S(1)} %get-tuple-element.36), channel_id=1, source_target_pairs={{3,0},{4,1},{5,2},{6,3},{7,4},{8,5},{9,6},{10,7},{11,8},{12,9},{13... | collective-permute-start | bytes 196616 | tf_op jit(solution)/shard_map/ppermute | solution.py:264
  16.4 3.6 %collective-permute-start.4 = (bf16[64,512]{1,0:T(8,128)(2,1)S(1)}, bf16[64,512]{1,0:T(8,128)(2,1)S(1)}, u32[]{:S(2)}, u32[]{:S(2)}) collective-permute-start(bf16[64,512]{1,0:T(8,128)(2,1)S(1)} %get-tuple-element.36), channel_id=1, source_target_pairs={{0,3},{1,4},{2,5},{3,6},{4,7},{5,8},{6,9},{7,10},{8,11},{9,12},{10... | collective-permute-start | bytes 196616 | tf_op jit(solution)/shard_map/ppermute | solution.py:264
  20.0 3.4 %collective-permute-start.2 = (bf16[128,512]{1,0:T(8,128)(2,1)S(1)}, bf16[128,512]{1,0:T(8,128)(2,1)S(1)}, u32[]{:S(2)}, u32[]{:S(2)}) collective-permute-start(bf16[128,512]{1,0:T(8,128)(2,1)S(1)} %get-tuple-element.34), channel_id=1, source_target_pairs={{0,2},{1,3},{2,4},{3,5},{4,6},{5,7},{6,8},{7,9},{8,10},{9,11},{10,... | collective-permute-start | bytes 393224 | tf_op jit(solution)/shard_map/ppermute | solution.py:264
  23.4 0.0 collective-permute-done.5.refs_11_
  23.4 3.3 %collective-permute-start.3 = (bf16[128,512]{1,0:T(8,128)(2,1)S(1)}, bf16[128,512]{1,0:T(8,128)(2,1)S(1)}, u32[]{:S(2)}, u32[]{:S(2)}) collective-permute-start(bf16[128,512]{1,0:T(8,128)(2,1)S(1)} %get-tuple-element.35), channel_id=1, source_target_pairs={{2,0},{3,1},{4,2},{5,3},{6,4},{7,5},{8,6},{9,7},{10,8},{11,9},{12,... | collective-permute-start | bytes 393224 | tf_op jit(solution)/shard_map/ppermute | solution.py:264
  26.8 0.0 copy-done
  26.8 0.0 copy-done.3
  26.8 2.9 %near.1 = (bf16[4096,512]{1,0:T(8,128)(2,1)S(1)}, bf16[2,128,128]{2,1,0:T(8,128)(2,1)S(1)}) custom-call(s32[3,32]{1,0:T(4,128)S(1)} %bitcast.3, bf16[4352,512]{1,0:T(8,128)(2,1)S(1)} %get-tuple-element.21.refs_1_, bf16[32,3,128,128]{3,2,1,0:T(8,128)(2,1)S(1)} %copy-done), custom_call_target="tpu_custom_call" | custom-call | flops 6000000000 | bytes 8388608 | tf_op jit(solution)/shard_map/near/pallas_call | solution.py:316
  29.7 0.0 collective-permute-done.4.refs_10_
  29.7 0.0 collective-permute-done.2.refs_8_
  29.7 4.6 %collective-permute-done.3.refs_9_ = bf16[128,512]{1,0:T(8,128)(2,1)S(1)} collective-permute-done((bf16[128,512]{1,0:T(8,128)(2,1)S(1)}, bf16[128,512]{1,0:T(8,128)(2,1)S(1)}, u32[]{:S(2)}, u32[]{:S(2)}) %collective-permute-start.3) | collective-permute-done | bytes 131104 | tf_op jit(solution)/shard_map/ppermute | solution.py:264
  34.4 0.0 collective-permute-done.refs_6_
  34.4 0.0 collective-permute-done.1.refs_7_
  34.4 4.7 %final.1 = bf16[4096,512]{1,0:T(8,128)(2,1)} custom-call(bf16[4096,512]{1,0:T(8,128)(2,1)S(1)} %get-tuple-element.22.refs_0_, f32[3840,512]{1,0:T(8,128)S(1)} %get-tuple-element.27.refs_1_, bf16[63,64,256]{2,1,0:T(8,128)(2,1)S(1)} %get-tuple-element.28.refs_2_, bf16[2,128,128]{2,1,0:T(8,128)(2,1)S(1)} %get-tuple-element.29.refs_3_, ...), custom_call_target="tpu_custom_call" | custom-call | tf_op jit(solution)/shard_map/final/pallas_call | solution.py:329
Async XLA Ops:
  0.0 10.8 %copy-start.2 = (s32[63,4]{0,1:T(4,128)S(1)}, s32[63,4]{0,1:T(4,128)}, u32[]{:S(2)}) copy-start(s32[63,4]{0,1:T(4,128)} %param.13) | copy-start | bytes 3028
  0.0 10.9 %copy-start.1 = (bf16[63,64,256]{2,1,0:T(8,128)(2,1)S(1)}, bf16[63,64,256]{2,1,0:T(8,128)(2,1)}, u32[]{:S(2)}) copy-start(bf16[63,64,256]{2,1,0:T(8,128)(2,1)} %refs_5_.1) | copy-start | bytes 6193156
  4.4 30.0 %collective-permute-start = (bf16[784,512]{1,0:T(8,128)(2,1)S(1)}, bf16[784,512]{1,0:T(8,128)(2,1)S(1)}, u32[]{:S(2)}, u32[]{:S(2)}) collective-permute-start(bf16[784,512]{1,0:T(8,128)(2,1)S(1)} %get-tuple-element.32), channel_id=1, source_target_pairs={{0,1},{1,2},{2,3},{3,4},{4,5},{5,6},{6,7},{7,8},{8,9},{9,10},{10,1... | collective-permute-start | bytes 2408456 | tf_op jit(solution)/shard_map/ppermute | solution.py:264
  6.3 28.1 %collective-permute-start.1 = (bf16[784,512]{1,0:T(8,128)(2,1)S(1)}, bf16[784,512]{1,0:T(8,128)(2,1)S(1)}, u32[]{:S(2)}, u32[]{:S(2)}) collective-permute-start(bf16[784,512]{1,0:T(8,128)(2,1)S(1)} %get-tuple-element.33), channel_id=1, source_target_pairs={{1,0},{2,1},{3,2},{4,3},{5,4},{6,5},{7,6},{8,7},{9,8},{10,9},{11,1... | collective-permute-start | bytes 2408456 | tf_op jit(solution)/shard_map/ppermute | solution.py:264
  10.9 15.9 %copy-start = (bf16[32,3,128,128]{3,2,1,0:T(8,128)(2,1)S(1)}, bf16[32,3,128,128]{3,2,1,0:T(8,128)(2,1)}, u32[]{:S(2)}) copy-start(bf16[32,3,128,128]{3,2,1,0:T(8,128)(2,1)} %refs_2_.3) | copy-start | bytes 9437188
  10.9 15.9 %copy-start.3 = (s32[32,3]{0,1:T(4,128)S(1)}, s32[32,3]{0,1:T(4,128)}, u32[]{:S(2)}) copy-start(s32[32,3]{0,1:T(4,128)} %param.9) | copy-start | bytes 1156
  14.4 9.0 %collective-permute-start.5 = (bf16[64,512]{1,0:T(8,128)(2,1)S(1)}, bf16[64,512]{1,0:T(8,128)(2,1)S(1)}, u32[]{:S(2)}, u32[]{:S(2)}) collective-permute-start(bf16[64,512]{1,0:T(8,128)(2,1)S(1)} %get-tuple-element.36), channel_id=1, source_target_pairs={{3,0},{4,1},{5,2},{6,3},{7,4},{8,5},{9,6},{10,7},{11,8},{12,9},{13... | collective-permute-start | bytes 196616 | tf_op jit(solution)/shard_map/ppermute | solution.py:264
  16.4 13.4 %collective-permute-start.4 = (bf16[64,512]{1,0:T(8,128)(2,1)S(1)}, bf16[64,512]{1,0:T(8,128)(2,1)S(1)}, u32[]{:S(2)}, u32[]{:S(2)}) collective-permute-start(bf16[64,512]{1,0:T(8,128)(2,1)S(1)} %get-tuple-element.36), channel_id=1, source_target_pairs={{0,3},{1,4},{2,5},{3,6},{4,7},{5,8},{6,9},{7,10},{8,11},{9,12},{10... | collective-permute-start | bytes 196616 | tf_op jit(solution)/shard_map/ppermute | solution.py:264
  20.0 9.7 %collective-permute-start.2 = (bf16[128,512]{1,0:T(8,128)(2,1)S(1)}, bf16[128,512]{1,0:T(8,128)(2,1)S(1)}, u32[]{:S(2)}, u32[]{:S(2)}) collective-permute-start(bf16[128,512]{1,0:T(8,128)(2,1)S(1)} %get-tuple-element.34), channel_id=1, source_target_pairs={{0,2},{1,3},{2,4},{3,5},{4,6},{5,7},{6,8},{7,9},{8,10},{9,11},{10,... | collective-permute-start | bytes 393224 | tf_op jit(solution)/shard_map/ppermute | solution.py:264
  23.4 10.9 %collective-permute-start.3 = (bf16[128,512]{1,0:T(8,128)(2,1)S(1)}, bf16[128,512]{1,0:T(8,128)(2,1)S(1)}, u32[]{:S(2)}, u32[]{:S(2)}) collective-permute-start(bf16[128,512]{1,0:T(8,128)(2,1)S(1)} %get-tuple-element.35), channel_id=1, source_target_pairs={{2,0},{3,1},{4,2},{5,3},{6,4},{7,5},{8,6},{9,7},{10,8},{11,9},{12,... | collective-permute-start | bytes 393224 | tf_op jit(solution)/shard_map/ppermute | solution.py:264

commit v8 on v7

--- a/solution.py
+++ b/solution.py
@@ -37,6 +37,11 @@
         self.padded = [sum(c + 6 for c in self.count[:level]) for level in range(FULL)]
         self.padded_boxes = sum(c + 6 for c in self.count[:FULL])
         self.inner_boxes = sum(self.count[:FULL])
+        self.rim, self.rim_boxes = [], 0
+        for m in self.count[:FULL]:
+            boxes = sorted({0, 1, 2, m - 3, m - 2, m - 1})
+            self.rim.append({box: self.rim_boxes + k for k, box in enumerate(boxes)})
+            self.rim_boxes += len(boxes)
         self.msg_pole = [panels + 2 * rank * level for level in range(FULL)]
         self.msg_top = panels + 2 * rank * FULL
         self.msg_small = self.msg_top + rank
@@ -171,11 +176,8 @@
     edge_near[1] = side(plan.leaves - 1, 2)
 
 
-def final_kernel(
-    plan, near, local, masked, edge_near, bs_t, ts_t, below, above, below2, above2, below3, above3,
-    out, loc, stage, sems,
-):
-    p, r, n = plan.panels, plan.rank, plan.leaves
+def rim_kernel(plan, local, masked, below, above, below3, above3, rims, outermost, summit):
+    p, r = plan.panels, plan.rank
     small = pl.ds(plan.msg_small, r)
     messages = (below, above)
 
@@ -190,18 +192,6 @@
                 matrix = jnp.concatenate([message[rows, pl.ds(part * p, p)] for part in range(plan.rhs // p)], axis=0)
             children = [sent[k][level - 1][r:], rim[k][-1]] if k == 0 else [rim[k][-1], sent[k][level - 1][:r]]
             rim[k].append(dot(matrix, jnp.concatenate(children, axis=0)).astype(BF))
-
-    def place(level, box):
-        return pl.ds((plan.first[level] + box) * r, r)
-
-    stack = jnp.concatenate([below3[...], below2[pl.ds(r, r)], above2[pl.ds(r, r)], above3[...]], axis=0)
-    summit = dot(masked[plan.first[LEVELS - 1]], stack).astype(BF)
-    pushed = dot(ts_t[plan.trans[LEVELS - 1]], summit)
-    low, high = below[pl.ds(plan.msg_top, r)], above[pl.ds(plan.msg_top, r)]
-    stacks = ([below2[pl.ds(0, r)], low, rim[1][FULL], high], [low, rim[0][FULL], high, above2[pl.ds(0, r)]])
-    for k, stack in enumerate(stacks):
-        gained = dot(masked[plan.first[FULL] + k], jnp.concatenate(stack, axis=0))
-        loc[place(FULL, k)] = (gained + pushed[k * r : (k + 1) * r]).astype(BF)
 
     def rim_gain(level, box):
         first, m = plan.first[level], plan.count[level]
@@ -219,13 +209,42 @@
             gain = value if gain is None else gain + value
         return gain
 
+    for k in range(2):
+        outermost[pl.ds(k * r, r)] = rim[k][FULL]
+    for level in range(FULL):
+        for box in plan.rim[level]:
+            rows = pl.ds((plan.first[level] + box) * r, r)
+            rims[pl.ds(plan.rim[level][box] * r, r)] = local[rows] + rim_gain(level, box)
+    box = plan.first[LEVELS - 1]
+    summit[...] = dot(masked[box, :, pl.ds(0, r)], below3[...]) + dot(masked[box, :, pl.ds(3 * r, r)], above3[...])
+
+
+def final_kernel(
+    plan, near, local, masked, edge_near, bs_t, ts_t, below2, above2, below, above, rims, outermost, partial,
+    out, loc, stage, sems,
+):
+    p, r, n = plan.panels, plan.rank, plan.leaves
+    rim_low, rim_high = outermost[pl.ds(0, r)], outermost[pl.ds(r, r)]
+
+    def place(level, box):
+        return pl.ds((plan.first[level] + box) * r, r)
+
+    stack = jnp.concatenate([below2[pl.ds(r, r)], above2[pl.ds(r, r)]], axis=0)
+    summit = (partial[...] + dot(masked[plan.first[LEVELS - 1], :, pl.ds(r, 2 * r)], stack)).astype(BF)
+    pushed = dot(ts_t[plan.trans[LEVELS - 1]], summit)
+    low, high = below[pl.ds(plan.msg_top, r)], above[pl.ds(plan.msg_top, r)]
+    stacks = ([below2[pl.ds(0, r)], low, rim_high, high], [low, rim_low, high, above2[pl.ds(0, r)]])
+    for k, stack in enumerate(stacks):
+        gained = dot(masked[plan.first[FULL] + k], jnp.concatenate(stack, axis=0))
+        loc[place(FULL, k)] = (gained + pushed[k * r : (k + 1) * r]).astype(BF)
+
     def descend(level, box):
         push = dot(ts_t[plan.trans[level] + box], loc[place(level, box)])
         for k in range(2):
             child = 2 * box + k
-            value = local[place(level - 1, child)] + push[k * r : (k + 1) * r]
-            gain = rim_gain(level - 1, child)
-            loc[place(level - 1, child)] = (value if gain is None else value + gain).astype(BF)
+            edge = plan.rim[level - 1].get(child)
+            own = local[place(level - 1, child)] if edge is None else rims[pl.ds(edge * r, r)]
+            loc[place(level - 1, child)] = (own + push[k * r : (k + 1) * r]).astype(BF)
 
     for level in range(FULL, 1, -1):
         for box in range(plan.count[level]):
@@ -326,9 +345,23 @@
         name="near",
     )(near_pattern.T, keep(padded_x), keep(near_blocks))
 
+    rims, outermost, partial = pl.pallas_call(
+        lambda *refs: rim_kernel(plan, *refs),
+        in_specs=[vmem] * 6,
+        out_specs=[vmem] * 3,
+        out_shape=[
+            resident((plan.rim_boxes * rank, rhs), F32),
+            resident((2 * rank, rhs), BF),
+            resident((rank, rhs), F32),
+        ],
+        compiler_params=pltpu.CompilerParams(vmem_limit_bytes=8 * MIB),
+        cost_estimate=pl.CostEstimate(flops=10_000_000, bytes_accessed=MIB // 32, transcendentals=0),
+        name="rim",
+    )(keep(local), keep(masked), keep(below), keep(above), keep(below3), keep(above3))
+
     return pl.pallas_call(
         lambda *refs: final_kernel(plan, *refs),
-        in_specs=[vmem] * 12,
+        in_specs=[vmem] * 13,
         out_specs=hbm,
         out_shape=jax.ShapeDtypeStruct((leaves * panels, rhs), BF),
         scratch_shapes=[
@@ -340,7 +373,7 @@
         name="final",
     )(
         keep(near), keep(local), keep(masked), keep(edge_near), keep(bs_t), keep(ts_t),
-        keep(below), keep(above), keep(below2), keep(above2), keep(below3), keep(above3),
+        keep(below2), keep(above2), keep(below), keep(above), keep(rims), keep(outermost), keep(partial),
     )
 
 

time: 39.3 us -> 38.3 us (0.975)
  waiting for transfers between devices: 4.65 us -> 3.45 us
    pallas_call x0 -> x1, Pallas kernels: none -> 1.26 us  [body(): pl.pallas_call(lambda *refs: rim_kernel(plan, *refs), in_specs=[vmem] * 6...]
    ppermute x6, waiting for transfers between devices: 4.65 us -> 3.45 us  [shifted(): return lax.ppermute(array, 'slab', pairs)]
    pallas_call x1, Pallas kernels: 4.67 us -> 3.67 us  [body(): pl.pallas_call(lambda *refs: final_kernel(plan, *refs), in_specs=[vmem] *...]
  transfers between devices with their start and end apart: 6 -> 6, of which waited for: 1 -> 1; matrix products, arithmetic and copies ran while one was open for 0% -> 0% of each run, Pallas kernels for 16% -> 20%
where the time goes in v8:
time: 38.3 us; the launch traced here: 38 us
  starting transfers between devices  18.8 us (49%)
  Pallas kernels  15.6 us (41%)
  waiting for transfers between devices  3.45 us (9%)
    ppermute x6, starting transfers between devices, shifted(): return lax.ppermute(array, 'slab', pairs)  18.8 us
    pallas_call x1, Pallas kernels, body(): pl.pallas_call(lambda *refs: upward_kernel(plan, chunks, *refs), in_specs...  4.36 us
    pallas_call x1, Pallas kernels, body(): pl.pallas_call(lambda *refs: final_kernel(plan, *refs), in_specs=[vmem] *...  3.67 us
    pallas_call x1, Pallas kernels, body(): pl.pallas_call(lambda *refs: couple_kernel(plan, *refs), in_specs=[smem,...  3.46 us
    ppermute x6, waiting for transfers between devices, shifted(): return lax.ppermute(array, 'slab', pairs)  3.45 us
    pallas_call x1, Pallas kernels, body(): pl.pallas_call(lambda *refs: near_kernel(plan, *refs), in_specs=[smem, vm...  2.91 us
    pallas_call x1, Pallas kernels, body(): pl.pallas_call(lambda *refs: rim_kernel(plan, *refs), in_specs=[vmem] * 6...  1.26 us
  transfers between devices with their start and end apart: 6, of which 1 were waited for; matrix products, arithmetic and copies ran while one was open for 0% of the time, Pallas kernels for 20%

profile of v8, /device:TPU:16, one launch (start us, length us, event | category | flops | bytes accessed | tf_op | source)
XLA Modules:
  0.0 38.0 jit_solution(754662564782955957)
XLA Ops:
  0.0 0.0 copy-start.2
  0.0 0.0 copy-start.1
  0.0 4.4 %upward.1 = (bf16[4352,512]{1,0:T(8,128)(2,1)S(1)}, bf16[5376,512]{1,0:T(8,128)(2,1)S(1)}, bf16[784,512]{1,0:T(8,128)(2,1)S(1)}, bf16[784,512]{1,0:T(8,128)(2,1)...) custom-call(bf16[4096,512]{1,0:T(8,128)(2,1)} %refs_0_.1, ...), custom_call_target="tpu_custom_call" | custom-call | tf_op jit(solution)/shard_map/upward/pallas_call | solution.py:294
  4.4 1.9 %collective-permute-start.2 = (bf16[784,512]{1,0:T(8,128)(2,1)S(1)}, bf16[784,512]{1,0:T(8,128)(2,1)S(1)}, u32[]{:S(2)}, u32[]{:S(2)}) collective-permute-start(bf16[784,512]{1,0:T(8,128)(2,1)S(1)} %get-tuple-element.37), channel_id=1, source_target_pairs={{0,1},{1,2},{2,3},{3,4},{4,5},{5,6},{6,7},{7,8},{8,9},{9,10},{10,1... | collective-permute-start | bytes 2408456 | tf_op jit(solution)/shard_map/ppermute | solution.py:283
  6.3 4.5 %collective-permute-start.3 = (bf16[784,512]{1,0:T(8,128)(2,1)S(1)}, bf16[784,512]{1,0:T(8,128)(2,1)S(1)}, u32[]{:S(2)}, u32[]{:S(2)}) collective-permute-start(bf16[784,512]{1,0:T(8,128)(2,1)S(1)} %get-tuple-element.38), channel_id=1, source_target_pairs={{1,0},{2,1},{3,2},{4,3},{5,4},{6,5},{7,6},{8,7},{9,8},{10,9},{11,1... | collective-permute-start | bytes 2408456 | tf_op jit(solution)/shard_map/ppermute | solution.py:283
  10.8 0.0 copy-done.2
  10.9 0.0 copy-done.1
  10.9 0.0 copy-start
  10.9 0.0 copy-start.3
  10.9 3.5 %couple.1 = (f32[3840,512]{1,0:T(8,128)S(1)}, bf16[63,64,256]{2,1,0:T(8,128)(2,1)S(1)}, bf16[32,128,64]{2,1,0:T(8,128)(2,1)S(1)}, bf16[31,128,64]{2,1,0:T(8,128)...) custom-call(s32[4,63]{1,0:T(4,128)S(1)} %bitcast.2, ...), custom_call_target="tpu_custom_call" | custom-call | flops 6000000000 | bytes 8388608 | tf_op jit(solution)/shard_map/couple/pallas_call | solution.py:314
  14.4 1.9 %collective-permute-start.5 = (bf16[64,512]{1,0:T(8,128)(2,1)S(1)}, bf16[64,512]{1,0:T(8,128)(2,1)S(1)}, u32[]{:S(2)}, u32[]{:S(2)}) collective-permute-start(bf16[64,512]{1,0:T(8,128)(2,1)S(1)} %get-tuple-element.39), channel_id=1, source_target_pairs={{3,0},{4,1},{5,2},{6,3},{7,4},{8,5},{9,6},{10,7},{11,8},{12,9},{13... | collective-permute-start | bytes 196616 | tf_op jit(solution)/shard_map/ppermute | solution.py:283
  16.3 3.6 %collective-permute-start.4 = (bf16[64,512]{1,0:T(8,128)(2,1)S(1)}, bf16[64,512]{1,0:T(8,128)(2,1)S(1)}, u32[]{:S(2)}, u32[]{:S(2)}) collective-permute-start(bf16[64,512]{1,0:T(8,128)(2,1)S(1)} %get-tuple-element.39), channel_id=1, source_target_pairs={{0,3},{1,4},{2,5},{3,6},{4,7},{5,8},{6,9},{7,10},{8,11},{9,12},{10... | collective-permute-start | bytes 196616 | tf_op jit(solution)/shard_map/ppermute | solution.py:283
  19.9 3.4 %collective-permute-start = (bf16[128,512]{1,0:T(8,128)(2,1)S(1)}, bf16[128,512]{1,0:T(8,128)(2,1)S(1)}, u32[]{:S(2)}, u32[]{:S(2)}) collective-permute-start(bf16[128,512]{1,0:T(8,128)(2,1)S(1)} %get-tuple-element.35), channel_id=1, source_target_pairs={{0,2},{1,3},{2,4},{3,5},{4,6},{5,7},{6,8},{7,9},{8,10},{9,11},{10,... | collective-permute-start | bytes 393224 | tf_op jit(solution)/shard_map/ppermute | solution.py:283
  23.3 0.0 collective-permute-done.5.refs_5_
  23.3 3.3 %collective-permute-start.1 = (bf16[128,512]{1,0:T(8,128)(2,1)S(1)}, bf16[128,512]{1,0:T(8,128)(2,1)S(1)}, u32[]{:S(2)}, u32[]{:S(2)}) collective-permute-start(bf16[128,512]{1,0:T(8,128)(2,1)S(1)} %get-tuple-element.36), channel_id=1, source_target_pairs={{2,0},{3,1},{4,2},{5,3},{6,4},{7,5},{8,6},{9,7},{10,8},{11,9},{12,... | collective-permute-start | bytes 393224 | tf_op jit(solution)/shard_map/ppermute | solution.py:283
  26.7 0.0 copy-done
  26.7 0.0 copy-done.3
  26.7 2.9 %near.1 = (bf16[4096,512]{1,0:T(8,128)(2,1)S(1)}, bf16[2,128,128]{2,1,0:T(8,128)(2,1)S(1)}) custom-call(s32[3,32]{1,0:T(4,128)S(1)} %bitcast.3, bf16[4352,512]{1,0:T(8,128)(2,1)S(1)} %get-tuple-element.24.refs_1_, bf16[32,3,128,128]{3,2,1,0:T(8,128)(2,1)S(1)} %copy-done), custom_call_target="tpu_custom_call" | custom-call | flops 6000000000 | bytes 8388608 | tf_op jit(solution)/shard_map/near/pallas_call | solution.py:335
  29.6 0.0 collective-permute-done.4.refs_4_
  29.6 0.0 collective-permute-done.2.refs_2_.refs_8_
  29.7 0.0 collective-permute-done.3.refs_3_.refs_9_
  29.7 1.3 %rim.1 = (f32[1408,512]{1,0:T(8,128)S(1)}, bf16[128,512]{1,0:T(8,128)(2,1)S(1)}, f32[64,512]{1,0:T(8,128)S(1)}) custom-call(f32[3840,512]{1,0:T(8,128)S(1)} %get-tuple-element.30.refs_0_.refs_1_, bf16[63,64,256]{2,1,0:T(8,128)(2,1)S(1)} %get-tuple-element.31.refs_1_.refs_2_, bf16[784,512]{1,0:T(8,128)(2,1)S(1)} %collective-permute-done.2.refs_2_.refs_8_, ...), custom_call_target="tpu_custom_call" | custom-call | flops 10000000 | bytes 32768 | tf_op jit(solution)/shard_map/rim/pallas_call | solution.py:348
  30.9 0.0 collective-permute-done.refs_6_
  30.9 3.4 %collective-permute-done.1.refs_7_ = bf16[128,512]{1,0:T(8,128)(2,1)S(1)} collective-permute-done((bf16[128,512]{1,0:T(8,128)(2,1)S(1)}, bf16[128,512]{1,0:T(8,128)(2,1)S(1)}, u32[]{:S(2)}, u32[]{:S(2)}) %collective-permute-start.1) | collective-permute-done | bytes 131104 | tf_op jit(solution)/shard_map/ppermute | solution.py:283
  34.4 3.7 %final.1 = bf16[4096,512]{1,0:T(8,128)(2,1)} custom-call(bf16[4096,512]{1,0:T(8,128)(2,1)S(1)} %get-tuple-element.25.refs_0_, f32[3840,512]{1,0:T(8,128)S(1)} %get-tuple-element.30.refs_0_.refs_1_, bf16[63,64,256]{2,1,0:T(8,128)(2,1)S(1)} %get-tuple-element.31.refs_1_.refs_2_, bf16[2,128,128]{2,1,0:T(8,128)(2,1)S(1)} %get-tuple-element.32.refs_3_, ...), custom_call_target="tpu_custom_call" | custom-call | tf_op jit(solution)/shard_map/final/pallas_call | solution.py:362
Async XLA Ops:
  0.0 10.8 %copy-start.2 = (s32[63,4]{0,1:T(4,128)S(1)}, s32[63,4]{0,1:T(4,128)}, u32[]{:S(2)}) copy-start(s32[63,4]{0,1:T(4,128)} %param.13) | copy-start | bytes 3028
  0.0 10.9 %copy-start.1 = (bf16[63,64,256]{2,1,0:T(8,128)(2,1)S(1)}, bf16[63,64,256]{2,1,0:T(8,128)(2,1)}, u32[]{:S(2)}) copy-start(bf16[63,64,256]{2,1,0:T(8,128)(2,1)} %refs_5_.1) | copy-start | bytes 6193156
  4.4 25.3 %collective-permute-start.2 = (bf16[784,512]{1,0:T(8,128)(2,1)S(1)}, bf16[784,512]{1,0:T(8,128)(2,1)S(1)}, u32[]{:S(2)}, u32[]{:S(2)}) collective-permute-start(bf16[784,512]{1,0:T(8,128)(2,1)S(1)} %get-tuple-element.37), channel_id=1, source_target_pairs={{0,1},{1,2},{2,3},{3,4},{4,5},{5,6},{6,7},{7,8},{8,9},{9,10},{10,1... | collective-permute-start | bytes 2408456 | tf_op jit(solution)/shard_map/ppermute | solution.py:283
  6.3 23.4 %collective-permute-start.3 = (bf16[784,512]{1,0:T(8,128)(2,1)S(1)}, bf16[784,512]{1,0:T(8,128)(2,1)S(1)}, u32[]{:S(2)}, u32[]{:S(2)}) collective-permute-start(bf16[784,512]{1,0:T(8,128)(2,1)S(1)} %get-tuple-element.38), channel_id=1, source_target_pairs={{1,0},{2,1},{3,2},{4,3},{5,4},{6,5},{7,6},{8,7},{9,8},{10,9},{11,1... | collective-permute-start | bytes 2408456 | tf_op jit(solution)/shard_map/ppermute | solution.py:283
  10.9 15.8 %copy-start = (bf16[32,3,128,128]{3,2,1,0:T(8,128)(2,1)S(1)}, bf16[32,3,128,128]{3,2,1,0:T(8,128)(2,1)}, u32[]{:S(2)}) copy-start(bf16[32,3,128,128]{3,2,1,0:T(8,128)(2,1)} %refs_2_.3) | copy-start | bytes 9437188
  10.9 15.8 %copy-start.3 = (s32[32,3]{0,1:T(4,128)S(1)}, s32[32,3]{0,1:T(4,128)}, u32[]{:S(2)}) copy-start(s32[32,3]{0,1:T(4,128)} %param.9) | copy-start | bytes 1156
  14.4 9.0 %collective-permute-start.5 = (bf16[64,512]{1,0:T(8,128)(2,1)S(1)}, bf16[64,512]{1,0:T(8,128)(2,1)S(1)}, u32[]{:S(2)}, u32[]{:S(2)}) collective-permute-start(bf16[64,512]{1,0:T(8,128)(2,1)S(1)} %get-tuple-element.39), channel_id=1, source_target_pairs={{3,0},{4,1},{5,2},{6,3},{7,4},{8,5},{9,6},{10,7},{11,8},{12,9},{13... | collective-permute-start | bytes 196616 | tf_op jit(solution)/shard_map/ppermute | solution.py:283
  16.3 13.4 %collective-permute-start.4 = (bf16[64,512]{1,0:T(8,128)(2,1)S(1)}, bf16[64,512]{1,0:T(8,128)(2,1)S(1)}, u32[]{:S(2)}, u32[]{:S(2)}) collective-permute-start(bf16[64,512]{1,0:T(8,128)(2,1)S(1)} %get-tuple-element.39), channel_id=1, source_target_pairs={{0,3},{1,4},{2,5},{3,6},{4,7},{5,8},{6,9},{7,10},{8,11},{9,12},{10... | collective-permute-start | bytes 196616 | tf_op jit(solution)/shard_map/ppermute | solution.py:283
  19.9 11.0 %collective-permute-start = (bf16[128,512]{1,0:T(8,128)(2,1)S(1)}, bf16[128,512]{1,0:T(8,128)(2,1)S(1)}, u32[]{:S(2)}, u32[]{:S(2)}) collective-permute-start(bf16[128,512]{1,0:T(8,128)(2,1)S(1)} %get-tuple-element.35), channel_id=1, source_target_pairs={{0,2},{1,3},{2,4},{3,5},{4,6},{5,7},{6,8},{7,9},{8,10},{9,11},{10,... | collective-permute-start | bytes 393224 | tf_op jit(solution)/shard_map/ppermute | solution.py:283
  23.3 11.0 %collective-permute-start.1 = (bf16[128,512]{1,0:T(8,128)(2,1)S(1)}, bf16[128,512]{1,0:T(8,128)(2,1)S(1)}, u32[]{:S(2)}, u32[]{:S(2)}) collective-permute-start(bf16[128,512]{1,0:T(8,128)(2,1)S(1)} %get-tuple-element.36), channel_id=1, source_target_pairs={{2,0},{3,1},{4,2},{5,3},{6,4},{7,5},{8,6},{9,7},{10,8},{11,9},{12,... | collective-permute-start | bytes 393224 | tf_op jit(solution)/shard_map/ppermute | solution.py:283

commit v9 on v8

--- a/solution.py
+++ b/solution.py
@@ -289,7 +289,7 @@
     hbm = pl.BlockSpec(memory_space=pltpu.HBM)
     vmem = pl.BlockSpec(memory_space=pltpu.VMEM)
     smem = pl.BlockSpec(memory_space=pltpu.SMEM)
-    chunks = 8
+    chunks = 16
 
     padded_x, poles, up, down, pair4, bs, ts = pl.pallas_call(
         lambda *refs: upward_kernel(plan, chunks, *refs),

time: 38.3 us -> 39.4 us (1.029)
  Pallas kernels: 15.6 us -> 16.8 us
    pallas_call x1, Pallas kernels: 4.36 us -> 5.47 us  [body(): pl.pallas_call(lambda *refs: upward_kernel(plan, chunks, *refs), in_specs...]
  transfers between devices with their start and end apart: 6 -> 6, of which waited for: 1 -> 1; matrix products, arithmetic and copies ran while one was open for 0% -> 0% of each run, Pallas kernels for 20% -> 19%
where the time goes in v9:
time: 39.4 us; the launch traced here: 39.2 us
  starting transfers between devices  18.8 us (48%)
  Pallas kernels  16.8 us (43%)
  waiting for transfers between devices  3.45 us (9%)
    ppermute x6, starting transfers between devices, shifted(): return lax.ppermute(array, 'slab', pairs)  18.8 us
    pallas_call x1, Pallas kernels, body(): pl.pallas_call(lambda *refs: upward_kernel(plan, chunks, *refs), in_specs...  5.47 us
    pallas_call x1, Pallas kernels, body(): pl.pallas_call(lambda *refs: final_kernel(plan, *refs), in_specs=[vmem] *...  3.67 us
    pallas_call x1, Pallas kernels, body(): pl.pallas_call(lambda *refs: couple_kernel(plan, *refs), in_specs=[smem,...  3.46 us
    ppermute x6, waiting for transfers between devices, shifted(): return lax.ppermute(array, 'slab', pairs)  3.45 us
    pallas_call x1, Pallas kernels, body(): pl.pallas_call(lambda *refs: near_kernel(plan, *refs), in_specs=[smem, vm...  2.91 us
    pallas_call x1, Pallas kernels, body(): pl.pallas_call(lambda *refs: rim_kernel(plan, *refs), in_specs=[vmem] * 6...  1.26 us
  transfers between devices with their start and end apart: 6, of which 1 were waited for; matrix products, arithmetic and copies ran while one was open for 0% of the time, Pallas kernels for 19%

profile of v9, /device:TPU:16, one launch (start us, length us, event | category | flops | bytes accessed | tf_op | source)
XLA Modules:
  0.0 39.2 jit_solution(407708076965603368)
XLA Ops:
  0.0 0.0 copy-start.2
  0.0 0.0 copy-start.1
  0.0 5.5 %upward.1 = (bf16[4352,512]{1,0:T(8,128)(2,1)S(1)}, bf16[5376,512]{1,0:T(8,128)(2,1)S(1)}, bf16[784,512]{1,0:T(8,128)(2,1)S(1)}, bf16[784,512]{1,0:T(8,128)(2,1)...) custom-call(bf16[4096,512]{1,0:T(8,128)(2,1)} %refs_0_.1, ...), custom_call_target="tpu_custom_call" | custom-call | tf_op jit(solution)/shard_map/upward/pallas_call | solution.py:294
  5.5 1.9 %collective-permute-start.2 = (bf16[784,512]{1,0:T(8,128)(2,1)S(1)}, bf16[784,512]{1,0:T(8,128)(2,1)S(1)}, u32[]{:S(2)}, u32[]{:S(2)}) collective-permute-start(bf16[784,512]{1,0:T(8,128)(2,1)S(1)} %get-tuple-element.37), channel_id=1, source_target_pairs={{0,1},{1,2},{2,3},{3,4},{4,5},{5,6},{6,7},{7,8},{8,9},{9,10},{10,1... | collective-permute-start | bytes 2408456 | tf_op jit(solution)/shard_map/ppermute | solution.py:283
  7.4 4.5 %collective-permute-start.3 = (bf16[784,512]{1,0:T(8,128)(2,1)S(1)}, bf16[784,512]{1,0:T(8,128)(2,1)S(1)}, u32[]{:S(2)}, u32[]{:S(2)}) collective-permute-start(bf16[784,512]{1,0:T(8,128)(2,1)S(1)} %get-tuple-element.38), channel_id=1, source_target_pairs={{1,0},{2,1},{3,2},{4,3},{5,4},{6,5},{7,6},{8,7},{9,8},{10,9},{11,1... | collective-permute-start | bytes 2408456 | tf_op jit(solution)/shard_map/ppermute | solution.py:283
  12.0 0.0 copy-done.2
  12.0 0.0 copy-done.1
  12.0 0.0 copy-start
  12.0 0.0 copy-start.3
  12.0 3.5 %couple.1 = (f32[3840,512]{1,0:T(8,128)S(1)}, bf16[63,64,256]{2,1,0:T(8,128)(2,1)S(1)}, bf16[32,128,64]{2,1,0:T(8,128)(2,1)S(1)}, bf16[31,128,64]{2,1,0:T(8,128)...) custom-call(s32[4,63]{1,0:T(4,128)S(1)} %bitcast.2, ...), custom_call_target="tpu_custom_call" | custom-call | flops 6000000000 | bytes 8388608 | tf_op jit(solution)/shard_map/couple/pallas_call | solution.py:314
  15.5 1.9 %collective-permute-start.5 = (bf16[64,512]{1,0:T(8,128)(2,1)S(1)}, bf16[64,512]{1,0:T(8,128)(2,1)S(1)}, u32[]{:S(2)}, u32[]{:S(2)}) collective-permute-start(bf16[64,512]{1,0:T(8,128)(2,1)S(1)} %get-tuple-element.39), channel_id=1, source_target_pairs={{3,0},{4,1},{5,2},{6,3},{7,4},{8,5},{9,6},{10,7},{11,8},{12,9},{13... | collective-permute-start | bytes 196616 | tf_op jit(solution)/shard_map/ppermute | solution.py:283
  17.4 3.6 %collective-permute-start.4 = (bf16[64,512]{1,0:T(8,128)(2,1)S(1)}, bf16[64,512]{1,0:T(8,128)(2,1)S(1)}, u32[]{:S(2)}, u32[]{:S(2)}) collective-permute-start(bf16[64,512]{1,0:T(8,128)(2,1)S(1)} %get-tuple-element.39), channel_id=1, source_target_pairs={{0,3},{1,4},{2,5},{3,6},{4,7},{5,8},{6,9},{7,10},{8,11},{9,12},{10... | collective-permute-start | bytes 196616 | tf_op jit(solution)/shard_map/ppermute | solution.py:283
  21.1 3.4 %collective-permute-start = (bf16[128,512]{1,0:T(8,128)(2,1)S(1)}, bf16[128,512]{1,0:T(8,128)(2,1)S(1)}, u32[]{:S(2)}, u32[]{:S(2)}) collective-permute-start(bf16[128,512]{1,0:T(8,128)(2,1)S(1)} %get-tuple-element.35), channel_id=1, source_target_pairs={{0,2},{1,3},{2,4},{3,5},{4,6},{5,7},{6,8},{7,9},{8,10},{9,11},{10,... | collective-permute-start | bytes 393224 | tf_op jit(solution)/shard_map/ppermute | solution.py:283
  24.5 0.0 collective-permute-done.5.refs_5_
  24.5 3.3 %collective-permute-start.1 = (bf16[128,512]{1,0:T(8,128)(2,1)S(1)}, bf16[128,512]{1,0:T(8,128)(2,1)S(1)}, u32[]{:S(2)}, u32[]{:S(2)}) collective-permute-start(bf16[128,512]{1,0:T(8,128)(2,1)S(1)} %get-tuple-element.36), channel_id=1, source_target_pairs={{2,0},{3,1},{4,2},{5,3},{6,4},{7,5},{8,6},{9,7},{10,8},{11,9},{12,... | collective-permute-start | bytes 393224 | tf_op jit(solution)/shard_map/ppermute | solution.py:283
  27.8 0.0 copy-done
  27.8 0.0 copy-done.3
  27.8 2.9 %near.1 = (bf16[4096,512]{1,0:T(8,128)(2,1)S(1)}, bf16[2,128,128]{2,1,0:T(8,128)(2,1)S(1)}) custom-call(s32[3,32]{1,0:T(4,128)S(1)} %bitcast.3, bf16[4352,512]{1,0:T(8,128)(2,1)S(1)} %get-tuple-element.24.refs_1_, bf16[32,3,128,128]{3,2,1,0:T(8,128)(2,1)S(1)} %copy-done), custom_call_target="tpu_custom_call" | custom-call | flops 6000000000 | bytes 8388608 | tf_op jit(solution)/shard_map/near/pallas_call | solution.py:335
  30.8 0.0 collective-permute-done.4.refs_4_
  30.8 0.0 collective-permute-done.2.refs_2_.refs_8_
  30.8 0.0 collective-permute-done.3.refs_3_.refs_9_
  30.8 1.3 %rim.1 = (f32[1408,512]{1,0:T(8,128)S(1)}, bf16[128,512]{1,0:T(8,128)(2,1)S(1)}, f32[64,512]{1,0:T(8,128)S(1)}) custom-call(f32[3840,512]{1,0:T(8,128)S(1)} %get-tuple-element.30.refs_0_.refs_1_, bf16[63,64,256]{2,1,0:T(8,128)(2,1)S(1)} %get-tuple-element.31.refs_1_.refs_2_, bf16[784,512]{1,0:T(8,128)(2,1)S(1)} %collective-permute-done.2.refs_2_.refs_8_, ...), custom_call_target="tpu_custom_call" | custom-call | flops 10000000 | bytes 32768 | tf_op jit(solution)/shard_map/rim/pallas_call | solution.py:348
  32.0 0.0 collective-permute-done.refs_6_
  32.1 3.4 %collective-permute-done.1.refs_7_ = bf16[128,512]{1,0:T(8,128)(2,1)S(1)} collective-permute-done((bf16[128,512]{1,0:T(8,128)(2,1)S(1)}, bf16[128,512]{1,0:T(8,128)(2,1)S(1)}, u32[]{:S(2)}, u32[]{:S(2)}) %collective-permute-start.1) | collective-permute-done | bytes 131104 | tf_op jit(solution)/shard_map/ppermute | solution.py:283
  35.5 3.7 %final.1 = bf16[4096,512]{1,0:T(8,128)(2,1)} custom-call(bf16[4096,512]{1,0:T(8,128)(2,1)S(1)} %get-tuple-element.25.refs_0_, f32[3840,512]{1,0:T(8,128)S(1)} %get-tuple-element.30.refs_0_.refs_1_, bf16[63,64,256]{2,1,0:T(8,128)(2,1)S(1)} %get-tuple-element.31.refs_1_.refs_2_, bf16[2,128,128]{2,1,0:T(8,128)(2,1)S(1)} %get-tuple-element.32.refs_3_, ...), custom_call_target="tpu_custom_call" | custom-call | tf_op jit(solution)/shard_map/final/pallas_call | solution.py:362
Async XLA Ops:
  0.0 12.0 %copy-start.2 = (s32[63,4]{0,1:T(4,128)S(1)}, s32[63,4]{0,1:T(4,128)}, u32[]{:S(2)}) copy-start(s32[63,4]{0,1:T(4,128)} %param.13) | copy-start | bytes 3028
  0.0 12.0 %copy-start.1 = (bf16[63,64,256]{2,1,0:T(8,128)(2,1)S(1)}, bf16[63,64,256]{2,1,0:T(8,128)(2,1)}, u32[]{:S(2)}) copy-start(bf16[63,64,256]{2,1,0:T(8,128)(2,1)} %refs_5_.1) | copy-start | bytes 6193156
  5.5 25.3 %collective-permute-start.2 = (bf16[784,512]{1,0:T(8,128)(2,1)S(1)}, bf16[784,512]{1,0:T(8,128)(2,1)S(1)}, u32[]{:S(2)}, u32[]{:S(2)}) collective-permute-start(bf16[784,512]{1,0:T(8,128)(2,1)S(1)} %get-tuple-element.37), channel_id=1, source_target_pairs={{0,1},{1,2},{2,3},{3,4},{4,5},{5,6},{6,7},{7,8},{8,9},{9,10},{10,1... | collective-permute-start | bytes 2408456 | tf_op jit(solution)/shard_map/ppermute | solution.py:283
  7.4 23.4 %collective-permute-start.3 = (bf16[784,512]{1,0:T(8,128)(2,1)S(1)}, bf16[784,512]{1,0:T(8,128)(2,1)S(1)}, u32[]{:S(2)}, u32[]{:S(2)}) collective-permute-start(bf16[784,512]{1,0:T(8,128)(2,1)S(1)} %get-tuple-element.38), channel_id=1, source_target_pairs={{1,0},{2,1},{3,2},{4,3},{5,4},{6,5},{7,6},{8,7},{9,8},{10,9},{11,1... | collective-permute-start | bytes 2408456 | tf_op jit(solution)/shard_map/ppermute | solution.py:283
  12.0 15.8 %copy-start = (bf16[32,3,128,128]{3,2,1,0:T(8,128)(2,1)S(1)}, bf16[32,3,128,128]{3,2,1,0:T(8,128)(2,1)}, u32[]{:S(2)}) copy-start(bf16[32,3,128,128]{3,2,1,0:T(8,128)(2,1)} %refs_2_.3) | copy-start | bytes 9437188
  12.0 15.8 %copy-start.3 = (s32[32,3]{0,1:T(4,128)S(1)}, s32[32,3]{0,1:T(4,128)}, u32[]{:S(2)}) copy-start(s32[32,3]{0,1:T(4,128)} %param.9) | copy-start | bytes 1156
  15.5 9.0 %collective-permute-start.5 = (bf16[64,512]{1,0:T(8,128)(2,1)S(1)}, bf16[64,512]{1,0:T(8,128)(2,1)S(1)}, u32[]{:S(2)}, u32[]{:S(2)}) collective-permute-start(bf16[64,512]{1,0:T(8,128)(2,1)S(1)} %get-tuple-element.39), channel_id=1, source_target_pairs={{3,0},{4,1},{5,2},{6,3},{7,4},{8,5},{9,6},{10,7},{11,8},{12,9},{13... | collective-permute-start | bytes 196616 | tf_op jit(solution)/shard_map/ppermute | solution.py:283
  17.4 13.4 %collective-permute-start.4 = (bf16[64,512]{1,0:T(8,128)(2,1)S(1)}, bf16[64,512]{1,0:T(8,128)(2,1)S(1)}, u32[]{:S(2)}, u32[]{:S(2)}) collective-permute-start(bf16[64,512]{1,0:T(8,128)(2,1)S(1)} %get-tuple-element.39), channel_id=1, source_target_pairs={{0,3},{1,4},{2,5},{3,6},{4,7},{5,8},{6,9},{7,10},{8,11},{9,12},{10... | collective-permute-start | bytes 196616 | tf_op jit(solution)/shard_map/ppermute | solution.py:283
  21.1 11.0 %collective-permute-start = (bf16[128,512]{1,0:T(8,128)(2,1)S(1)}, bf16[128,512]{1,0:T(8,128)(2,1)S(1)}, u32[]{:S(2)}, u32[]{:S(2)}) collective-permute-start(bf16[128,512]{1,0:T(8,128)(2,1)S(1)} %get-tuple-element.35), channel_id=1, source_target_pairs={{0,2},{1,3},{2,4},{3,5},{4,6},{5,7},{6,8},{7,9},{8,10},{9,11},{10,... | collective-permute-start | bytes 393224 | tf_op jit(solution)/shard_map/ppermute | solution.py:283
  24.5 11.0 %collective-permute-start.1 = (bf16[128,512]{1,0:T(8,128)(2,1)S(1)}, bf16[128,512]{1,0:T(8,128)(2,1)S(1)}, u32[]{:S(2)}, u32[]{:S(2)}) collective-permute-start(bf16[128,512]{1,0:T(8,128)(2,1)S(1)} %get-tuple-element.36), channel_id=1, source_target_pairs={{2,0},{3,1},{4,2},{5,3},{6,4},{7,5},{8,6},{9,7},{10,8},{11,9},{12,... | collective-permute-start | bytes 393224 | tf_op jit(solution)/shard_map/ppermute | solution.py:283

commit v10 on v9

--- a/solution.py
+++ b/solution.py
@@ -289,7 +289,7 @@
     hbm = pl.BlockSpec(memory_space=pltpu.HBM)
     vmem = pl.BlockSpec(memory_space=pltpu.VMEM)
     smem = pl.BlockSpec(memory_space=pltpu.SMEM)
-    chunks = 16
+    chunks = 4
 
     padded_x, poles, up, down, pair4, bs, ts = pl.pallas_call(
         lambda *refs: upward_kernel(plan, chunks, *refs),

time: 39.4 us -> 37.8 us (0.959)
  Pallas kernels: 16.8 us -> 15.2 us
    pallas_call x1, Pallas kernels: 5.47 us -> 3.87 us  [body(): pl.pallas_call(lambda *refs: upward_kernel(plan, chunks, *refs), in_specs...]
  transfers between devices with their start and end apart: 6 -> 6, of which waited for: 1 -> 1; matrix products, arithmetic and copies ran while one was open for 0% -> 0% of each run, Pallas kernels for 19% -> 20%
where the time goes in v10:
time: 37.8 us; the launch traced here: 37.6 us
  starting transfers between devices  18.8 us (50%)
  Pallas kernels  15.2 us (40%)
  waiting for transfers between devices  3.45 us (9%)
    ppermute x6, starting transfers between devices, shifted(): return lax.ppermute(array, 'slab', pairs)  18.8 us
    pallas_call x1, Pallas kernels, body(): pl.pallas_call(lambda *refs: upward_kernel(plan, chunks, *refs), in_specs...  3.87 us
    pallas_call x1, Pallas kernels, body(): pl.pallas_call(lambda *refs: final_kernel(plan, *refs), in_specs=[vmem] *...  3.67 us
    pallas_call x1, Pallas kernels, body(): pl.pallas_call(lambda *refs: couple_kernel(plan, *refs), in_specs=[smem,...  3.46 us
    ppermute x6, waiting for transfers between devices, shifted(): return lax.ppermute(array, 'slab', pairs)  3.45 us
    pallas_call x1, Pallas kernels, body(): pl.pallas_call(lambda *refs: near_kernel(plan, *refs), in_specs=[smem, vm...  2.91 us
    pallas_call x1, Pallas kernels, body(): pl.pallas_call(lambda *refs: rim_kernel(plan, *refs), in_specs=[vmem] * 6...  1.26 us
  transfers between devices with their start and end apart: 6, of which 1 were waited for; matrix products, arithmetic and copies ran while one was open for 0% of the time, Pallas kernels for 20%

profile of v10, /device:TPU:16, one launch (start us, length us, event | category | flops | bytes accessed | tf_op | source)
XLA Modules:
  0.0 37.6 jit_solution(274431062492821606)
XLA Ops:
  0.0 0.0 copy-start.2
  0.0 0.0 copy-start.1
  0.0 3.9 %upward.1 = (bf16[4352,512]{1,0:T(8,128)(2,1)S(1)}, bf16[5376,512]{1,0:T(8,128)(2,1)S(1)}, bf16[784,512]{1,0:T(8,128)(2,1)S(1)}, bf16[784,512]{1,0:T(8,128)(2,1)...) custom-call(bf16[4096,512]{1,0:T(8,128)(2,1)} %refs_0_.1, ...), custom_call_target="tpu_custom_call" | custom-call | tf_op jit(solution)/shard_map/upward/pallas_call | solution.py:294
  3.9 1.9 %collective-permute-start.2 = (bf16[784,512]{1,0:T(8,128)(2,1)S(1)}, bf16[784,512]{1,0:T(8,128)(2,1)S(1)}, u32[]{:S(2)}, u32[]{:S(2)}) collective-permute-start(bf16[784,512]{1,0:T(8,128)(2,1)S(1)} %get-tuple-element.37), channel_id=1, source_target_pairs={{0,1},{1,2},{2,3},{3,4},{4,5},{5,6},{6,7},{7,8},{8,9},{9,10},{10,1... | collective-permute-start | bytes 2408456 | tf_op jit(solution)/shard_map/ppermute | solution.py:283
  5.8 4.5 %collective-permute-start.3 = (bf16[784,512]{1,0:T(8,128)(2,1)S(1)}, bf16[784,512]{1,0:T(8,128)(2,1)S(1)}, u32[]{:S(2)}, u32[]{:S(2)}) collective-permute-start(bf16[784,512]{1,0:T(8,128)(2,1)S(1)} %get-tuple-element.38), channel_id=1, source_target_pairs={{1,0},{2,1},{3,2},{4,3},{5,4},{6,5},{7,6},{8,7},{9,8},{10,9},{11,1... | collective-permute-start | bytes 2408456 | tf_op jit(solution)/shard_map/ppermute | solution.py:283
  10.4 0.0 copy-done.2
  10.4 0.0 copy-done.1
  10.4 0.0 copy-start
  10.4 0.0 copy-start.3
  10.4 3.5 %couple.1 = (f32[3840,512]{1,0:T(8,128)S(1)}, bf16[63,64,256]{2,1,0:T(8,128)(2,1)S(1)}, bf16[32,128,64]{2,1,0:T(8,128)(2,1)S(1)}, bf16[31,128,64]{2,1,0:T(8,128)...) custom-call(s32[4,63]{1,0:T(4,128)S(1)} %bitcast.2, ...), custom_call_target="tpu_custom_call" | custom-call | flops 6000000000 | bytes 8388608 | tf_op jit(solution)/shard_map/couple/pallas_call | solution.py:314
  13.9 1.9 %collective-permute-start.5 = (bf16[64,512]{1,0:T(8,128)(2,1)S(1)}, bf16[64,512]{1,0:T(8,128)(2,1)S(1)}, u32[]{:S(2)}, u32[]{:S(2)}) collective-permute-start(bf16[64,512]{1,0:T(8,128)(2,1)S(1)} %get-tuple-element.39), channel_id=1, source_target_pairs={{3,0},{4,1},{5,2},{6,3},{7,4},{8,5},{9,6},{10,7},{11,8},{12,9},{13... | collective-permute-start | bytes 196616 | tf_op jit(solution)/shard_map/ppermute | solution.py:283
  15.8 3.6 %collective-permute-start.4 = (bf16[64,512]{1,0:T(8,128)(2,1)S(1)}, bf16[64,512]{1,0:T(8,128)(2,1)S(1)}, u32[]{:S(2)}, u32[]{:S(2)}) collective-permute-start(bf16[64,512]{1,0:T(8,128)(2,1)S(1)} %get-tuple-element.39), channel_id=1, source_target_pairs={{0,3},{1,4},{2,5},{3,6},{4,7},{5,8},{6,9},{7,10},{8,11},{9,12},{10... | collective-permute-start | bytes 196616 | tf_op jit(solution)/shard_map/ppermute | solution.py:283
  19.4 3.4 %collective-permute-start = (bf16[128,512]{1,0:T(8,128)(2,1)S(1)}, bf16[128,512]{1,0:T(8,128)(2,1)S(1)}, u32[]{:S(2)}, u32[]{:S(2)}) collective-permute-start(bf16[128,512]{1,0:T(8,128)(2,1)S(1)} %get-tuple-element.35), channel_id=1, source_target_pairs={{0,2},{1,3},{2,4},{3,5},{4,6},{5,7},{6,8},{7,9},{8,10},{9,11},{10,... | collective-permute-start | bytes 393224 | tf_op jit(solution)/shard_map/ppermute | solution.py:283
  22.8 0.0 collective-permute-done.5.refs_5_
  22.9 3.3 %collective-permute-start.1 = (bf16[128,512]{1,0:T(8,128)(2,1)S(1)}, bf16[128,512]{1,0:T(8,128)(2,1)S(1)}, u32[]{:S(2)}, u32[]{:S(2)}) collective-permute-start(bf16[128,512]{1,0:T(8,128)(2,1)S(1)} %get-tuple-element.36), channel_id=1, source_target_pairs={{2,0},{3,1},{4,2},{5,3},{6,4},{7,5},{8,6},{9,7},{10,8},{11,9},{12,... | collective-permute-start | bytes 393224 | tf_op jit(solution)/shard_map/ppermute | solution.py:283
  26.2 0.0 copy-done
  26.2 0.0 copy-done.3
  26.2 2.9 %near.1 = (bf16[4096,512]{1,0:T(8,128)(2,1)S(1)}, bf16[2,128,128]{2,1,0:T(8,128)(2,1)S(1)}) custom-call(s32[3,32]{1,0:T(4,128)S(1)} %bitcast.3, bf16[4352,512]{1,0:T(8,128)(2,1)S(1)} %get-tuple-element.24.refs_1_, bf16[32,3,128,128]{3,2,1,0:T(8,128)(2,1)S(1)} %copy-done), custom_call_target="tpu_custom_call" | custom-call | flops 6000000000 | bytes 8388608 | tf_op jit(solution)/shard_map/near/pallas_call | solution.py:335
  29.1 0.0 collective-permute-done.4.refs_4_
  29.2 0.0 collective-permute-done.2.refs_2_.refs_8_
  29.2 0.0 collective-permute-done.3.refs_3_.refs_9_
  29.2 1.3 %rim.1 = (f32[1408,512]{1,0:T(8,128)S(1)}, bf16[128,512]{1,0:T(8,128)(2,1)S(1)}, f32[64,512]{1,0:T(8,128)S(1)}) custom-call(f32[3840,512]{1,0:T(8,128)S(1)} %get-tuple-element.30.refs_0_.refs_1_, bf16[63,64,256]{2,1,0:T(8,128)(2,1)S(1)} %get-tuple-element.31.refs_1_.refs_2_, bf16[784,512]{1,0:T(8,128)(2,1)S(1)} %collective-permute-done.2.refs_2_.refs_8_, ...), custom_call_target="tpu_custom_call" | custom-call | flops 10000000 | bytes 32768 | tf_op jit(solution)/shard_map/rim/pallas_call | solution.py:348
  30.4 0.0 collective-permute-done.refs_6_
  30.4 3.4 %collective-permute-done.1.refs_7_ = bf16[128,512]{1,0:T(8,128)(2,1)S(1)} collective-permute-done((bf16[128,512]{1,0:T(8,128)(2,1)S(1)}, bf16[128,512]{1,0:T(8,128)(2,1)S(1)}, u32[]{:S(2)}, u32[]{:S(2)}) %collective-permute-start.1) | collective-permute-done | bytes 131104 | tf_op jit(solution)/shard_map/ppermute | solution.py:283
  33.9 3.7 %final.1 = bf16[4096,512]{1,0:T(8,128)(2,1)} custom-call(bf16[4096,512]{1,0:T(8,128)(2,1)S(1)} %get-tuple-element.25.refs_0_, f32[3840,512]{1,0:T(8,128)S(1)} %get-tuple-element.30.refs_0_.refs_1_, bf16[63,64,256]{2,1,0:T(8,128)(2,1)S(1)} %get-tuple-element.31.refs_1_.refs_2_, bf16[2,128,128]{2,1,0:T(8,128)(2,1)S(1)} %get-tuple-element.32.refs_3_, ...), custom_call_target="tpu_custom_call" | custom-call | tf_op jit(solution)/shard_map/final/pallas_call | solution.py:362
Async XLA Ops:
  0.0 10.4 %copy-start.2 = (s32[63,4]{0,1:T(4,128)S(1)}, s32[63,4]{0,1:T(4,128)}, u32[]{:S(2)}) copy-start(s32[63,4]{0,1:T(4,128)} %param.13) | copy-start | bytes 3028
  0.0 10.4 %copy-start.1 = (bf16[63,64,256]{2,1,0:T(8,128)(2,1)S(1)}, bf16[63,64,256]{2,1,0:T(8,128)(2,1)}, u32[]{:S(2)}) copy-start(bf16[63,64,256]{2,1,0:T(8,128)(2,1)} %refs_5_.1) | copy-start | bytes 6193156
  3.9 25.3 %collective-permute-start.2 = (bf16[784,512]{1,0:T(8,128)(2,1)S(1)}, bf16[784,512]{1,0:T(8,128)(2,1)S(1)}, u32[]{:S(2)}, u32[]{:S(2)}) collective-permute-start(bf16[784,512]{1,0:T(8,128)(2,1)S(1)} %get-tuple-element.37), channel_id=1, source_target_pairs={{0,1},{1,2},{2,3},{3,4},{4,5},{5,6},{6,7},{7,8},{8,9},{9,10},{10,1... | collective-permute-start | bytes 2408456 | tf_op jit(solution)/shard_map/ppermute | solution.py:283
  5.8 23.4 %collective-permute-start.3 = (bf16[784,512]{1,0:T(8,128)(2,1)S(1)}, bf16[784,512]{1,0:T(8,128)(2,1)S(1)}, u32[]{:S(2)}, u32[]{:S(2)}) collective-permute-start(bf16[784,512]{1,0:T(8,128)(2,1)S(1)} %get-tuple-element.38), channel_id=1, source_target_pairs={{1,0},{2,1},{3,2},{4,3},{5,4},{6,5},{7,6},{8,7},{9,8},{10,9},{11,1... | collective-permute-start | bytes 2408456 | tf_op jit(solution)/shard_map/ppermute | solution.py:283
  10.4 15.8 %copy-start = (bf16[32,3,128,128]{3,2,1,0:T(8,128)(2,1)S(1)}, bf16[32,3,128,128]{3,2,1,0:T(8,128)(2,1)}, u32[]{:S(2)}) copy-start(bf16[32,3,128,128]{3,2,1,0:T(8,128)(2,1)} %refs_2_.3) | copy-start | bytes 9437188
  10.4 15.8 %copy-start.3 = (s32[32,3]{0,1:T(4,128)S(1)}, s32[32,3]{0,1:T(4,128)}, u32[]{:S(2)}) copy-start(s32[32,3]{0,1:T(4,128)} %param.9) | copy-start | bytes 1156
  13.9 9.0 %collective-permute-start.5 = (bf16[64,512]{1,0:T(8,128)(2,1)S(1)}, bf16[64,512]{1,0:T(8,128)(2,1)S(1)}, u32[]{:S(2)}, u32[]{:S(2)}) collective-permute-start(bf16[64,512]{1,0:T(8,128)(2,1)S(1)} %get-tuple-element.39), channel_id=1, source_target_pairs={{3,0},{4,1},{5,2},{6,3},{7,4},{8,5},{9,6},{10,7},{11,8},{12,9},{13... | collective-permute-start | bytes 196616 | tf_op jit(solution)/shard_map/ppermute | solution.py:283
  15.8 13.4 %collective-permute-start.4 = (bf16[64,512]{1,0:T(8,128)(2,1)S(1)}, bf16[64,512]{1,0:T(8,128)(2,1)S(1)}, u32[]{:S(2)}, u32[]{:S(2)}) collective-permute-start(bf16[64,512]{1,0:T(8,128)(2,1)S(1)} %get-tuple-element.39), channel_id=1, source_target_pairs={{0,3},{1,4},{2,5},{3,6},{4,7},{5,8},{6,9},{7,10},{8,11},{9,12},{10... | collective-permute-start | bytes 196616 | tf_op jit(solution)/shard_map/ppermute | solution.py:283
  19.4 11.0 %collective-permute-start = (bf16[128,512]{1,0:T(8,128)(2,1)S(1)}, bf16[128,512]{1,0:T(8,128)(2,1)S(1)}, u32[]{:S(2)}, u32[]{:S(2)}) collective-permute-start(bf16[128,512]{1,0:T(8,128)(2,1)S(1)} %get-tuple-element.35), channel_id=1, source_target_pairs={{0,2},{1,3},{2,4},{3,5},{4,6},{5,7},{6,8},{7,9},{8,10},{9,11},{10,... | collective-permute-start | bytes 393224 | tf_op jit(solution)/shard_map/ppermute | solution.py:283
  22.9 11.0 %collective-permute-start.1 = (bf16[128,512]{1,0:T(8,128)(2,1)S(1)}, bf16[128,512]{1,0:T(8,128)(2,1)S(1)}, u32[]{:S(2)}, u32[]{:S(2)}) collective-permute-start(bf16[128,512]{1,0:T(8,128)(2,1)S(1)} %get-tuple-element.36), channel_id=1, source_target_pairs={{2,0},{3,1},{4,2},{5,3},{6,4},{7,5},{8,6},{9,7},{10,8},{11,9},{12,... | collective-permute-start | bytes 393224 | tf_op jit(solution)/shard_map/ppermute | solution.py:283
